TPU v7x, 128 devices: a whole 4x4x4 slice. The times are simulated.
128 devices in a mesh: dp: 16 (over x_hi, y, core), head: 8 (over z, x_lo).
Axes of the slice: x: 4 (x_hi: 2, x_lo: 2; x = x_hi * 2 + x_lo), y: 4, z: 4, core: 2. Of those that a mesh axis runs over, the one named last changes fastest.
Arguments:
- inputs: bfloat16 [16, 1024, 512], P('dp', 'head'), may hold values from -6 to 6
- cotangent: bfloat16 [16, 1024, 512], P('dp', 'head'), may hold values from -6 to 6
- qkv_weight: float32 [3, 512, 512], P(None, None, 'head'), may hold values from -0.25 to 0.25
- qkv_first: float32 [3, 512, 512], P(None, None, 'head'), may hold values from -16 to 16
- qkv_second: float32 [3, 512, 512], P(None, None, 'head'), may hold values from 0.65536 to 2.62144
- out_weight: float32 [512, 512], P('head'), may hold values from -0.75 to 0.75
- out_first: float32 [512, 512], P('head'), may hold values from -6 to 6
- out_second: float32 [512, 512], P('head'), may hold values from 0.2359296 to 0.9437184
- up_weight: float32 [512, 2048], P(None, 'head'), may hold values from -0.25 to 0.25
- up_first: float32 [512, 2048], P(None, 'head'), may hold values from -6 to 6
- up_second: float32 [512, 2048], P(None, 'head'), may hold values from 0.36864 to 1.47456
- down_weight: float32 [2048, 512], P('head'), may hold values from -0.125 to 0.125
- down_first: float32 [2048, 512], P('head'), may hold values from -24 to 24
- down_second: float32 [2048, 512], P('head'), may hold values from 1.47456 to 5.89824
- gate_weight: float32 [2, 512, 512], replicated, may hold values from -0.25 to 0.25
- gate_first: float32 [2, 512, 512], replicated, may hold values from -32 to 32
- gate_second: float32 [2, 512, 512], replicated, may hold values from 2.00704 to 8.02816
- norm_gains: float32 [2, 512], replicated, may hold values from 0.5 to 1.5
- gains_first: float32 [2, 512], replicated, may hold values from -40 to 40
- gains_second: float32 [2, 512], replicated, may hold values from 4.096 to 16.384
- biases: float32 [4, 512], replicated, may hold values from -4 to 4
- biases_first: float32 [4, 512], replicated, may hold values from -40 to 40
- biases_second: float32 [4, 512], replicated, may hold values from 4.096 to 16.384
Outputs:
- mixed: float32 [16, 1024, 512], P('dp', 'head')
- input_grad: float32 [16, 1024, 512], P('dp', 'head')
- new_qkv: float32 [3, 512, 512], P(None, None, 'head')
- new_qkv_first: float32 [3, 512, 512], P(None, None, 'head')
- new_qkv_second: float32 [3, 512, 512], P(None, None, 'head')
- new_out: float32 [512, 512], P('head')
- new_out_first: float32 [512, 512], P('head')
- new_out_second: float32 [512, 512], P('head')
- new_up: float32 [512, 2048], P(None, 'head')
- new_up_first: float32 [512, 2048], P(None, 'head')
- new_up_second: float32 [512, 2048], P(None, 'head')
- new_down: float32 [2048, 512], P('head')
- new_down_first: float32 [2048, 512], P('head')
- new_down_second: float32 [2048, 512], P('head')
- new_gate: float32 [2, 512, 512], replicated
- new_gate_first: float32 [2, 512, 512], replicated
- new_gate_second: float32 [2, 512, 512], replicated
- new_gains: float32 [2, 512], replicated
- new_gains_first: float32 [2, 512], replicated
- new_gains_second: float32 [2, 512], replicated
- new_biases: float32 [4, 512], replicated
- new_biases_first: float32 [4, 512], replicated
- new_biases_second: float32 [4, 512], replicated
All inputs are finite; a program needn't handle non-finite values.
Results may differ from a plain program's by a relative error of at most 0.034.
Values may be sent and summed in bfloat16 or wider, within the bound.
A program may use at most 128 MiB of HBM per device.

v0:
```python
import math

import jax
import jax.numpy as jnp
from jax import lax
from jax.sharding import PartitionSpec as P

HDIM = 64
STEP = 10


NORM_EPS = 1e-05
BETA_ONE = 0.9
BETA_TWO = 0.999
ADAM_EPS = 1e-08
DECAY = 0.01
RATES = (0.04, 0.1, 0.04, 0.02, 0.04, 0.4, 0.3)


def norm_layer(value, gain, shift):
    center = value - jnp.mean(value, axis=-1, keepdims=True)
    spread = jnp.mean(center * center, axis=-1, keepdims=True)
    return center * lax.rsqrt(spread + NORM_EPS) * gain + shift


def adamw(weight, first, second, grad, rate):
    first = BETA_ONE * first + (1.0 - BETA_ONE) * grad
    second = BETA_TWO * second + (1.0 - BETA_TWO) * grad * grad
    first_hat = first / (1.0 - BETA_ONE**STEP)
    second_hat = second / (1.0 - BETA_TWO**STEP)
    weight = weight - rate * (first_hat / (jnp.sqrt(second_hat) + ADAM_EPS) + DECAY * weight)
    return (weight, first, second)


def head_total(partial_value):
    return lax.psum(partial_value.astype(jnp.bfloat16), "head").astype(jnp.float32)


def attend_forward(query, keys, values):
    batch, length, heads, size = query.shape
    block = min(512, length)
    scale = 1.0 / math.sqrt(size)
    columns = jnp.arange(length, dtype=jnp.int32)

    def block_rows(start):
        rows_query = lax.dynamic_slice_in_dim(query, start, block, 1)
        scores = (
            jnp.einsum("bqhe,bkhe->bhqk", rows_query, keys, preferred_element_type=jnp.float32)
            * scale
        )
        positions = start + jnp.arange(block, dtype=jnp.int32)
        keep = columns[None, :] <= positions[:, None]
        scores = jnp.where(keep, scores, -1e30)
        ceiling = jnp.max(scores, axis=-1, keepdims=True)
        raised = jnp.exp(scores - ceiling)
        total_mass = jnp.sum(raised, axis=-1, keepdims=True)
        weights = (raised / total_mass).astype(jnp.bfloat16)
        result = jnp.einsum("bhqk,bkhe->bqhe", weights, values, preferred_element_type=jnp.float32)
        return (result.astype(jnp.bfloat16), ceiling[..., 0] + jnp.log(total_mass[..., 0]))

    starts = jnp.arange(length // block, dtype=jnp.int32) * block
    pieces, log_total = lax.map(block_rows, starts)
    heads_out = jnp.moveaxis(pieces, 0, 1).reshape(batch, length, heads, size)
    return (heads_out, log_total)


def attend_backward(query, keys, values, log_total, grad_out):
    batch, length, heads, size = query.shape
    block = min(512, length)
    scale = 1.0 / math.sqrt(size)
    columns = jnp.arange(length, dtype=jnp.int32)

    def block_step(carry, items):
        grad_keys, grad_values = carry
        start, block_log = items
        rows_query = lax.dynamic_slice_in_dim(query, start, block, 1)
        rows_grad = lax.dynamic_slice_in_dim(grad_out, start, block, 1)
        scores = (
            jnp.einsum("bqhe,bkhe->bhqk", rows_query, keys, preferred_element_type=jnp.float32)
            * scale
        )
        positions = start + jnp.arange(block, dtype=jnp.int32)
        keep = columns[None, :] <= positions[:, None]
        scores = jnp.where(keep, scores, -1e30)
        probs = jnp.exp(scores - block_log[..., None])
        grad_values = grad_values + jnp.einsum(
            "bhqk,bqhe->bkhe",
            probs.astype(jnp.bfloat16),
            rows_grad,
            preferred_element_type=jnp.float32,
        )
        grad_probs = jnp.einsum(
            "bqhe,bkhe->bhqk", rows_grad, values, preferred_element_type=jnp.float32
        )
        inner = jnp.sum(grad_probs * probs, axis=-1, keepdims=True)
        grad_scores = (probs * (grad_probs - inner)).astype(jnp.bfloat16)
        grad_query = (
            jnp.einsum("bhqk,bkhe->bqhe", grad_scores, keys, preferred_element_type=jnp.float32)
            * scale
        )
        grad_keys = (
            grad_keys
            + jnp.einsum(
                "bhqk,bqhe->bkhe", grad_scores, rows_query, preferred_element_type=jnp.float32
            )
            * scale
        )
        return ((grad_keys, grad_values), grad_query.astype(jnp.bfloat16))

    starts = jnp.arange(length // block, dtype=jnp.int32) * block
    zeros = jnp.zeros(keys.shape, jnp.float32)
    (grad_keys, grad_values), pieces = lax.scan(block_step, (zeros, zeros), (starts, log_total))
    grad_query = jnp.moveaxis(pieces, 0, 1).reshape(batch, length, heads, size)
    return (grad_query, grad_keys.astype(jnp.bfloat16), grad_values.astype(jnp.bfloat16))


def local(
    inputs,
    cotangent,
    qkv_weight,
    qkv_first,
    qkv_second,
    out_weight,
    out_first,
    out_second,
    up_weight,
    up_first,
    up_second,
    down_weight,
    down_first,
    down_second,
    gate_weight,
    gate_first,
    gate_second,
    norm_gains,
    gains_first,
    gains_second,
    biases,
    biases_first,
    biases_second,
):
    own_rows = inputs.shape[1]
    proj_weight = qkv_weight.astype(jnp.bfloat16)
    out_low = out_weight.astype(jnp.bfloat16)
    up_low = up_weight.astype(jnp.bfloat16)
    down_low = down_weight.astype(jnp.bfloat16)
    gate_low = gate_weight.astype(jnp.bfloat16)
    whole_in, whole_cot = (
        lax.all_gather(inputs, "head", axis=1, tiled=True),
        lax.all_gather(cotangent, "head", axis=1, tiled=True),
    )
    x_rows = whole_in.astype(jnp.float32)
    grad_rows = whole_cot.astype(jnp.float32)
    h1_f, norm_one_pull = jax.vjp(norm_layer, x_rows, norm_gains[0], biases[0])
    h1_rows = h1_f.astype(jnp.bfloat16)
    batch, length, width = h1_rows.shape
    proj = jnp.einsum(
        "bld,jde->jble", h1_rows, proj_weight, preferred_element_type=jnp.float32
    ).astype(jnp.bfloat16)
    heads_here = proj.shape[-1] // HDIM
    query = proj[0].reshape(batch, length, heads_here, HDIM)
    keys = proj[1].reshape(batch, length, heads_here, HDIM)
    values = proj[2].reshape(batch, length, heads_here, HDIM)
    heads_out, log_total = attend_forward(query, keys, values)
    heads_flat = heads_out.reshape(batch, length, heads_here * HDIM)
    attn = head_total(
        jnp.einsum("ble,ed->bld", heads_flat, out_low, preferred_element_type=jnp.float32)
    )
    gate_one = jax.nn.sigmoid(
        jnp.einsum("bld,de->ble", h1_rows, gate_low[0], preferred_element_type=jnp.float32)
        + biases[2]
    )
    middle = gate_one * attn + (1.0 - gate_one) * x_rows
    h2_f, norm_two_pull = jax.vjp(norm_layer, middle, norm_gains[1], biases[1])
    h2_rows = h2_f.astype(jnp.bfloat16)
    hidden = jnp.einsum("bld,df->blf", h2_rows, up_low, preferred_element_type=jnp.float32)
    active_f, gelu_pull = jax.vjp(jax.nn.gelu, hidden)
    active = active_f.astype(jnp.bfloat16)
    ffn = head_total(
        jnp.einsum("blf,fd->bld", active, down_low, preferred_element_type=jnp.float32)
    )
    gate_two = jax.nn.sigmoid(
        jnp.einsum("bld,de->ble", h2_rows, gate_low[1], preferred_element_type=jnp.float32)
        + biases[3]
    )
    mixed = gate_two * ffn + (1.0 - gate_two) * middle
    grad_ffn = (gate_two * grad_rows).astype(jnp.bfloat16)
    grad_z_two = (grad_rows * (ffn - middle) * gate_two * (1.0 - gate_two)).astype(jnp.bfloat16)
    grad_middle = (1.0 - gate_two) * grad_rows
    grad_active = jnp.einsum("bld,fd->blf", grad_ffn, down_low, preferred_element_type=jnp.float32)
    grad_hidden = gelu_pull(grad_active)[0].astype(jnp.bfloat16)
    grad_down = jnp.einsum("blf,bld->fd", active, grad_ffn, preferred_element_type=jnp.float32)
    grad_up = jnp.einsum("bld,blf->df", h2_rows, grad_hidden, preferred_element_type=jnp.float32)
    grad_h2 = head_total(
        jnp.einsum("blf,df->bld", grad_hidden, up_low, preferred_element_type=jnp.float32)
    )
    grad_h2 = grad_h2 + jnp.einsum(
        "ble,de->bld", grad_z_two, gate_low[1], preferred_element_type=jnp.float32
    )
    grad_gate_two = jnp.einsum(
        "bld,ble->de", h2_rows, grad_z_two, preferred_element_type=jnp.float32
    )
    grad_bias_two = jnp.sum(grad_z_two.astype(jnp.float32), axis=(0, 1))
    grad_mid_norm, grad_gain_two, grad_shift_two = norm_two_pull(grad_h2)
    grad_middle = grad_middle + grad_mid_norm
    grad_attn = (gate_one * grad_middle).astype(jnp.bfloat16)
    grad_z_one = (grad_middle * (attn - x_rows) * gate_one * (1.0 - gate_one)).astype(jnp.bfloat16)
    grad_input = (1.0 - gate_one) * grad_middle
    grad_heads = jnp.einsum(
        "bld,ed->ble", grad_attn, out_low, preferred_element_type=jnp.float32
    ).astype(jnp.bfloat16)
    grad_out = jnp.einsum("ble,bld->ed", heads_flat, grad_attn, preferred_element_type=jnp.float32)
    grad_query, grad_keys, grad_values = attend_backward(
        query, keys, values, log_total, grad_heads.reshape(batch, length, heads_here, HDIM)
    )
    grad_proj = jnp.stack([grad_query, grad_keys, grad_values]).reshape(
        3, batch, length, heads_here * HDIM
    )
    grad_qkv = jnp.einsum("bld,jble->jde", h1_rows, grad_proj, preferred_element_type=jnp.float32)
    grad_h1 = head_total(
        jnp.einsum("jble,jde->bld", grad_proj, proj_weight, preferred_element_type=jnp.float32)
    )
    grad_h1 = grad_h1 + jnp.einsum(
        "ble,de->bld", grad_z_one, gate_low[0], preferred_element_type=jnp.float32
    )
    grad_gate_one = jnp.einsum(
        "bld,ble->de", h1_rows, grad_z_one, preferred_element_type=jnp.float32
    )
    grad_bias_one = jnp.sum(grad_z_one.astype(jnp.float32), axis=(0, 1))
    grad_in_norm, grad_gain_one, grad_shift_one = norm_one_pull(grad_h1)
    grad_input = grad_input + grad_in_norm
    grad_gates = jnp.stack([grad_gate_one, grad_gate_two])
    grad_gains = jnp.stack([grad_gain_one, grad_gain_two])
    grad_biases = jnp.stack([grad_shift_one, grad_shift_two, grad_bias_one, grad_bias_two])
    grad_qkv, grad_out, grad_up, grad_down = (
        lax.psum(grad_qkv.astype(jnp.bfloat16), "dp").astype(jnp.float32),
        lax.psum(grad_out.astype(jnp.bfloat16), "dp").astype(jnp.float32),
        lax.psum(grad_up.astype(jnp.bfloat16), "dp").astype(jnp.float32),
        lax.psum(grad_down.astype(jnp.bfloat16), "dp").astype(jnp.float32),
    )
    grad_gates, grad_gains, grad_biases = (
        lax.psum(grad_gates.astype(jnp.bfloat16), "dp").astype(jnp.float32),
        lax.psum(grad_gains.astype(jnp.bfloat16), "dp").astype(jnp.float32),
        lax.psum(grad_biases.astype(jnp.bfloat16), "dp").astype(jnp.float32),
    )
    offset = lax.axis_index("head") * own_rows
    mixed = lax.dynamic_slice_in_dim(mixed, offset, own_rows, 1)
    grad_input = lax.dynamic_slice_in_dim(grad_input, offset, own_rows, 1)
    new_qkv = adamw(qkv_weight, qkv_first, qkv_second, grad_qkv, RATES[0])
    new_out = adamw(out_weight, out_first, out_second, grad_out, RATES[1])
    new_up = adamw(up_weight, up_first, up_second, grad_up, RATES[2])
    new_down = adamw(down_weight, down_first, down_second, grad_down, RATES[3])
    new_gate = adamw(gate_weight, gate_first, gate_second, grad_gates, RATES[4])
    new_gains = adamw(norm_gains, gains_first, gains_second, grad_gains, RATES[5])
    new_biases = adamw(biases, biases_first, biases_second, grad_biases, RATES[6])
    return (
        mixed,
        grad_input,
        new_qkv[0],
        new_qkv[1],
        new_qkv[2],
        new_out[0],
        new_out[1],
        new_out[2],
        new_up[0],
        new_up[1],
        new_up[2],
        new_down[0],
        new_down[1],
        new_down[2],
        new_gate[0],
        new_gate[1],
        new_gate[2],
        new_gains[0],
        new_gains[1],
        new_gains[2],
        new_biases[0],
        new_biases[1],
        new_biases[2],
    )


def solution(mesh):
    return jax.shard_map(
        local,
        mesh=mesh,
        in_specs=(
            P("dp", "head", None),
            P("dp", "head", None),
            P(None, None, "head"),
            P(None, None, "head"),
            P(None, None, "head"),
            P("head", None),
            P("head", None),
            P("head", None),
            P(None, "head"),
            P(None, "head"),
            P(None, "head"),
            P("head", None),
            P("head", None),
            P("head", None),
            P(),
            P(),
            P(),
            P(),
            P(),
            P(),
            P(),
            P(),
            P(),
        ),
        out_specs=(
            P("dp", "head", None),
            P("dp", "head", None),
            P(None, None, "head"),
            P(None, None, "head"),
            P(None, None, "head"),
            P("head", None),
            P("head", None),
            P("head", None),
            P(None, "head"),
            P(None, "head"),
            P(None, "head"),
            P("head", None),
            P("head", None),
            P("head", None),
            P(),
            P(),
            P(),
            P(),
            P(),
            P(),
            P(),
            P(),
            P(),
        ),
        check_vma=False,
    )
```

profile of v0, /device:TPU:1, one launch (start us, length us, event | category | flops | bytes accessed | tf_op | source)
XLA Modules:
  0.0 596.4 jit_solution(7120060084813102718)
XLA Ops:
  12.8 36.6 %all-gather.3.cloned.1.call-done = bf16[1,1024,512]{1,2,0:T(8,128)(2,1)} async-done(((bf16[1,128,512]{1,2,0:T(8,128)(2,1)}), bf16[1,1024,512]{1,2,0:T(8,128)(2,1)}) %all-gather.3.cloned.1.call-update) | async-done | bytes 1048592 | tf_op jit(solution)/shard_map/all_gather | solution.py:149
  53.9 12.5 %while.28 = (s32[]{:T(128)}, bf16[2,1,512,1,64]{2,4,3,1,0:T(8,128)(2,1)}, f32[2,1,1,512]{3,2,1,0:T(1,128)S(1)}, s32[2]{0:T(128)}, bf16[1,1024,1,64]{1,3,2,0:T(8,...) while((s32[]{:T(128)}, ...), condition=%wide.region_5.6_spmd.clone, body=%wide.region_2.5_spmd.clone.sunk | while | flops 138969088 | bytes 7758051 | solution.py:62
  68.4 2.4 fusion.60
  73.7 78.6 %all-reduce.8.cloned.1.call-done = bf16[1,1024,512]{1,2,0:T(8,128)(2,1)} async-done(((bf16[1,1024,512]{1,2,0:T(8,128)(2,1)}), bf16[1,1024,512]{1,2,0:T(8,128)(2,1)}) %all-reduce.8.cloned.1.call-update) | async-done | bytes 1048592 | tf_op jit(solution)/shard_map/psum | solution.py:36
  152.3 4.2 fusion.142
  160.9 2.4 add_divide_fusion
  163.3 30.6 %all-gather.5.cloned.1.call-done = bf16[1,1024,512]{1,2,0:T(8,128)(2,1)} async-done(((bf16[1,128,512]{1,2,0:T(8,128)(2,1)}), bf16[1,1024,512]{1,2,0:T(8,128)(2,1)}) %all-gather.5.cloned.1.call-update) | async-done | bytes 1048592 | tf_op jit(solution)/shard_map/all_gather | solution.py:150
  193.9 3.5 fusion.73
  200.0 2.5 convolution_convert_fusion.7
  202.5 3.4 subtract_bitcast_fusion
  210.3 99.8 %all-reduce.14.cloned.1.call-done = (bf16[1,1024,512]{1,2,0:T(8,128)(2,1)}, bf16[1,1024,512]{1,2,0:T(8,128)(2,1)}) async-done(((bf16[1,1024,512]{1,2,0:T(8,128)(2,1)}, bf16[1,1024,512]{1,2,0:T(8,128)(2,1)}), (bf16[1,1024,512]{1,2,0:T(8,128)(2,1)}, bf16[1,1024,512]{1,2,0:T(8,128)(2,1)})) %all-reduce.14.cloned.1.call-update) | async-done | bytes 2097168 | tf_op jit(solution)/shard_map/psum | solution.py:36
  310.1 4.8 fusion.129
  318.9 3.0 fusion.126
  324.8 19.8 %while.29 = (s32[]{:T(128)}, f32[1,1024,1,64]{1,3,2,0:T(8,128)}, f32[1,1024,1,64]{1,3,2,0:T(8,128)S(1)}, bf16[2,1,512,1,64]{2,4,3,1,0:T(8,128)(2,1)}, s32[2]{0:T...) while((s32[]{:T(128)}, f32[1,1024,1,64]{1,3,2,0:T(8,128)}, ...), condition=%wide.region_15.16_spmd.clone, body=%wide.region_13.15_spmd.clone.sunk | while | flops 341180416 | bytes 22231452 | solution.py:112
  348.0 2.4 fusion.59
  350.8 2.4 fusion.64
  359.8 66.7 %all-reduce.10.cloned.1.call-done = bf16[1,1024,512]{1,2,0:T(8,128)(2,1)} async-done(((bf16[1,1024,512]{1,2,0:T(8,128)(2,1)}), bf16[1,1024,512]{1,2,0:T(8,128)(2,1)}) %all-reduce.10.cloned.1.call-update) | async-done | bytes 1048592 | tf_op jit(solution)/shard_map/psum | solution.py:36
  426.5 3.5 fusion.43
  436.2 38.3 %all-reduce = (bf16[2,512]{1,0:T(2,128)(2,1)S(1)}, bf16[4,512]{1,0:T(4,128)(2,1)S(1)}) all-reduce(bf16[2,512]{1,0:T(2,128)(2,1)S(1)} %pad_maximum_fusion.2, bf16[4,512]{1,0:T(4,128)(2,1)S(1)} %pad_maximum_fusion.1), channel_id=1, replica_groups=mesh['dp'=16,'head'=8] {'dp'}, use_global_device_ids=true, to_apply=%region_26.27 | all-reduce | flops 3072 | bytes 12288 | tf_op jit(solution)/shard_map/psum | solution.py:243
  477.2 99.3 %all-reduce.12.cloned.1.call-done = (bf16[3,512,64]{1,2,0:T(8,128)(2,1)}, bf16[64,512]{1,0:T(8,128)(2,1)}, bf16[512,256]{1,0:T(8,128)(2,1)}, bf16[256,512]{1,0:T(8,128)(2,1)}, bf16[2,512,512]{2,1,0:T(8,128)(2,1)}) async-done(((bf16[3,512,64]{1,2,0:T(8,128)(2,1)}, bf16[64,512]{1,0:T(8,128)(2,1)}, bf16[512,256]{1,0:T(8,128)(2,1)}, bf16[256,512]{1,0:T(8,128)(2,1)}, bf16[2,512,512]{2,1,0:T(8,128)(2,1)}), ...) | async-done | bytes 1835024 | tf_op jit(solution)/shard_map/psum | solution.py:236
  576.5 1.7 multiply_subtract_fusion.4
  578.3 2.6 multiply_subtract_fusion.3
  580.9 2.5 multiply_subtract_fusion.2
  585.7 3.9 multiply_subtract_fusion
  (266 shorter events, 78.5 us)
Async XLA Ops:
  7.2 42.2 %all-gather.3.cloned.1.call-start = ((), (), s32[]{:S(2)}) async-start(), calls=%async_computation | async-start | bytes 1179648 | tf_op jit(solution)/shard_map/all_gather | solution.py:149
  8.9 143.3 %all-reduce.8.cloned.1.call-start = ((), (), s32[]{:S(2)}) async-start(), calls=%async_computation.1 | async-start | bytes 2097152 | tf_op jit(solution)/shard_map/psum | solution.py:36
  10.0 43.1 %copy-start.40 = (bf16[3,512,64]{1,2,0:T(8,128)(2,1)}, bf16[3,512,64]{1,2,0:T(8,128)(2,1)S(1)}, u32[]{:S(2)}) copy-start(bf16[3,512,64]{1,2,0:T(8,128)(2,1)S(1)} %convert_element_type.189) | copy-start | bytes 589828
  11.3 41.8 %copy-start.61 = (f32[1,512]{1,0:T(1,128)}, f32[1,512]{1,0:T(1,128)S(1)}, u32[]{:S(2)}) copy-start(f32[1,512]{1,0:T(1,128)S(1)} %get-tuple-element.337) | copy-start | bytes 6148
  12.8 40.4 %copy-start.68 = (f32[1,512]{1,0:T(1,128)}, f32[1,512]{1,0:T(1,128)S(1)}, u32[]{:S(2)}) copy-start(f32[1,512]{1,0:T(1,128)S(1)} %get-tuple-element.335) | copy-start | bytes 6148
  66.5 7.2 %copy-start.14 = (bf16[1,1024,1,64]{1,3,2,0:T(8,128)(2,1)}, bf16[1,1024,1,64]{1,3,2,0:T(8,128)(2,1)S(1)}, u32[]{:S(2)}) copy-start(bf16[1,1024,1,64]{1,3,2,0:T(8,128)(2,1)S(1)} %get-tuple-element.544) | copy-start | bytes 393220
  66.5 7.2 %copy-start.16 = (bf16[1,1024,1,64]{1,3,2,0:T(8,128)(2,1)}, bf16[1,1024,1,64]{1,3,2,0:T(8,128)(2,1)S(1)}, u32[]{:S(2)}) copy-start(bf16[1,1024,1,64]{1,3,2,0:T(8,128)(2,1)S(1)} %get-tuple-element.545) | copy-start | bytes 393220
  66.5 7.2 %copy-start.29 = (bf16[1,1024,1,64]{1,3,2,0:T(8,128)(2,1)}, bf16[1,1024,1,64]{1,3,2,0:T(8,128)(2,1)S(1)}, u32[]{:S(2)}) copy-start(bf16[1,1024,1,64]{1,3,2,0:T(8,128)(2,1)S(1)} %get-tuple-element.554) | copy-start | bytes 393220
  66.5 6.1 %copy-start.12 = (f32[2,512,512]{2,1,0:T(8,128)S(1)}, f32[2,512,512]{2,1,0:T(8,128)}, u32[]{:S(2)}) copy-start(f32[2,512,512]{2,1,0:T(8,128)} %param.41) | copy-start | bytes 6291460
  70.8 123.1 %all-gather.5.cloned.1.call-start = ((), (), s32[]{:S(2)}) async-start(), calls=%async_computation.2 | async-start | bytes 1179648 | tf_op jit(solution)/shard_map/all_gather | solution.py:150
  72.5 237.6 %all-reduce.14.cloned.1.call-start = ((), (), s32[]{:S(2)}) async-start(), calls=%async_computation.5 | async-start | bytes 4194304 | tf_op jit(solution)/shard_map/psum | solution.py:36
  199.7 226.8 %all-reduce.10.cloned.1.call-start = ((), (), s32[]{:S(2)}) async-start(), calls=%async_computation.3 | async-start | bytes 2097152 | tf_op jit(solution)/shard_map/psum | solution.py:36
  350.6 226.0 %all-reduce.12.cloned.1.call-start = ((), (), s32[]{:S(2)}) async-start(), calls=%async_computation.4 | async-start | bytes 3670016 | tf_op jit(solution)/shard_map/psum | solution.py:236
  430.7 43.8 %copy-start.60 = (f32[2,512]{1,0:T(2,128)S(1)}, f32[2,512]{1,0:T(2,128)}, u32[]{:S(2)}) copy-start(f32[2,512]{1,0:T(2,128)} %param.44) | copy-start | bytes 12292
  430.7 45.1 %copy-start.57 = (f32[4,512]{1,0:T(4,128)S(1)}, f32[4,512]{1,0:T(4,128)}, u32[]{:S(2)}) copy-start(f32[4,512]{1,0:T(4,128)} %param.47) | copy-start | bytes 24580
  430.7 145.8 %copy-start.35 = (f32[64,512]{1,0:T(8,128)S(1)}, f32[64,512]{1,0:T(8,128)}, u32[]{:S(2)}) copy-start(f32[64,512]{1,0:T(8,128)} %param.32) | copy-start | bytes 393220
  430.7 145.8 %copy-start.56 = (f32[64,512]{1,0:T(8,128)S(1)}, f32[64,512]{1,0:T(8,128)}, u32[]{:S(2)}) copy-start(f32[64,512]{1,0:T(8,128)} %param.33) | copy-start | bytes 393220
  430.8 147.5 %copy-start.31 = (f32[3,512,64]{1,2,0:T(8,128)S(1)}, f32[3,512,64]{1,2,0:T(8,128)}, u32[]{:S(2)}) copy-start(f32[3,512,64]{1,2,0:T(8,128)} %param.29) | copy-start | bytes 1179652
  433.2 147.7 %copy-start.20 = (f32[512,256]{1,0:T(8,128)S(1)}, f32[512,256]{1,0:T(8,128)}, u32[]{:S(2)}) copy-start(f32[512,256]{1,0:T(8,128)} %param.35) | copy-start | bytes 1572868
  433.2 147.7 %copy-start.48 = (f32[512,256]{1,0:T(8,128)S(1)}, f32[512,256]{1,0:T(8,128)}, u32[]{:S(2)}) copy-start(f32[512,256]{1,0:T(8,128)} %param.36) | copy-start | bytes 1572868
  433.2 147.7 %copy-start.49 = (f32[512,256]{1,0:T(8,128)S(1)}, f32[512,256]{1,0:T(8,128)}, u32[]{:S(2)}) copy-start(f32[512,256]{1,0:T(8,128)} %param.37) | copy-start | bytes 1572868
  578.3 5.1 copy-start.53
  578.3 5.1 copy-start.55
  578.3 6.6 %copy-start.39 = (bf16[2,512,512]{2,1,0:T(8,128)(2,1)S(1)}, bf16[2,512,512]{2,1,0:T(8,128)(2,1)}, u32[]{:S(2)}) copy-start(bf16[2,512,512]{2,1,0:T(8,128)(2,1)} %get-tuple-element.291) | copy-start | bytes 3145732
  (62 other events, 132.3 us)
Sparse Core Ops, SparseCore 0:
  10.2 39.2 all-gather.2
  70.9 81.3 all-reduce.7
  154.4 39.4 all-gather.4
  199.9 110.2 all-reduce.13
  350.7 75.8 all-reduce.9
  429.8 146.6 all-reduce.11
where the time goes:
time: 598 us; the launch traced here: 596 us
  waiting for transfers between devices  412 us (69%)
  other arithmetic  44.7 us (7%)
  matrix products  43.7 us (7%)
  blocking collectives  38.3 us (6%)
  local copies, waits for them, and re-layouts  34.5 us (6%)
  between operations  14.7 us (2%)
  loops' own time  8.08 us (1%)
    psum x3, waiting for transfers between devices, head_total(): lax.psum(partial_value.astype(jnp.bfloat16), 'head').astype(jnp.float32)  245 us
    psum x1, waiting for transfers between devices, local(): lax.psum(grad_qkv.astype(jnp.bfloat16), 'dp').astype(jnp.float32)  99.3 us
    psum x1, blocking collectives, local(): lax.psum(grad_gains.astype(jnp.bfloat16), 'dp').astype(jnp.float32)  38.3 us
    all_gather x1, waiting for transfers between devices, local(): lax.all_gather(inputs, 'head', axis=1, tiled=True)  36.6 us
    all_gather x1, waiting for transfers between devices, local(): lax.all_gather(cotangent, 'head', axis=1, tiled=True)  30.6 us
    sub x7, other arithmetic, adamw(): weight - rate * (first_hat / (jnp.sqrt(second_hat) + ADAM_EPS) + DECAY *...  14.8 us
    unnamed x129, local copies, waits for them, and re-layouts  13.9 us
  transfers between devices with their start and end apart: 6, of which 6 were waited for; matrix products, arithmetic and copies ran while one was open for 8% of the time, Pallas kernels for 0%

commit v1 on v0

v1 whole, which is shorter than its diff:
```python
import jax
import jax.numpy as jnp
from jax import lax
from jax.experimental import pallas as pl
from jax.experimental.pallas import tpu as pltpu
from jax.sharding import PartitionSpec as P

F32 = jnp.float32
BF16 = jnp.bfloat16
STEP = 10
NORM_EPS = 1e-05
BETA_ONE = 0.9
BETA_TWO = 0.999
ADAM_EPS = 1e-08
DECAY = 0.01
RATES = (0.04, 0.1, 0.04, 0.02, 0.04, 0.4, 0.3)
D = 512
ROWS = 128
LEN = 1024
QB = 256
NN = ((1,), (0,))
NT = ((1,), (1,))
TN = ((0,), (0,))


def dot(a, b, dims=NN):
    return lax.dot_general(a, b, (dims, ((), ())), preferred_element_type=F32)


def aligned(value, by):
    return pl.multiple_of(value, by)


class Links:
    def __init__(self, send_sems, recv_sems):
        self.send_sems, self.recv_sems, self.used, self.sent = send_sems, recv_sems, 0, []

    def start(self, src, dst, device):
        copy = pltpu.make_async_remote_copy(
            src_ref=src,
            dst_ref=dst,
            send_sem=self.send_sems.at[self.used],
            recv_sem=self.recv_sems.at[self.used],
            device_id=device,
            device_id_type=pl.DeviceIdType.MESH,
        )
        self.used += 1
        copy.start()
        self.sent.append(copy)
        return copy

    def drain(self):
        for copy in self.sent:
            copy.wait_send()


N_SEMS = 240


def layer_kernel(
    x_ref,
    dy_ref,
    qkv_ref,
    out_ref,
    up_ref,
    down_ref,
    gate_ref,
    gains_ref,
    biases_ref,
    mixed_ref,
    ingrad_ref,
    o_qkv_ref,
    o_out_ref,
    o_up_ref,
    o_down_ref,
    o_gate_ref,
    o_vec_ref,
    x_all,
    h1_all,
    w_all,
    out_all,
    up_all,
    down_all,
    gate_low,
    proj_t,
    k_nat,
    v_nat,
    s_buf,
    p_buf,
    ds_buf,
    o_t,
    o_low,
    lse,
    heads_t,
    g1_buf,
    attn_buf,
    x1_buf,
    xhat_buf,
    rstd_buf,
    h1_pair,
    h2_pair,
    g2_buf,
    act_buf,
    dgelu_buf,
    ffn_own,
    ffn_send,
    ffn_recv,
    dffn_pair,
    dz2_full,
    dz1_full,
    dattn_full,
    dz2_half,
    dz1_half,
    dattn_half,
    dhid_buf,
    dh2_own,
    dh2_send,
    dh2_recv,
    dh2_gate,
    dheads_t,
    do_t,
    vec,
    vec_a,
    vec_b,
    dq_t,
    dk_t,
    dv_t,
    dproj_low,
    dproj_all,
    gq_send,
    gq_recv,
    gq_all,
    su1,
    ru1,
    su2,
    ru2,
    su3,
    ru3,
    sd1,
    rd1,
    sd2,
    rd2,
    sd3,
    rd3,
    sg1,
    rg1,
    sg2,
    rg2,
    sg3,
    rg3,
    gout_all,
    gup_all,
    gdown_all,
    ggate_all,
    send_sems,
    recv_sems,
):
    dp, head = lax.axis_index("dp"), lax.axis_index("head")
    x_hi, y, core = dp // 8, (dp // 2) % 4, dp % 2
    z, x_lo = head // 2, head % 2
    xx = x_hi * 2 + x_lo
    sub = x_hi * 4 + y
    sibling = (x_hi * 8 + y * 2 + (1 - core), head)
    links = Links(send_sems, recv_sems)

    def head_peer(o):
        return (head + o) % 8

    def head_from(o):
        return (head + 8 - o) % 8

    def dp_peer(o):
        return (dp + o) % 16

    def dp_from(o):
        return (dp + 16 - o) % 16

    def ring(axis, o):
        nx = (xx + o) % 4 if axis == "x" else xx
        ny = (y + o) % 4 if axis == "y" else y
        nz = (z + o) % 4 if axis == "z" else z
        return ((nx // 2) * 8 + ny * 2 + core, nz * 2 + nx % 2)

    barrier = pltpu.get_barrier_semaphore()
    greeted = [(dp, head_peer(o)) for o in range(1, 8)]
    greeted += [(dp_peer(o), head) for o in range(1, 16)]
    greeted += [((1 - x_hi) * 8 + y * 2 + core, z * 2 + 1 - x_lo)]
    for device in greeted:
        pl.semaphore_signal(
            barrier, inc=1, device_id=device, device_id_type=pl.DeviceIdType.MESH
        )

    own = pl.ds(aligned(head * ROWS, ROWS), ROWS)
    own_core = pl.ds(aligned(core * ROWS, ROWS), ROWS)
    sib_core = pl.ds(aligned((1 - core) * ROWS, ROWS), ROWS)

    x_all[own, :] = x_ref[...]
    own_w = pl.ds(aligned(head * 192, 64), 192)
    for j in range(3):
        w_all[pl.ds(aligned(head * 192 + j * 64, 64), 64), :] = qkv_ref[j].T.astype(BF16)
    own_out = pl.ds(aligned(head * 64, 64), 64)
    out_all[own_out, :] = out_ref[...].astype(BF16)
    up_all[:, own] = up_ref[:, own_core].astype(BF16)
    down_all[own, :] = down_ref[own_core, :].astype(BF16)

    pl.semaphore_wait(barrier, len(greeted))

    x_copies = [
        links.start(x_ref, x_all.at[own, :], (dp, head_peer(o))) for o in range(1, 8)
    ]

    gate_low[...] = gate_ref[...].astype(BF16)
    gain_one, shift_one = gains_ref[0:1, :], biases_ref[0:1, :]
    gain_two, shift_two = gains_ref[1:2, :], biases_ref[1:2, :]

    def project(block):
        for s in range(4):
            rows = pl.ds(aligned(block * ROWS + 32 * s, 32), 32)
            v = x_all[rows, :].astype(F32)
            center = v - jnp.mean(v, axis=-1, keepdims=True)
            spread = jnp.mean(center * center, axis=-1, keepdims=True)
            h = center * lax.rsqrt(spread + NORM_EPS) * gain_one + shift_one
            h1_all[rows, :] = h.astype(BF16)
        rows = pl.ds(aligned(block * ROWS, ROWS), ROWS)
        pt = dot(w_all[own_w, :], h1_all[rows, :], NT)
        proj_t[0:64, rows] = (pt[0:64].astype(BF16).astype(F32) * 0.125).astype(BF16)
        proj_t[64:192, rows] = pt[64:192].astype(BF16)
        k_nat[rows, :] = pt[64:128].T.astype(BF16)
        v_nat[rows, :] = pt[128:192].T.astype(BF16)

    project(head)
    for o in range(1, 8):
        x_copies[o - 1].wait_recv()
        project(head_from(o))

    weight_copies = []
    for o in range(1, 8):
        to = (dp, head_peer(o))
        weight_copies.append(links.start(out_all.at[own_out, :], out_all.at[own_out, :], to))
    for o in range(1, 8):
        to = (dp, head_peer(o))
        weight_copies.append(links.start(up_all.at[:, own], up_all.at[:, own], to))
    for o in range(1, 8):
        to = (dp, head_peer(o))
        weight_copies.append(links.start(down_all.at[own, :], down_all.at[own, :], to))
    for o in range(1, 8):
        to = (dp, head_peer(o))
        weight_copies.append(links.start(w_all.at[own_w, :], w_all.at[own_w, :], to))

    h1_pair[own_core, :] = h1_all[own, :]
    h1_copy = links.start(h1_pair.at[own_core, :], h1_pair.at[own_core, :], sibling)

    for j in range(LEN // QB):
        cols = slice(QB * j, QB * (j + 1))
        queries = proj_t[0:64, cols]
        ceiling = jnp.full((1, QB), -1e30, F32)
        tiles = QB * (j + 1) // ROWS
        for t in range(tiles):
            s = dot(k_nat[ROWS * t : ROWS * (t + 1), :], queries)
            if ROWS * t >= QB * j:
                keys_at = lax.broadcasted_iota(jnp.int32, (ROWS, QB), 0) + ROWS * t
                queries_at = lax.broadcasted_iota(jnp.int32, (ROWS, QB), 1) + QB * j
                s = jnp.where(keys_at <= queries_at, s, -1e30)
            s_buf[ROWS * t : ROWS * (t + 1), :] = s
            ceiling = jnp.maximum(ceiling, jnp.max(s, axis=0, keepdims=True))
        mass = jnp.zeros((1, QB), F32)
        for t in range(tiles):
            e = jnp.exp(s_buf[ROWS * t : ROWS * (t + 1), :] - ceiling)
            mass = mass + jnp.sum(e, axis=0, keepdims=True)
            p_buf[ROWS * t : ROWS * (t + 1), :] = e.astype(BF16)
        total = dot(proj_t[128:192, 0 : QB * (j + 1)], p_buf[0 : QB * (j + 1), :])
        total = total / mass
        o_t[:, cols] = total
        o_low[:, cols] = total.astype(BF16)
        lse[:, cols] = ceiling + jnp.log(mass)

    own_heads = pl.ds(aligned(head * 64, 64), 64)
    heads_copies = []
    for o in range(1, 8):
        peer = head_peer(o)
        block = o_low.at[:, pl.ds(aligned(peer * ROWS, ROWS), ROWS)]
        heads_copies.append(links.start(block, heads_t.at[own_heads, own_core], (dp, peer)))
    heads_t[own_heads, own_core] = o_low[:, own]

    h1_own = h1_all[own, :]
    g1_buf[...] = dot(h1_own, gate_low[0]) + biases_ref[2:3, :]
    for c in heads_copies:
        c.wait_recv()
    headst_copy = links.start(heads_t.at[:, own_core], heads_t.at[:, own_core], sibling)
    for c in weight_copies[0:7]:
        c.wait_recv()
    attn_buf[...] = dot(heads_t[:, own_core], out_all[...], TN)
    for s in range(4):
        rows = slice(32 * s, 32 * s + 32)
        g1 = jax.nn.sigmoid(g1_buf[rows, :])
        g1_buf[rows, :] = g1
        x = x_ref[rows, :].astype(F32)
        x1 = g1 * attn_buf[rows, :] + (1.0 - g1) * x
        x1_buf[rows, :] = x1
        center = x1 - jnp.mean(x1, axis=-1, keepdims=True)
        spread = jnp.mean(center * center, axis=-1, keepdims=True)
        rstd = lax.rsqrt(spread + NORM_EPS)
        xhat = center * rstd
        xhat_buf[rows, :] = xhat
        rstd_buf[rows, :] = jnp.broadcast_to(rstd, (32, 128))
        h2 = xhat * gain_two + shift_two
        h2_pair[pl.ds(aligned(core * ROWS + 32 * s, 32), 32), :] = h2.astype(BF16)
    h2_copy = links.start(h2_pair.at[own_core, :], h2_pair.at[own_core, :], sibling)
    g2_buf[...] = dot(h2_pair[own_core, :], gate_low[1]) + biases_ref[3:4, :]
    for c in weight_copies[7:14]:
        c.wait_recv()
    h2_copy.wait_recv()
    for n in range(4):
        cols = slice(256 * n, 256 * n + 256)
        u = dot(h2_pair[...], up_all[:, cols])
        c0 = 0.7978845608028654
        inner = jnp.tanh(c0 * (u + 0.044715 * u * u * u))
        act_buf[:, cols] = (0.5 * u * (1.0 + inner)).astype(BF16)
        dgelu_buf[:, cols] = 0.5 * (1.0 + inner) + 0.5 * u * (1.0 - inner * inner) * c0 * (
            1.0 + 3.0 * 0.044715 * u * u
        )
    for c in weight_copies[14:21]:
        c.wait_recv()
    ffn_send[...] = dot(act_buf[sib_core, :], down_all[...]).astype(BF16)
    ffn_copy = links.start(ffn_send, ffn_recv, sibling)
    ffn_own[...] = dot(act_buf[own_core, :], down_all[...])
    ffn_copy.wait_recv()
    bias_two = jnp.zeros((1, D), F32)
    for s in range(4):
        rows = slice(32 * s, 32 * s + 32)
        ffn = ffn_own[rows, :] + ffn_recv[rows, :].astype(F32)
        g2 = jax.nn.sigmoid(g2_buf[rows, :])
        g2_buf[rows, :] = g2
        x1 = x1_buf[rows, :]
        dy = dy_ref[rows, :].astype(F32)
        mixed_ref[rows, :] = g2 * ffn + (1.0 - g2) * x1
        dffn_pair[pl.ds(aligned(core * ROWS + 32 * s, 32), 32), :] = (g2 * dy).astype(BF16)
        dz = (dy * (ffn - x1) * g2 * (1.0 - g2)).astype(BF16)
        dz2_full[rows, :] = dz
        bias_two = bias_two + jnp.sum(dz.astype(F32), axis=0, keepdims=True)
    dffn_copy = links.start(dffn_pair.at[own_core, :], dffn_pair.at[own_core, :], sibling)
    half = pl.ds(aligned(core * 256, 256), 256)
    sib_half = pl.ds(aligned((1 - core) * 256, 256), 256)
    dz2_half[own_core, :] = dz2_full[:, half]
    dz2_copy = links.start(dz2_full.at[:, sib_half], dz2_half.at[own_core, :], sibling)
    dh2_gate[...] = dot(dz2_full[...], gate_low[1], NT)
    dffn_copy.wait_recv()
    for n in range(4):
        cols = slice(256 * n, 256 * n + 256)
        da = dot(dffn_pair[...], down_all[cols, :], NT)
        dhid_buf[:, cols] = (da * dgelu_buf[:, cols]).astype(BF16)
    dh2_send[...] = dot(dhid_buf[sib_core, :], up_all[...], NT).astype(BF16)
    dh2_copy = links.start(dh2_send, dh2_recv, sibling)
    dh2_own[...] = dot(dhid_buf[own_core, :], up_all[...], NT)
    dh2_copy.wait_recv()
    gain_sum = jnp.zeros((1, D), F32)
    shift_sum = jnp.zeros((1, D), F32)
    bias_one = jnp.zeros((1, D), F32)
    for s in range(4):
        rows = slice(32 * s, 32 * s + 32)
        dh2 = dh2_own[rows, :] + dh2_recv[rows, :].astype(F32) + dh2_gate[rows, :]
        xhat = xhat_buf[rows, :]
        gain_sum = gain_sum + jnp.sum(dh2 * xhat, axis=0, keepdims=True)
        shift_sum = shift_sum + jnp.sum(dh2, axis=0, keepdims=True)
        dxhat = dh2 * gain_two
        mean_a = jnp.mean(dxhat, axis=-1, keepdims=True)
        mean_b = jnp.mean(dxhat * xhat, axis=-1, keepdims=True)
        rstd = rstd_buf[rows, 0:1]
        dx1 = (1.0 - g2_buf[rows, :]) * dy_ref[rows, :].astype(F32) + rstd * (
            dxhat - mean_a - xhat * mean_b
        )
        g1 = g1_buf[rows, :]
        dattn_full[rows, :] = (g1 * dx1).astype(BF16)
        x = x_ref[rows, :].astype(F32)
        dz = (dx1 * (attn_buf[rows, :] - x) * g1 * (1.0 - g1)).astype(BF16)
        dz1_full[rows, :] = dz
        bias_one = bias_one + jnp.sum(dz.astype(F32), axis=0, keepdims=True)
        ingrad_ref[rows, :] = (1.0 - g1) * dx1
    vec[1:2, :] = gain_sum
    vec[3:4, :] = shift_sum
    vec[4:5, :] = bias_one
    vec[5:6, :] = bias_two
    vec[6:8, :] = jnp.zeros((2, D), F32)

    dheads_t[...] = dot(out_all[...], dattn_full[...], NT).astype(BF16)
    dheads_copies = []
    for o in range(1, 8):
        peer = head_peer(o)
        block = dheads_t.at[pl.ds(aligned(peer * 64, 64), 64), :]
        dheads_copies.append(links.start(block, do_t.at[:, own], (dp, peer)))
    do_t[:, own] = dheads_t[own_heads, :]
    dz1_half[own_core, :] = dz1_full[:, half]
    dz1_copy = links.start(dz1_full.at[:, sib_half], dz1_half.at[own_core, :], sibling)
    dattn_half[own_core, :] = dattn_full[:, half]
    dattn_copy = links.start(dattn_full.at[:, sib_half], dattn_half.at[own_core, :], sibling)

    for h in range(8):
        cols = slice(128 * h, 128 * h + 128)
        gu = dot(h2_pair[...], dhid_buf[:, cols], TN).astype(BF16)
        gd = dot(act_buf[:, cols], dffn_pair[...], TN).astype(BF16)
        for g in range(8):
            ch_x, ch_y, ch_z = (g // 4) * 2 + h % 2, g % 4, h // 2
            su1[ch_z * 16 + ch_y * 4 + ch_x] = gu[64 * g : 64 * g + 64, :]
            sd1[ch_y * 16 + ch_x * 4 + ch_z] = gd[16 * g : 16 * g + 16, :]

    def stage(axis, at, src, dst, size):
        copies = []
        for o in range(1, 4):
            t = (at + o) % 4
            copies.append(
                links.start(
                    src.at[pl.ds(t * size, size)],
                    dst.at[pl.ds((o - 1) * size, size)],
                    ring(axis, o),
                )
            )
        return copies

    def gather(copies, at, src, got, size, store):
        for c in copies:
            c.wait_recv()

        def add(i, carry):
            total = src[at * size + i].astype(F32)
            for o in range(3):
                total = total + got[o * size + i].astype(F32)
            store(i, total)
            return carry

        lax.fori_loop(0, size, add, 0)

    up_copies = stage("z", z, su1, ru1, 16)
    down_copies = stage("y", y, sd1, rd1, 16)

    for c in (h1_copy, headst_copy, dz2_copy, dz1_copy, dattn_copy):
        c.wait_recv()
    gates = (
        dot(h1_pair[...], dz1_half[...], TN).astype(BF16),
        dot(h2_pair[...], dz2_half[...], TN).astype(BF16),
    )
    go = dot(heads_t[...], dattn_half[...]).astype(BF16)
    for h in range(8):
        for g in range(8):
            ch = ((g // 4) * 2 + h % 2) * 16 + (h // 2) * 4 + g % 4
            q = 16 * (8 * h + g)
            sg1[ch, :, 0:256] = gates[q // 512][q % 512 : q % 512 + 16, :]
            r = 64 * h + 16 * (g % 4)
            sg1[ch, :, 256:384] = go[r : r + 16, 128 * (g // 4) : 128 * (g // 4) + 128]
    gate_copies = stage("x", xx, sg1, rg1, 16)

    for c in dheads_copies:
        c.wait_recv()
    dk_t[...] = jnp.zeros_like(dk_t)
    dv_t[...] = jnp.zeros_like(dv_t)
    for j in range(LEN // QB):
        cols = slice(QB * j, QB * (j + 1))
        upto = QB * (j + 1)
        queries = proj_t[0:64, cols]
        grads = do_t[:, cols]
        delta = jnp.sum(o_t[:, cols] * grads.astype(F32), axis=0, keepdims=True)
        row_lse = lse[:, cols]
        for t in range(upto // ROWS):
            keys = slice(ROWS * t, ROWS * (t + 1))
            p = jnp.exp(dot(k_nat[keys, :], queries) - row_lse)
            if ROWS * t >= QB * j:
                keys_at = lax.broadcasted_iota(jnp.int32, (ROWS, QB), 0) + ROWS * t
                queries_at = lax.broadcasted_iota(jnp.int32, (ROWS, QB), 1) + QB * j
                p = jnp.where(keys_at <= queries_at, p, 0.0)
            d = dot(v_nat[keys, :], grads)
            p_buf[keys, :] = p.astype(BF16)
            ds_buf[keys, :] = (p * (d - delta)).astype(BF16)
        dq_t[:, cols] = dot(proj_t[64:128, 0:upto], ds_buf[0:upto, :]) * 0.125
        dk_t[:, 0:upto] += dot(queries, ds_buf[0:upto, :], NT)
        dv_t[:, 0:upto] += dot(grads, p_buf[0:upto, :], NT)
    dproj_low[0:64, :] = dq_t[...].astype(BF16)
    dproj_low[64:128, :] = dk_t[...].astype(BF16)
    dproj_low[128:192, :] = dv_t[...].astype(BF16)

    dproj_copies = []
    for o in range(1, 8):
        peer = head_peer(o)
        block = dproj_low.at[:, pl.ds(aligned(peer * ROWS, ROWS), ROWS)]
        dproj_copies.append(links.start(block, dproj_all.at[own_w, :], (dp, peer)))
    dproj_all[own_w, :] = dproj_low[:, own]

    gq = dot(dproj_low[...], h1_all[...]).astype(BF16)
    for i in range(16):
        r, c = 48 * (i // 4), 128 * (i % 4)
        gq_send[i] = gq[r : r + 48, c : c + 128]
    gq_copies = []
    for o in range(1, 16):
        peer = dp_peer(o)
        gq_copies.append(links.start(gq_send.at[peer], gq_recv.at[o - 1], (peer, head)))

    def to_bf16(ref):
        def store(i, total):
            ref[i] = total.astype(BF16)

        return store

    gather(up_copies, z, su1, ru1, 16, to_bf16(su2))
    up_copies = stage("y", y, su2, ru2, 4)
    gather(down_copies, y, sd1, rd1, 16, to_bf16(sd2))
    down_copies = stage("x", xx, sd2, rd2, 4)
    gather(gate_copies, xx, sg1, rg1, 16, to_bf16(sg2))
    gate_copies = stage("z", z, sg2, rg2, 4)

    for c in dproj_copies:
        c.wait_recv()
    for c in weight_copies[21:28]:
        c.wait_recv()
    dh2_own[...] = dot(dproj_all[...], w_all[...], TN) + dot(dz1_full[...], gate_low[0], NT)
    gain_sum = jnp.zeros((1, D), F32)
    shift_sum = jnp.zeros((1, D), F32)
    for s in range(4):
        rows = slice(32 * s, 32 * s + 32)
        v = x_ref[rows, :].astype(F32)
        center = v - jnp.mean(v, axis=-1, keepdims=True)
        spread = jnp.mean(center * center, axis=-1, keepdims=True)
        rstd = lax.rsqrt(spread + NORM_EPS)
        xhat = center * rstd
        dh = dh2_own[rows, :]
        gain_sum = gain_sum + jnp.sum(dh * xhat, axis=0, keepdims=True)
        shift_sum = shift_sum + jnp.sum(dh, axis=0, keepdims=True)
        dxhat = dh * gain_one
        mean_a = jnp.mean(dxhat, axis=-1, keepdims=True)
        mean_b = jnp.mean(dxhat * xhat, axis=-1, keepdims=True)
        ingrad_ref[rows, :] += rstd * (dxhat - mean_a - xhat * mean_b)
    vec[0:1, :] = gain_sum
    vec[2:3, :] = shift_sum
    vec_copies = [
        links.start(vec, vec_a.at[o - 1], (dp, head_peer(o))) for o in range(1, 8)
    ]

    for c in gq_copies:
        c.wait_recv()
    total = gq_send[dp].astype(F32)
    for o in range(15):
        total = total + gq_recv[o].astype(F32)
    gq_rows = pl.ds(aligned((dp // 4) * 48, 48), 48)
    gq_cols = pl.ds(aligned((dp % 4) * 128, 128), 128)
    gq_all[gq_rows, gq_cols] = total.astype(BF16)
    gq_copies = []
    for o in range(1, 16):
        block = gq_all.at[gq_rows, gq_cols]
        gq_copies.append(links.start(block, block, (dp_peer(o), head)))

    gather(up_copies, y, su2, ru2, 4, to_bf16(su3))
    up_copies = stage("x", xx, su3, ru3, 1)
    gather(down_copies, xx, sd2, rd2, 4, to_bf16(sd3))
    down_copies = stage("z", z, sd3, rd3, 1)
    gather(gate_copies, z, sg2, rg2, 4, to_bf16(sg3))
    gate_copies = stage("y", y, sg3, rg3, 1)

    for c in vec_copies:
        c.wait_recv()
    total = vec[...]
    for o in range(7):
        total = total + vec_a[o]
    vec_b[15] = total
    vec_copies = [
        links.start(vec_b.at[15], vec_b.at[o - 1], (dp_peer(o), head)) for o in range(1, 16)
    ]

    up_rows = pl.ds(aligned(sub * 64, 64), 64)
    down_rows = pl.ds(aligned(core * 128 + sub * 16, 16), 16)
    out_rows = pl.ds(aligned(y * 16, 16), 16)
    out_cols = pl.ds(aligned(core * 256 + x_hi * 128, 128), 128)
    gate_rows = pl.ds(aligned(head * 128 + sub * 16, 16), 16)

    def store_up(i, total):
        gup_all[up_rows, own_core] = total.astype(BF16)

    def store_down(i, total):
        gdown_all[down_rows, :] = total.astype(BF16)

    def store_gate(i, total):
        ggate_all[gate_rows, half] = total[:, 0:256].astype(BF16)
        gout_all[out_rows, out_cols] = total[:, 256:384].astype(BF16)

    last_copies, gate_gather = [], []
    gather(gate_copies, y, sg3, rg3, 1, store_gate)
    for o in range(1, 16):
        to = (dp_peer(o), head)
        block = ggate_all.at[gate_rows, half]
        gate_gather.append(links.start(block, block, to))
    for o in range(1, 16):
        to = (dp_peer(o), head)
        block = gout_all.at[out_rows, out_cols]
        last_copies.append(links.start(block, block, to))
    gather(up_copies, xx, su3, ru3, 1, store_up)
    for o in range(1, 16):
        to = (dp_peer(o), head)
        block = gup_all.at[up_rows, own_core]
        last_copies.append(links.start(block, block, to))
    gather(down_copies, z, sd3, rd3, 1, store_down)
    for o in range(1, 16):
        to = (dp_peer(o), head)
        block = gdown_all.at[down_rows, :]
        last_copies.append(links.start(block, block, to))
    for c in gate_gather:
        c.wait_recv()
    block = ggate_all.at[own, :]
    for o in range(1, 8):
        last_copies.append(links.start(block, block, (dp, head_peer(o))))

    for c in vec_copies:
        c.wait_recv()
    total = vec_b[15]
    for o in range(15):
        total = total + vec_b[o]
    o_vec_ref[...] = total
    for c in gq_copies + last_copies:
        c.wait_recv()
    o_qkv_ref[...] = gq_all[...]
    o_out_ref[...] = gout_all[...]
    o_up_ref[...] = gup_all[...]
    o_down_ref[...] = gdown_all[...]
    o_gate_ref[...] = ggate_all[...]
    links.drain()


VMEM = pl.BlockSpec(memory_space=pltpu.VMEM)


def run_layer(*args):
    shapes = [
        ((ROWS, D), F32),
        ((ROWS, D), F32),
        ((192, D), BF16),
        ((64, D), BF16),
        ((D, 256), BF16),
        ((256, D), BF16),
        ((LEN, D), BF16),
        ((8, D), F32),
    ]
    scratch = [
        ((LEN, D), BF16),
        ((LEN, D), BF16),
        ((1536, D), BF16),
        ((D, D), BF16),
        ((D, 1024), BF16),
        ((1024, D), BF16),
        ((2, D, D), BF16),
        ((192, LEN), BF16),
        ((LEN, 64), BF16),
        ((LEN, 64), BF16),
        ((LEN, QB), F32),
        ((LEN, QB), BF16),
        ((LEN, QB), BF16),
        ((64, LEN), F32),
        ((64, LEN), BF16),
        ((1, LEN), F32),
        ((D, 256), BF16),
        ((ROWS, D), F32),
        ((ROWS, D), F32),
        ((ROWS, D), F32),
        ((ROWS, D), F32),
        ((ROWS, 128), F32),
        ((256, D), BF16),
        ((256, D), BF16),
        ((ROWS, D), F32),
        ((256, 1024), BF16),
        ((256, 1024), F32),
        ((ROWS, D), F32),
        ((ROWS, D), BF16),
        ((ROWS, D), BF16),
        ((256, D), BF16),
        ((ROWS, D), BF16),
        ((ROWS, D), BF16),
        ((ROWS, D), BF16),
        ((256, 256), BF16),
        ((256, 256), BF16),
        ((256, 256), BF16),
        ((256, 1024), BF16),
        ((ROWS, D), F32),
        ((ROWS, D), BF16),
        ((ROWS, D), BF16),
        ((ROWS, D), F32),
        ((D, ROWS), BF16),
        ((64, LEN), BF16),
        ((8, D), F32),
        ((7, 8, D), F32),
        ((16, 8, D), F32),
        ((64, LEN), F32),
        ((64, LEN), F32),
        ((64, LEN), F32),
        ((192, LEN), BF16),
        ((1536, ROWS), BF16),
        ((16, 48, 128), BF16),
        ((15, 48, 128), BF16),
        ((192, D), BF16),
    ]
    for rows, cols in ((64, 128), (16, 512), (16, 384)):
        for count in (64, 48, 16, 12, 4, 3):
            scratch.append(((count, rows, cols), BF16))
    scratch += [
        ((64, D), BF16),
        ((D, 256), BF16),
        ((256, D), BF16),
        ((LEN, D), BF16),
    ]
    return pl.pallas_call(
        layer_kernel,
        out_shape=[jax.ShapeDtypeStruct(s, t) for s, t in shapes],
        in_specs=[VMEM] * 9,
        out_specs=[VMEM] * len(shapes),
        scratch_shapes=[pltpu.VMEM(s, t) for s, t in scratch]
        + [pltpu.SemaphoreType.DMA((N_SEMS,)), pltpu.SemaphoreType.DMA((N_SEMS,))],
        compiler_params=pltpu.CompilerParams(
            collective_id=0, has_side_effects=True, vmem_limit_bytes=60 * 1024 * 1024
        ),
        name="layer",
    )(*args)


def adamw(weight, first, second, grad, rate):
    first = BETA_ONE * first + (1.0 - BETA_ONE) * grad
    second = BETA_TWO * second + (1.0 - BETA_TWO) * grad * grad
    first_hat = first / (1.0 - BETA_ONE**STEP)
    second_hat = second / (1.0 - BETA_TWO**STEP)
    weight = weight - rate * (first_hat / (jnp.sqrt(second_hat) + ADAM_EPS) + DECAY * weight)
    return (weight, first, second)


def adamw_kernel(*refs):
    states, grads, outs = refs[0:21], refs[21:27], refs[27:48]
    for i in range(7):
        w, m, v = (r[...] for r in states[3 * i : 3 * i + 3])
        if i == 0:
            g = jnp.stack([grads[0][64 * j : 64 * j + 64, :].astype(F32).T for j in range(3)])
        elif i == 5:
            g = grads[5][0:2, :]
        elif i == 6:
            g = grads[5][2:6, :]
        else:
            g = grads[i][...].astype(F32)
        for ref, value in zip(outs[3 * i : 3 * i + 3], adamw(w, m, v, g, RATES[i])):
            ref[...] = value


GRID = 4


def run_adamw(states, grads):
    blocks = [
        ((3, D // GRID, 64), lambda i: (0, i, 0)),
        ((64 // GRID, D), lambda i: (i, 0)),
        ((D // GRID, 256), lambda i: (i, 0)),
        ((256 // GRID, D), lambda i: (i, 0)),
        ((LEN // GRID, D), lambda i: (i, 0)),
        ((2, D), lambda i: (0, 0)),
        ((4, D), lambda i: (0, 0)),
    ]
    state_specs = [pl.BlockSpec(*b) for b in blocks for _ in range(3)]
    grad_specs = [
        pl.BlockSpec((192, D // GRID), lambda i: (0, i)),
        *(pl.BlockSpec(*b) for b in blocks[1:5]),
        pl.BlockSpec((8, D), lambda i: (0, 0)),
    ]
    return pl.pallas_call(
        adamw_kernel,
        grid=(GRID,),
        out_shape=[jax.ShapeDtypeStruct(s.shape, F32) for s in states],
        in_specs=state_specs + grad_specs,
        out_specs=state_specs,
        compiler_params=pltpu.CompilerParams(vmem_limit_bytes=56 * 1024 * 1024),
        name="adamw",
    )(*states, *grads)


def local(inputs, cotangent, *state):
    rows = inputs.shape[1]
    weights = [state[3 * i] for i in range(7)]
    results = run_layer(
        inputs.reshape(rows, D),
        cotangent.reshape(rows, D),
        *weights,
    )
    mixed, ingrad, gq, gout, gup, gdown, ggate, gvec = results
    flat = list(state)
    for i in (12, 13, 14):
        flat[i] = flat[i].reshape(2 * D, D)
    new = list(run_adamw(flat, (gq, gout, gup, gdown, ggate, gvec)))
    for i in (12, 13, 14):
        new[i] = new[i].reshape(2, D, D)
    return (mixed.reshape(1, rows, D), ingrad.reshape(1, rows, D), *new)


def solution(mesh):
    batch = P("dp", "head", None)
    qkv = P(None, None, "head")
    first = P("head", None)
    second = P(None, "head")
    state = (qkv,) * 3 + (first,) * 3 + (second,) * 3 + (first,) * 3 + (P(),) * 9
    return jax.shard_map(
        local,
        mesh=mesh,
        in_specs=(batch, batch, *state),
        out_specs=(batch, batch, *state),
        check_vma=False,
    )
```

time: 598 us -> 165 us (0.28)
  waiting for transfers between devices: 412 us -> 0 us
  Pallas kernels: 0 us -> 152 us
  other arithmetic: 44.7 us -> 0 us
  matrix products: 43.7 us -> 0 us
  blocking collectives: 38.3 us -> 0 us
  local copies, waits for them, and re-layouts: 34.5 us -> 12.3 us
  between operations: 14.7 us -> 0.71 us
  loops' own time: 8.08 us -> 0 us
    psum x4 -> x0, waiting for transfers between devices: 344 us -> none  [the longest x3 245 us: head_total(): lax.psum(partial_value.astype(jnp.bfloat16), 'head').astype(jnp.float32)]
    pallas_call x0 -> x2, Pallas kernels: none -> 152 us  [the longest x1 139 us: run_layer(): pl.pallas_call(layer_kernel, out_shape=[jax.ShapeDtypeStruct(s, t) for s,...]
    all_gather x2 -> x0, waiting for transfers between devices: 67.3 us -> none  [the longest x1 36.6 us: local(): lax.all_gather(inputs, 'head', axis=1, tiled=True)]
    dot_general x31 -> x0, matrix products: 43.1 us -> none  [the longest x1 4.21 us: local(): jnp.einsum('bld,de->ble', h1_rows, gate_low[0], preferred_element_type=jn...]
    psum x1 -> x0, blocking collectives: 38.3 us -> none  [local(): lax.psum(grad_gains.astype(jnp.bfloat16), 'dp').astype(jnp.float32)]
    sub x9 -> x0, other arithmetic: 19.6 us -> none  [the longest x7 14.8 us: adamw(): weight - rate * (first_hat / (jnp.sqrt(second_hat) + ADAM_EPS) + DECAY *...]
    reduce_sum x9 -> x0, other arithmetic: 14.1 us -> none  [the longest x1 4.77 us: local(): grad_bias_two = jnp.sum(grad_z_two.astype(jnp.float32), axis=(0, 1))]
    another operation x2 -> x0, loops' own time: 8.08 us -> none  [the longest x1 4.1 us: attend_backward(): lax.scan(block_step, (zeros, zeros), (starts, log_total))]
  transfers between devices with their start and end apart: 6 -> 0, of which waited for: 6 -> 0; matrix products, arithmetic and copies ran while one was open for 8% -> 0% of each run, Pallas kernels for 0% -> 0%
where the time goes in v1:
time: 165 us
  Pallas kernels  152 us (92%)
  local copies, waits for them, and re-layouts  12.3 us (7%)
    pallas_call x1, Pallas kernels, run_layer(): pl.pallas_call(layer_kernel, out_shape=[jax.ShapeDtypeStruct(s, t) for s,...  139 us
    pallas_call x1, Pallas kernels, run_adamw(): pl.pallas_call(adamw_kernel, grid=(GRID,), out_shape=[jax.ShapeDtypeStruc...  12.9 us
    unnamed x16, local copies, waits for them, and re-layouts  12.3 us

profile of v1, /device:TPU:1, one launch (start us, length us, event | category | flops | bytes accessed | tf_op | source)
XLA Modules:
  0.0 164.7 jit_solution(9656444598717336582)
XLA Ops:
  0.7 0.0 copy-start.1
  0.7 2.2 %copy.46.qkv_ref.refs_0_ = f32[3,512,64]{2,1,0:T(8,128)} copy(f32[3,512,64]{1,2,0:T(8,128)} %param.25) | data formatting | bytes 786432 | tf_op args[2]
  2.9 2.1 %copy.48.refs_1_ = f32[3,512,64]{2,1,0:T(8,128)} copy(f32[3,512,64]{1,2,0:T(8,128)} %param.26) | data formatting | bytes 786432 | tf_op args[3]
  5.0 0.0 copy-done.1
  5.0 1.2 copy.49.refs_2_
  6.2 138.8 %layer.1 = (f32[128,512]{1,0:T(8,128)}, f32[128,512]{1,0:T(8,128)}, bf16[192,512]{1,0:T(8,128)(2,1)}, bf16[64,512]{1,0:T(8,128)(2,1)}, bf16[512,256]{1,0:T(8,128...) custom-call(bf16[128,512]{1,0:T(8,128)(2,1)} %bitcast.15, ...), custom_call_target="tpu_custom_call" | custom-call | tf_op jit(solution)/shard_map/layer/pallas_call | solution.py:703
  145.0 12.9 %adamw.1 = (f32[3,512,64]{2,1,0:T(8,128)}, f32[3,512,64]{2,1,0:T(8,128)}, f32[3,512,64]{2,1,0:T(8,128)}, f32[64,512]{1,0:T(8,128)}, f32[64,512]{1,0:T(8,128)}, /...) custom-call(f32[3,512,64]{2,1,0:T(8,128)} %copy.46.qkv_ref.refs_0_, ...), custom_call_target="tpu_custom_call" | custom-call | tf_op jit(solution)/shard_map/adamw/pallas_call | solution.py:761
  157.9 0.0 copy-start
  157.9 0.0 copy-start.3
  157.9 0.0 copy-start.2
  157.9 2.2 %copy.50 = f32[3,512,64]{1,2,0:T(8,128)} copy(f32[3,512,64]{2,1,0:T(8,128)} %get-tuple-element.83) | data formatting | bytes 786432
  160.1 2.1 %copy.51 = f32[3,512,64]{1,2,0:T(8,128)} copy(f32[3,512,64]{2,1,0:T(8,128)} %get-tuple-element.84) | data formatting | bytes 786432
  162.3 0.0 copy-done
  162.3 1.0 copy.52
  163.3 0.0 copy-done.3
  163.3 0.7 copy.55
  164.0 0.0 copy-done.2
  164.0 0.7 copy.56
Async XLA Ops:
  0.7 4.4 %copy-start.1 = (f32[3,512,64]{1,2,0:T(8,128)S(1)}, f32[3,512,64]{1,2,0:T(8,128)}, u32[]{:S(2)}) copy-start(f32[3,512,64]{1,2,0:T(8,128)} %param.27) | copy-start | bytes 1179652
  157.9 4.4 %copy-start = (f32[3,512,64]{2,1,0:T(8,128)S(1)}, f32[3,512,64]{2,1,0:T(8,128)}, u32[]{:S(2)}) copy-start(f32[3,512,64]{2,1,0:T(8,128)} %get-tuple-element.85) | copy-start | bytes 1179652
  157.9 5.4 %copy-start.3 = (f32[128,512]{1,0:T(8,128)S(1)}, f32[128,512]{1,0:T(8,128)}, u32[]{:S(2)}) copy-start(f32[128,512]{1,0:T(8,128)} %get-tuple-element.52) | copy-start | bytes 786436
  157.9 6.1 %copy-start.2 = (f32[128,512]{1,0:T(8,128)S(1)}, f32[128,512]{1,0:T(8,128)}, u32[]{:S(2)}) copy-start(f32[128,512]{1,0:T(8,128)} %get-tuple-element.53) | copy-start | bytes 786436

commit v2 on v1

v2 whole, which is shorter than its diff:
```python
import jax
import jax.numpy as jnp
from jax import lax
from jax.experimental import pallas as pl
from jax.experimental.pallas import tpu as pltpu
from jax.sharding import PartitionSpec as P

F32 = jnp.float32
BF16 = jnp.bfloat16
STEP = 10
NORM_EPS = 1e-05
BETA_ONE = 0.9
BETA_TWO = 0.999
ADAM_EPS = 1e-08
DECAY = 0.01
RATES = (0.04, 0.1, 0.04, 0.02, 0.04, 0.4, 0.3)
D = 512
ROWS = 128
LEN = 1024
QB = 256
NN = ((1,), (0,))
NT = ((1,), (1,))
TN = ((0,), (0,))


def dot(a, b, dims=NN):
    return lax.dot_general(a, b, (dims, ((), ())), preferred_element_type=F32)


def aligned(value, by):
    return pl.multiple_of(value, by)


class Group:
    def __init__(self, links, total, receives=1, each=None):
        self.send_sem, self.total = links.semaphore(), total
        self.each = total if each is None else each
        self.recv_sems = [links.semaphore() for _ in range(receives)]
        links.groups.append(self)

    def send(self, src, dst, device, k=0):
        pltpu.make_async_remote_copy(
            src_ref=src,
            dst_ref=dst,
            send_sem=self.send_sem,
            recv_sem=self.recv_sems[k],
            device_id=device,
            device_id_type=pl.DeviceIdType.MESH,
        ).start()

    def wait(self, k=0):
        pltpu.make_async_copy(self.each, self.each, self.recv_sems[k]).wait()


class Links:
    def __init__(self, sems):
        self.sems, self.used, self.groups = sems, 0, []

    def semaphore(self):
        self.used += 1
        return self.sems.at[self.used - 1]

    def drain(self):
        for g in self.groups:
            pltpu.make_async_copy(g.total, g.total, g.send_sem).wait()


N_SEMS = 128
N_LOCAL = 32


def layer_kernel(
    x_hbm,
    dy_hbm,
    gains_hbm,
    biases_hbm,
    qkv_hbm,
    out_hbm,
    up_hbm,
    down_hbm,
    gate_hbm,
    *rest,
):
    states = [r for i, w in enumerate((qkv_hbm, out_hbm, up_hbm, down_hbm, gate_hbm)) for r in (w, *rest[2 * i : 2 * i + 2])]
    kept = rest[18:33]
    layer_body(x_hbm, dy_hbm, gains_hbm, biases_hbm, qkv_hbm, out_hbm, up_hbm, down_hbm, gate_hbm, *rest[10:18], states, kept, *rest[33:])


def layer_body(
    x_hbm,
    dy_hbm,
    gains_hbm,
    biases_hbm,
    qkv_hbm,
    out_hbm,
    up_hbm,
    down_hbm,
    gate_hbm,
    mixed_ref,
    ingrad_ref,
    o_qkv_ref,
    o_out_ref,
    o_up_ref,
    o_down_ref,
    o_gate_ref,
    o_vec_ref,
    states,
    kept,
    x_ref,
    dy_ref,
    gains_ref,
    biases_ref,
    qkv_ref,
    out_ref,
    up_ref,
    down_ref,
    gate_ref,
    x_all,
    h1_all,
    w_all,
    out_all,
    up_all,
    down_all,
    gate_low,
    proj_t,
    k_nat,
    v_nat,
    s_buf,
    p_buf,
    ds_buf,
    o_t,
    o_low,
    lse,
    heads_t,
    g1_buf,
    attn_buf,
    x1_buf,
    xhat_buf,
    rstd_buf,
    h1_pair,
    h2_pair,
    g2_buf,
    act_buf,
    dgelu_buf,
    ffn_own,
    ffn_send,
    ffn_recv,
    dffn_pair,
    dz2_full,
    dz1_full,
    dattn_full,
    dz2_half,
    late_half,
    dhid_buf,
    dh2_own,
    dh2_send,
    dh2_recv,
    dh2_gate,
    dheads_t,
    do_t,
    vec,
    vec_s,
    vec_a,
    vec_b,
    dq_t,
    dk_t,
    dv_t,
    dproj_low,
    dproj_all,
    gq_low,
    gq_sib,
    gq_send,
    gq_recv,
    gq_all,
    gates_low,
    gates_recv,
    gates_sum,
    gout_low,
    gout_recv,
    gout_sum,
    gout_all,
    gup_all,
    gdown_all,
    ggate_all,
    su1,
    ru1,
    su2,
    ru2,
    su3,
    ru3,
    sd1,
    rd1,
    sd2,
    rd2,
    sd3,
    rd3,
    sems,
    local_sems,
):
    loads = [
        pltpu.make_async_copy(src, dst, local_sems.at[i])
        for i, (src, dst) in enumerate(
            (
                (x_hbm, x_ref),
                (qkv_hbm, qkv_ref),
                (out_hbm, out_ref),
                (up_hbm, up_ref),
                (down_hbm, down_ref),
                (gains_hbm, gains_ref),
                (biases_hbm, biases_ref),
                (gate_hbm, gate_ref),
                (dy_hbm, dy_ref),
            )
        )
    ]
    for load in loads:
        load.start()
    keeps = [
        pltpu.make_async_copy(src, dst, local_sems.at[14 + i])
        for i, (src, dst) in enumerate(zip(states, kept))
    ]

    dp, head = lax.axis_index("dp"), lax.axis_index("head")
    x_hi, y, core = dp // 8, (dp // 2) % 4, dp % 2
    z, x_lo = head // 2, head % 2
    xx = x_hi * 2 + x_lo
    sub = x_hi * 4 + y
    links = Links(sems)

    def head_peer(o):
        return (head + o) % 8

    def in_head(o):
        return (dp, (head + o) % 8)

    def head_from(o):
        return (head + 8 - o) % 8

    def sub_peer(o):
        return (sub + o) % 8

    def in_sub(o):
        return (((sub + o) % 8) * 2 + core, head)

    def ring(axis, o):
        nx = (xx + o) % 4 if axis == "x" else xx
        ny = (y + o) % 4 if axis == "y" else y
        nz = (z + o) % 4 if axis == "z" else z
        return ((nx // 2) * 8 + ny * 2 + core, nz * 2 + nx % 2)

    sibling = (sub * 2 + (1 - core), head)

    barrier = pltpu.get_barrier_semaphore()
    greeted = [in_head(o) for o in range(1, 8)] + [in_sub(o) for o in range(1, 8)]
    greeted += [sibling, ((1 - x_hi) * 8 + y * 2 + core, z * 2 + 1 - x_lo)]
    for device in greeted:
        pl.semaphore_signal(
            barrier, inc=1, device_id=device, device_id_type=pl.DeviceIdType.MESH
        )

    own = pl.ds(aligned(head * ROWS, ROWS), ROWS)
    own_core = pl.ds(aligned(core * ROWS, ROWS), ROWS)
    sib_core = pl.ds(aligned((1 - core) * ROWS, ROWS), ROWS)
    half = pl.ds(aligned(core * 256, 256), 256)
    sib_half = pl.ds(aligned((1 - core) * 256, 256), 256)
    own_heads = pl.ds(aligned(head * 64, 64), 64)
    own_w = pl.ds(aligned(head * 192, 64), 192)
    sub_rows = pl.ds(aligned(sub * 128, 128), 128)

    for load in loads[0:5]:
        load.wait()
    x_all[own, :] = x_ref[...]
    w_all[own_w, :] = qkv_ref[...].astype(BF16)
    out_all[own_heads, :] = out_ref[...].astype(BF16)
    up_all[:, own] = up_ref[:, own_core].astype(BF16)
    down_all[own, :] = down_ref[own_core, :].astype(BF16)

    def out_at(s):
        return [out_all.at[pl.ds(aligned(s * 64 + a, 32), n), :] for a, n in ((0, 64), (0, 32), (32, 32))]

    def up_at(s):
        cols = pl.ds(aligned(s * 128, 128), 128)
        return [up_all.at[a : a + n, cols] for a, n in ((0, 512), (0, 256), (256, 256))]

    def down_at(s):
        return [down_all.at[pl.ds(aligned(s * 128 + a, 64), n), :] for a, n in ((0, 128), (0, 64), (64, 64))]

    def w_at(s):
        return [w_all.at[pl.ds(aligned(s * 192 + a, 96), n), :] for a, n in ((0, 192), (0, 96), (96, 96))]

    class Spread:
        def __init__(self, at, three, four):
            self.at, self.one = at, at(head)[0]
            self.ring_z = Group(links, three, 3, self.one)
            self.over_x = Group(links, four)

        def begin(self):
            for o in range(1, 4):
                self.ring_z.send(self.one, self.one, ring("z", o), o - 1)
            self.forward(head)

        def forward(self, s):
            _, first, second = self.at(s)
            self.over_x.send(first, first, ring("x", 1))
            self.over_x.send(second, second, ring("x", 3))

        def pass_on(self):
            for o in range(1, 4):
                self.ring_z.wait(o - 1)
                self.forward(((z + 4 - o) % 4) * 2 + x_lo)

    x_group = Group(links, x_all.at[0 : 7 * ROWS, :], 7, x_ref)
    spread_out = Spread(out_at, out_all.at[0:192, :], out_all.at[0:256, :])
    spread_up = Spread(up_at, up_all.at[:, 0:384], up_all.at[:, 0:512])
    spread_down = Spread(down_at, down_all.at[0:384, :], down_all.at[0:512, :])
    spread_w = Spread(w_at, w_all.at[0:576, :], w_all.at[0:768, :])

    pl.semaphore_wait(barrier, len(greeted))
    for o in range(1, 8):
        x_group.send(x_ref, x_all.at[own, :], in_head(o), o - 1)
    for keep in keeps:
        keep.start()
    spread_out.begin()
    spread_up.begin()
    spread_down.begin()

    for load in loads[5:9]:
        load.wait()
    for i in range(2):
        gate_low[i] = gate_ref[D * i : D * i + D, :].astype(BF16)
    gain_one, shift_one = gains_ref[0:1, :], biases_ref[0:1, :]
    gain_two, shift_two = gains_ref[1:2, :], biases_ref[1:2, :]

    def project(block):
        for s in range(4):
            rows = pl.ds(aligned(block * ROWS + 32 * s, 32), 32)
            v = x_all[rows, :].astype(F32)
            center = v - jnp.mean(v, axis=-1, keepdims=True)
            spread = jnp.mean(center * center, axis=-1, keepdims=True)
            h = center * lax.rsqrt(spread + NORM_EPS) * gain_one + shift_one
            h1_all[rows, :] = h.astype(BF16)
        rows = pl.ds(aligned(block * ROWS, ROWS), ROWS)
        pt = dot(w_all[own_w, :], h1_all[rows, :], NT)
        proj_t[0:64, rows] = (pt[0:64].astype(BF16).astype(F32) * 0.125).astype(BF16)
        proj_t[64:192, rows] = pt[64:192].astype(BF16)
        k_nat[rows, :] = pt[64:128].T.astype(BF16)
        v_nat[rows, :] = pt[128:192].T.astype(BF16)

    project(head)
    for o in range(1, 8):
        x_group.wait(o - 1)
        project(head_from(o))
    h1_pair[own_core, :] = h1_all[own, :]
    h1_group = Group(links, h1_pair.at[0:ROWS, :])
    h1_group.send(h1_pair.at[own_core, :], h1_pair.at[own_core, :], sibling)
    spread_out.pass_on()

    for j in range(LEN // QB):
        cols = slice(QB * j, QB * (j + 1))
        queries = proj_t[0:64, cols]
        ceiling = jnp.full((1, QB), -1e30, F32)
        tiles = QB * (j + 1) // ROWS
        for t in range(tiles):
            s = dot(k_nat[ROWS * t : ROWS * (t + 1), :], queries)
            if ROWS * t >= QB * j:
                keys_at = lax.broadcasted_iota(jnp.int32, (ROWS, QB), 0) + ROWS * t
                queries_at = lax.broadcasted_iota(jnp.int32, (ROWS, QB), 1) + QB * j
                s = jnp.where(keys_at <= queries_at, s, -1e30)
            s_buf[ROWS * t : ROWS * (t + 1), :] = s
            ceiling = jnp.maximum(ceiling, jnp.max(s, axis=0, keepdims=True))
        mass = jnp.zeros((1, QB), F32)
        for t in range(tiles):
            e = jnp.exp(s_buf[ROWS * t : ROWS * (t + 1), :] - ceiling)
            mass = mass + jnp.sum(e, axis=0, keepdims=True)
            p_buf[ROWS * t : ROWS * (t + 1), :] = e.astype(BF16)
        total = dot(proj_t[128:192, 0 : QB * (j + 1)], p_buf[0 : QB * (j + 1), :])
        total = total / mass
        o_t[:, cols] = total
        o_low[:, cols] = total.astype(BF16)
        lse[:, cols] = ceiling + jnp.log(mass)
    heads_group = Group(links, heads_t.at[0:448, 0:ROWS])
    for o in range(1, 8):
        block = o_low.at[:, pl.ds(aligned(head_peer(o) * ROWS, ROWS), ROWS)]
        heads_group.send(block, heads_t.at[own_heads, own_core], in_head(o))
    heads_t[own_heads, own_core] = o_low[:, own]

    g1_buf[...] = dot(h1_all[own, :], gate_low[0]) + biases_ref[2:3, :]
    spread_up.pass_on()
    heads_group.wait()
    headst_group = Group(links, heads_t.at[:, 0:ROWS])
    headst_group.send(heads_t.at[:, own_core], heads_t.at[:, own_core], sibling)
    spread_out.over_x.wait()
    attn_buf[...] = dot(heads_t[:, own_core], out_all[...], TN)
    for s in range(4):
        rows = slice(32 * s, 32 * s + 32)
        g1 = jax.nn.sigmoid(g1_buf[rows, :])
        g1_buf[rows, :] = g1
        x = x_ref[rows, :].astype(F32)
        x1 = g1 * attn_buf[rows, :] + (1.0 - g1) * x
        x1_buf[rows, :] = x1
        center = x1 - jnp.mean(x1, axis=-1, keepdims=True)
        spread = jnp.mean(center * center, axis=-1, keepdims=True)
        rstd = lax.rsqrt(spread + NORM_EPS)
        xhat = center * rstd
        xhat_buf[rows, :] = xhat
        rstd_buf[rows, :] = jnp.broadcast_to(rstd, (32, 128))
        h2 = xhat * gain_two + shift_two
        h2_pair[pl.ds(aligned(core * ROWS + 32 * s, 32), 32), :] = h2.astype(BF16)
    h2_group = Group(links, h2_pair.at[0:ROWS, :])
    h2_group.send(h2_pair.at[own_core, :], h2_pair.at[own_core, :], sibling)
    spread_down.pass_on()
    spread_w.begin()
    g2_buf[...] = dot(h2_pair[own_core, :], gate_low[1]) + biases_ref[3:4, :]
    spread_up.over_x.wait()
    h2_group.wait()
    for n in range(4):
        cols = slice(256 * n, 256 * n + 256)
        u = dot(h2_pair[...], up_all[:, cols])
        c0 = 0.7978845608028654
        inner = jnp.tanh(c0 * (u + 0.044715 * u * u * u))
        act_buf[:, cols] = (0.5 * u * (1.0 + inner)).astype(BF16)
        dgelu_buf[:, cols] = 0.5 * (1.0 + inner) + 0.5 * u * (1.0 - inner * inner) * c0 * (
            1.0 + 3.0 * 0.044715 * u * u
        )
    spread_down.over_x.wait()
    ffn_send[...] = dot(act_buf[sib_core, :], down_all[...]).astype(BF16)
    ffn_group = Group(links, ffn_recv)
    ffn_group.send(ffn_send, ffn_recv, sibling)
    ffn_own[...] = dot(act_buf[own_core, :], down_all[...])
    ffn_group.wait()
    bias_two = jnp.zeros((1, D), F32)
    for s in range(4):
        rows = slice(32 * s, 32 * s + 32)
        ffn = ffn_own[rows, :] + ffn_recv[rows, :].astype(F32)
        g2 = jax.nn.sigmoid(g2_buf[rows, :])
        g2_buf[rows, :] = g2
        x1 = x1_buf[rows, :]
        dy = dy_ref[rows, :].astype(F32)
        mixed_ref[rows, :] = g2 * ffn + (1.0 - g2) * x1
        dffn_pair[pl.ds(aligned(core * ROWS + 32 * s, 32), 32), :] = (g2 * dy).astype(BF16)
        dz = (dy * (ffn - x1) * g2 * (1.0 - g2)).astype(BF16)
        dz2_full[rows, :] = dz
        bias_two = bias_two + jnp.sum(dz.astype(F32), axis=0, keepdims=True)
    dffn_group = Group(links, dffn_pair.at[0:ROWS, :])
    dffn_group.send(dffn_pair.at[own_core, :], dffn_pair.at[own_core, :], sibling)
    dz2_group = Group(links, dz2_half.at[0:ROWS, :])
    dz2_group.send(dz2_full.at[:, sib_half], dz2_half.at[own_core, :], sibling)
    dz2_half[own_core, :] = dz2_full[:, half]
    dh2_gate[...] = dot(dz2_full[...], gate_low[1], NT)
    dffn_group.wait()

    def stage(axis, at, src, dst, size):
        group = Group(links, dst)
        for o in range(1, 4):
            t = (at + o) % 4
            group.send(
                src.at[pl.ds(t * size, size)],
                dst.at[pl.ds((o - 1) * size, size)],
                ring(axis, o),
            )
        return group

    def add_up(group, at, src, got, size, store):
        group.wait()

        def add(i, carry):
            total = src[at * size + i].astype(F32)
            for o in range(3):
                total = total + got[o * size + i].astype(F32)
            store(i, total)
            return carry

        lax.fori_loop(0, size, add, 0)

    def to_bf16(ref):
        def store(i, total):
            ref[i] = total.astype(BF16)

        return store

    for h in range(8):
        gd = dot(act_buf[:, 128 * h : 128 * h + 128], dffn_pair[...], TN).astype(BF16)
        for g in range(8):
            ch_x, ch_y, ch_z = (g // 4) * 2 + h % 2, g % 4, h // 2
            sd1[ch_y * 16 + ch_x * 4 + ch_z] = gd[16 * g : 16 * g + 16, :]
    down_group = stage("y", y, sd1, rd1, 16)
    for n in range(4):
        cols = slice(256 * n, 256 * n + 256)
        da = dot(dffn_pair[...], down_all[cols, :], NT)
        dhid_buf[:, cols] = (da * dgelu_buf[:, cols]).astype(BF16)
    dh2_send[...] = dot(dhid_buf[sib_core, :], up_all[...], NT).astype(BF16)
    dh2_group = Group(links, dh2_recv)
    dh2_group.send(dh2_send, dh2_recv, sibling)
    for h in range(8):
        gu = dot(h2_pair[...], dhid_buf[:, 128 * h : 128 * h + 128], TN).astype(BF16)
        for g in range(8):
            ch_x, ch_y, ch_z = (g // 4) * 2 + h % 2, g % 4, h // 2
            su1[ch_z * 16 + ch_y * 4 + ch_x] = gu[64 * g : 64 * g + 64, :]
    up_group = stage("z", z, su1, ru1, 16)
    dh2_own[...] = dot(dhid_buf[own_core, :], up_all[...], NT)
    dh2_group.wait()
    gain_sum = jnp.zeros((1, D), F32)
    shift_sum = jnp.zeros((1, D), F32)
    bias_one = jnp.zeros((1, D), F32)
    for s in range(4):
        rows = slice(32 * s, 32 * s + 32)
        dh2 = dh2_own[rows, :] + dh2_recv[rows, :].astype(F32) + dh2_gate[rows, :]
        xhat = xhat_buf[rows, :]
        gain_sum = gain_sum + jnp.sum(dh2 * xhat, axis=0, keepdims=True)
        shift_sum = shift_sum + jnp.sum(dh2, axis=0, keepdims=True)
        dxhat = dh2 * gain_two
        mean_a = jnp.mean(dxhat, axis=-1, keepdims=True)
        mean_b = jnp.mean(dxhat * xhat, axis=-1, keepdims=True)
        rstd = rstd_buf[rows, 0:1]
        dx1 = (1.0 - g2_buf[rows, :]) * dy_ref[rows, :].astype(F32) + rstd * (
            dxhat - mean_a - xhat * mean_b
        )
        g1 = g1_buf[rows, :]
        dattn_full[rows, :] = (g1 * dx1).astype(BF16)
        x = x_ref[rows, :].astype(F32)
        dz = (dx1 * (attn_buf[rows, :] - x) * g1 * (1.0 - g1)).astype(BF16)
        dz1_full[rows, :] = dz
        bias_one = bias_one + jnp.sum(dz.astype(F32), axis=0, keepdims=True)
        ingrad_ref[rows, :] = (1.0 - g1) * dx1
    vec[1:2, :] = gain_sum
    vec[3:4, :] = shift_sum
    vec[4:5, :] = bias_one
    vec[5:6, :] = bias_two
    vec[6:8, :] = jnp.zeros((2, D), F32)

    late_group = Group(links, late_half.at[0])
    late_group.send(dz1_full.at[:, sib_half], late_half.at[0, own_core, :], sibling)
    late_group.send(dattn_full.at[:, sib_half], late_half.at[1, own_core, :], sibling)
    dheads_t[...] = dot(out_all[...], dattn_full[...], NT).astype(BF16)
    dheads_group = Group(links, do_t.at[:, 0 : 7 * ROWS])
    for o in range(1, 8):
        block = dheads_t.at[pl.ds(aligned(head_peer(o) * 64, 64), 64), :]
        dheads_group.send(block, do_t.at[:, own], in_head(o))
    do_t[:, own] = dheads_t[own_heads, :]
    late_half[0, own_core, :] = dz1_full[:, half]
    late_half[1, own_core, :] = dattn_full[:, half]

    h1_group.wait()
    dz2_group.wait()
    headst_group.wait()
    late_group.wait()
    gates_low[0:512, :] = dot(h1_pair[...], late_half[0], TN).astype(BF16)
    gates_low[512:1024, :] = dot(h2_pair[...], dz2_half[...], TN).astype(BF16)
    gates_group = Group(links, gates_recv.at[0, 0:7])
    for o in range(1, 8):
        block = gates_low.at[pl.ds(aligned(sub_peer(o) * 128, 128), 128), :]
        gates_group.send(block, gates_recv.at[0, sub], in_sub(o))
    gates_recv[0, sub] = gates_low[sub_rows, :]
    gout_low[...] = dot(heads_t[...], late_half[1]).astype(BF16)
    gout_group = Group(links, gout_recv.at[0, 0:7])
    for o in range(1, 8):
        block = gout_low.at[pl.ds(aligned(head_peer(o) * 64, 64), 64), :]
        gout_group.send(block, gout_recv.at[0, head], in_head(o))
    gout_recv[0, head] = gout_low[own_heads, :]
    spread_w.pass_on()

    def add_eight(ref):
        total = ref[0].astype(F32)
        for o in range(1, 8):
            total = total + ref[o].astype(F32)
        return total

    dheads_group.wait()
    dk_t[...] = jnp.zeros_like(dk_t)
    dv_t[...] = jnp.zeros_like(dv_t)
    for j in range(LEN // QB):
        cols = slice(QB * j, QB * (j + 1))
        upto = QB * (j + 1)
        queries = proj_t[0:64, cols]
        grads = do_t[:, cols]
        delta = jnp.sum(o_t[:, cols] * grads.astype(F32), axis=0, keepdims=True)
        row_lse = lse[:, cols]
        for t in range(upto // ROWS):
            keys = slice(ROWS * t, ROWS * (t + 1))
            p = jnp.exp(dot(k_nat[keys, :], queries) - row_lse)
            if ROWS * t >= QB * j:
                keys_at = lax.broadcasted_iota(jnp.int32, (ROWS, QB), 0) + ROWS * t
                queries_at = lax.broadcasted_iota(jnp.int32, (ROWS, QB), 1) + QB * j
                p = jnp.where(keys_at <= queries_at, p, 0.0)
            d = dot(v_nat[keys, :], grads)
            p_buf[keys, :] = p.astype(BF16)
            ds_buf[keys, :] = (p * (d - delta)).astype(BF16)
        dq_t[:, cols] = dot(proj_t[64:128, 0:upto], ds_buf[0:upto, :]) * 0.125
        dk_t[:, 0:upto] += dot(queries, ds_buf[0:upto, :], NT)
        dv_t[:, 0:upto] += dot(grads, p_buf[0:upto, :], NT)
    dproj_low[0:64, :] = dq_t[...].astype(BF16)
    dproj_low[64:128, :] = dk_t[...].astype(BF16)
    dproj_low[128:192, :] = dv_t[...].astype(BF16)
    dproj_group = Group(links, dproj_all.at[0 : 7 * 192, :])
    for o in range(1, 8):
        block = dproj_low.at[:, pl.ds(aligned(head_peer(o) * ROWS, ROWS), ROWS)]
        dproj_group.send(block, dproj_all.at[own_w, :], in_head(o))
    dproj_all[own_w, :] = dproj_low[:, own]

    gq_low[...] = dot(dproj_low[...], h1_all[...]).astype(BF16)
    gq_pair = Group(links, gq_sib)
    gq_pair.send(gq_low.at[:, sib_half], gq_sib, sibling)

    gout_group.wait()
    gout_sum[...] = add_eight(gout_recv.at[0]).astype(BF16)
    gout_group = Group(links, gout_recv.at[1, 0:7])
    for o in range(1, 8):
        gout_group.send(gout_sum, gout_recv.at[1, sub], in_sub(o))
    gout_recv[1, sub] = gout_sum[...]
    gates_group.wait()
    gates_sum[...] = add_eight(gates_recv.at[0]).astype(BF16)
    gates_group = Group(links, gates_recv.at[1, 0:7])
    for o in range(1, 8):
        gates_group.send(gates_sum, gates_recv.at[1, head], in_head(o))
    gates_recv[1, head] = gates_sum[...]

    gq_pair.wait()
    total = gq_low[:, half].astype(F32) + gq_sib[...].astype(F32)
    for i in range(8):
        r, c = 48 * (i // 2), 128 * (i % 2)
        gq_send[i] = total[r : r + 48, c : c + 128].astype(BF16)
    gq_group = Group(links, gq_recv.at[0:7])
    for o in range(1, 8):
        gq_group.send(gq_send.at[sub_peer(o)], gq_recv.at[sub], in_sub(o))
    gq_recv[sub] = gq_send[sub]

    add_up(down_group, y, sd1, rd1, 16, to_bf16(sd2))
    down_group = stage("x", xx, sd2, rd2, 4)
    add_up(up_group, z, su1, ru1, 16, to_bf16(su2))
    up_group = stage("y", y, su2, ru2, 4)

    spread_w.over_x.wait()
    dproj_group.wait()
    dh2_own[...] = dot(dproj_all[...], w_all[...], TN) + dot(dz1_full[...], gate_low[0], NT)
    gain_sum = jnp.zeros((1, D), F32)
    shift_sum = jnp.zeros((1, D), F32)
    for s in range(4):
        rows = slice(32 * s, 32 * s + 32)
        v = x_ref[rows, :].astype(F32)
        center = v - jnp.mean(v, axis=-1, keepdims=True)
        spread = jnp.mean(center * center, axis=-1, keepdims=True)
        rstd = lax.rsqrt(spread + NORM_EPS)
        xhat = center * rstd
        dh = dh2_own[rows, :]
        gain_sum = gain_sum + jnp.sum(dh * xhat, axis=0, keepdims=True)
        shift_sum = shift_sum + jnp.sum(dh, axis=0, keepdims=True)
        dxhat = dh * gain_one
        mean_a = jnp.mean(dxhat, axis=-1, keepdims=True)
        mean_b = jnp.mean(dxhat * xhat, axis=-1, keepdims=True)
        ingrad_ref[rows, :] += rstd * (dxhat - mean_a - xhat * mean_b)
    vec[0:1, :] = gain_sum
    vec[2:3, :] = shift_sum
    vec_group = Group(links, vec_s)
    vec_group.send(vec, vec_s, sibling)

    gq_group.wait()
    gq_rows = pl.ds(aligned((sub // 2) * 48, 48), 48)
    gq_cols = pl.ds(aligned(core * 256 + (sub % 2) * 128, 128), 128)
    gq_all[gq_rows, gq_cols] = add_eight(gq_recv).astype(BF16)
    gq_group = Group(links, gq_recv.at[0:7])
    for o in range(1, 8):
        block = gq_all.at[gq_rows, gq_cols]
        gq_group.send(block, block, in_sub(o))

    vec_group.wait()
    vec_a[sub] = vec[...] + vec_s[...]
    vec_group = Group(links, vec_a.at[0:7])
    for o in range(1, 8):
        vec_group.send(vec_a.at[sub], vec_a.at[sub], in_sub(o))

    gout_group.wait()
    gout_all[:, half] = add_eight(gout_recv.at[1]).astype(BF16)
    gout_pair = Group(links, gout_sum)
    gout_pair.send(gout_all.at[:, half], gout_all.at[:, half], sibling)
    gates_group.wait()
    ggate_all[sub_rows, half] = add_eight(gates_recv.at[1]).astype(BF16)
    gates_group = Group(links, gates_recv.at[0, 0:7])
    for o in range(1, 8):
        block = ggate_all.at[sub_rows, half]
        gates_group.send(block, block, in_sub(o))

    add_up(down_group, xx, sd2, rd2, 4, to_bf16(sd3))
    down_group = stage("z", z, sd3, rd3, 1)
    add_up(up_group, y, su2, ru2, 4, to_bf16(su3))
    up_group = stage("x", xx, su3, ru3, 1)

    vec_group.wait()
    vec_b[head] = add_eight(vec_a)
    vec_group = Group(links, vec_b.at[0:7])
    for o in range(1, 8):
        vec_group.send(vec_b.at[head], vec_b.at[head], in_head(o))
    gq_group.wait()
    gq_pair = Group(links, gq_sib)
    gq_pair.send(gq_all.at[:, half], gq_all.at[:, half], sibling)

    up_rows = pl.ds(aligned(sub * 64, 64), 64)
    down_rows = pl.ds(aligned(core * 128 + sub * 16, 16), 16)

    def store_up(i, total):
        gup_all[up_rows, own_core] = total.astype(BF16)

    def store_down(i, total):
        gdown_all[down_rows, :] = total.astype(BF16)

    add_up(down_group, z, sd3, rd3, 1, store_down)
    down_group = Group(links, gdown_all.at[0:112, :])
    for o in range(1, 8):
        block = gdown_all.at[down_rows, :]
        down_group.send(block, block, in_sub(o))
    add_up(up_group, xx, su3, ru3, 1, store_up)
    up_group = Group(links, gup_all.at[0:448, 0:128])
    for o in range(1, 8):
        block = gup_all.at[up_rows, own_core]
        up_group.send(block, block, in_sub(o))

    gates_group.wait()
    gates_pair = Group(links, gates_low)
    gates_pair.send(ggate_all.at[:, half], ggate_all.at[:, half], sibling)
    down_group.wait()
    down_pair = Group(links, gdown_all.at[0:128, :])
    down_pair.send(gdown_all.at[own_core, :], gdown_all.at[own_core, :], sibling)
    up_group.wait()
    up_pair = Group(links, gup_all.at[:, 0:128])
    up_pair.send(gup_all.at[:, own_core], gup_all.at[:, own_core], sibling)
    vec_group.wait()
    o_vec_ref[...] = add_eight(vec_b)

    stores = []
    for i, (group, src, dst) in enumerate(
        (
            (gq_pair, gq_all, o_qkv_ref),
            (gout_pair, gout_all, o_out_ref),
            (gates_pair, ggate_all, o_gate_ref),
            (down_pair, gdown_all, o_down_ref),
            (up_pair, gup_all, o_up_ref),
        )
    ):
        group.wait()
        stores.append(pltpu.make_async_copy(src, dst, local_sems.at[9 + i]))
        stores[-1].start()
    links.drain()
    for store in stores + keeps:
        store.wait()


VMEM = pl.BlockSpec(memory_space=pltpu.VMEM)
ANY = pl.BlockSpec(memory_space=pl.ANY)
HBM = pl.BlockSpec(memory_space=pltpu.HBM)


def run_layer(*args):
    shapes = [
        ((ROWS, D), F32),
        ((ROWS, D), F32),
        ((192, D), BF16),
        ((64, D), BF16),
        ((D, 256), BF16),
        ((256, D), BF16),
        ((LEN, D), BF16),
        ((8, D), F32),
    ]
    scratch = [
        ((ROWS, D), BF16),
        ((ROWS, D), BF16),
        ((2, D), F32),
        ((4, D), F32),
        ((192, D), F32),
        ((64, D), F32),
        ((D, 256), F32),
        ((256, D), F32),
        ((2 * D, D), F32),
        ((LEN, D), BF16),
        ((LEN, D), BF16),
        ((1536, D), BF16),
        ((D, D), BF16),
        ((D, 1024), BF16),
        ((1024, D), BF16),
        ((2, D, D), BF16),
        ((192, LEN), BF16),
        ((LEN, 64), BF16),
        ((LEN, 64), BF16),
        ((LEN, QB), F32),
        ((LEN, QB), BF16),
        ((LEN, QB), BF16),
        ((64, LEN), F32),
        ((64, LEN), BF16),
        ((1, LEN), F32),
        ((D, 256), BF16),
        ((ROWS, D), F32),
        ((ROWS, D), F32),
        ((ROWS, D), F32),
        ((ROWS, D), F32),
        ((ROWS, 128), F32),
        ((256, D), BF16),
        ((256, D), BF16),
        ((ROWS, D), F32),
        ((256, 1024), BF16),
        ((256, 1024), F32),
        ((ROWS, D), F32),
        ((ROWS, D), BF16),
        ((ROWS, D), BF16),
        ((256, D), BF16),
        ((ROWS, D), BF16),
        ((ROWS, D), BF16),
        ((ROWS, D), BF16),
        ((256, 256), BF16),
        ((2, 256, 256), BF16),
        ((256, 1024), BF16),
        ((ROWS, D), F32),
        ((ROWS, D), BF16),
        ((ROWS, D), BF16),
        ((ROWS, D), F32),
        ((D, ROWS), BF16),
        ((64, LEN), BF16),
        ((8, D), F32),
        ((8, D), F32),
        ((8, 8, D), F32),
        ((8, 8, D), F32),
        ((64, LEN), F32),
        ((64, LEN), F32),
        ((64, LEN), F32),
        ((192, LEN), BF16),
        ((1536, ROWS), BF16),
        ((192, D), BF16),
        ((192, 256), BF16),
        ((8, 48, 128), BF16),
        ((8, 48, 128), BF16),
        ((192, D), BF16),
        ((LEN, 256), BF16),
        ((2, 8, 128, 256), BF16),
        ((128, 256), BF16),
        ((D, 256), BF16),
        ((2, 8, 64, 256), BF16),
        ((64, 256), BF16),
        ((64, D), BF16),
        ((D, 256), BF16),
        ((256, D), BF16),
        ((LEN, D), BF16),
    ]
    for rows, cols in ((64, 128), (16, 512)):
        for count in (64, 48, 16, 12, 4, 3):
            scratch.append(((count, rows, cols), BF16))
    return pl.pallas_call(
        layer_kernel,
        out_shape=[jax.ShapeDtypeStruct(s, t) for s, t in shapes]
        + [pltpu.VMEM(s, F32) for s in SHAPES[0:5] for _ in range(3)],
        in_specs=[HBM] * 19,
        out_specs=[VMEM] * 2 + [ANY] * 5 + [VMEM] + [VMEM] * 15,
        scratch_shapes=[pltpu.VMEM(s, t) for s, t in scratch]
        + [pltpu.SemaphoreType.DMA((N_SEMS,)), pltpu.SemaphoreType.DMA((N_LOCAL,))],
        compiler_params=pltpu.CompilerParams(
            collective_id=0, has_side_effects=True, vmem_limit_bytes=40 * 1024 * 1024
        ),
        name="layer",
    )(*args)


SHAPES = ((192, D), (64, D), (D, 256), (256, D), (LEN, D), (2, D), (4, D))
JOBS = [(0, 0, 192), (1, 0, 64), (2, 0, 512), (3, 0, 256)] + [(4, 256 * i, 256) for i in range(4)]


def adamw(weight, first, second, grad, rate):
    first = BETA_ONE * first + (1.0 - BETA_ONE) * grad
    second = BETA_TWO * second + (1.0 - BETA_TWO) * grad * grad
    first_hat = first * (1.0 / (1.0 - BETA_ONE**STEP))
    second_hat = second * (1.0 / (1.0 - BETA_TWO**STEP))
    weight = weight - rate * (first_hat / (jnp.sqrt(second_hat) + ADAM_EPS) + DECAY * weight)
    return (weight, first, second)


def adamw_kernel(*refs):
    states, grads, passed = refs[0:21], refs[21:27], refs[27:29]
    outs, passed_on = refs[29:50], refs[50:52]
    bufs, gbufs = refs[52:57], refs[57:62]
    grad_sems, out_sems, pass_sems = refs[62:65]

    passes = [
        pltpu.make_async_copy(a, b, pass_sems.at[i])
        for i, (a, b) in enumerate(zip(passed, passed_on))
    ]
    for j, (a, r, n) in enumerate(JOBS):
        rows = pl.ds(r, n)
        pltpu.make_async_copy(grads[a].at[rows, :], gbufs[a].at[rows, :], grad_sems.at[j]).start()
    for c in passes:
        c.start()
    for a, lo, hi in ((5, 0, 2), (6, 2, 6)):
        new = adamw(*(states[3 * a + k][...] for k in range(3)), grads[5][lo:hi, :], RATES[a])
        for k in range(3):
            outs[3 * a + k][...] = new[k]
    for j, (a, r, n) in enumerate(JOBS):
        rows = pl.ds(r, n)
        part = gbufs[a].at[rows, :]
        pltpu.make_async_copy(part, part, grad_sems.at[j]).wait()
        step = 16 if SHAPES[a][1] == D else 32

        def update(i, carry):
            at = pl.ds(aligned(r + i * step, step), step)
            new = adamw(*(states[3 * a + k][at, :] for k in range(3)), gbufs[a][at, :].astype(F32), RATES[a])
            for k in range(3):
                bufs[a][k, at, :] = new[k]
            return carry

        lax.fori_loop(0, n // step, update, 0)
        for k in range(3):
            pltpu.make_async_copy(
                bufs[a].at[k, rows, :], outs[3 * a + k].at[rows, :], out_sems.at[j]
            ).start()
    for j, (a, r, n) in enumerate(JOBS):
        whole = bufs[a].at[:, pl.ds(r, n), :]
        pltpu.make_async_copy(whole, whole, out_sems.at[j]).wait()
    for c in passes:
        c.wait()


def run_adamw(states, grads, passed):
    n = len(JOBS)
    state_specs = [VMEM] * 21
    new_specs = [ANY] * 15 + [VMEM] * 6
    return pl.pallas_call(
        adamw_kernel,
        out_shape=[jax.ShapeDtypeStruct(s.shape, F32) for s in (*states, *passed)],
        in_specs=state_specs + [ANY] * 5 + [VMEM] + [ANY] * 2,
        out_specs=new_specs + [ANY] * 2,
        scratch_shapes=[pltpu.VMEM((3, *s), F32) for s in SHAPES[0:5]]
        + [pltpu.VMEM(s, BF16) for s in SHAPES[0:5]]
        + [pltpu.SemaphoreType.DMA((k,)) for k in (n, n, 2)],
        compiler_params=pltpu.CompilerParams(vmem_limit_bytes=20 * 1024 * 1024),
        name="adamw",
    )(*states, *grads, *passed)


def local(inputs, cotangent, *state):
    rows = inputs.shape[1]
    flat = list(state)
    for i in (0, 1, 2):
        flat[i] = jnp.transpose(flat[i], (0, 2, 1)).reshape(192, D)
    for i in (12, 13, 14):
        flat[i] = flat[i].reshape(2 * D, D)
    operands = (inputs.reshape(rows, D), cotangent.reshape(rows, D), flat[15], flat[18])
    operands += tuple(flat[3 * i] for i in range(5))
    operands += tuple(flat[3 * i + k] for i in range(5) for k in (1, 2))
    results = run_layer(*(pltpu.with_memory_space_constraint(a, pltpu.HBM) for a in operands))
    mixed, ingrad, grads, kept = results[0], results[1], results[2:8], results[8:23]
    *new, mixed, ingrad = run_adamw([*kept, *flat[15:21]], grads, (mixed, ingrad))
    for i in (0, 1, 2):
        new[i] = jnp.transpose(new[i].reshape(3, 64, D), (0, 2, 1))
    for i in (12, 13, 14):
        new[i] = new[i].reshape(2, D, D)
    return (mixed.reshape(1, rows, D), ingrad.reshape(1, rows, D), *new)


def solution(mesh):
    batch = P("dp", "head", None)
    qkv = P(None, None, "head")
    first = P("head", None)
    second = P(None, "head")
    state = (qkv,) * 3 + (first,) * 3 + (second,) * 3 + (first,) * 3 + (P(),) * 9
    return jax.shard_map(
        local,
        mesh=mesh,
        in_specs=(batch, batch, *state),
        out_specs=(batch, batch, *state),
        check_vma=False,
    )
```

time: 165 us -> 113 us (0.68)
  Pallas kernels: 152 us -> 112 us
  local copies, waits for them, and re-layouts: 12.3 us -> 0.03 us
    pallas_call x1, Pallas kernels: 139 us -> 105 us  [run_layer(): pl.pallas_call(layer_kernel, out_shape=[jax.ShapeDtypeStruct(s, t) for s,...]
    unnamed x16 -> x12, local copies, waits for them, and re-layouts: 12.3 us -> 0.03 us
    pallas_call x1, Pallas kernels: 12.9 us -> 6.93 us  [run_adamw(): pl.pallas_call(adamw_kernel, out_shape=[jax.ShapeDtypeStruct(s.shape, F32...]
where the time goes in v2:
time: 113 us
  Pallas kernels  112 us (99%)
    pallas_call x1, Pallas kernels, run_layer(): pl.pallas_call(layer_kernel, out_shape=[jax.ShapeDtypeStruct(s, t) for s,...  105 us
    pallas_call x1, Pallas kernels, run_adamw(): pl.pallas_call(adamw_kernel, out_shape=[jax.ShapeDtypeStruct(s.shape, F32...  6.93 us

profile of v2, /device:TPU:1, one launch (start us, length us, event | category | flops | bytes accessed | tf_op | source)
XLA Modules:
  0.0 112.7 jit_solution(12817204581105581840)
XLA Ops:
  0.7 0.0 copy-start
  0.7 0.0 copy-start.1
  0.7 0.0 copy-start.2
  0.7 0.0 copy-start.3
  0.7 0.0 copy-start.4
  0.7 0.0 copy-start.5
  0.7 105.0 %layer.1 = (f32[128,512]{1,0:T(8,128)S(1)}, f32[128,512]{1,0:T(8,128)S(1)}, bf16[192,512]{1,0:T(8,128)(2,1)S(1)}, bf16[64,512]{1,0:T(8,128)(2,1)S(1)}, bf16[512,...) custom-call(bf16[128,512]{1,0:T(8,128)(2,1)} %bitcast.34, ...), custom_call_target="tpu_custom_call" | custom-call | tf_op jit(solution)/shard_map/layer/pallas_call | solution.py:843
  105.7 0.0 copy-done
  105.7 0.0 copy-done.1
  105.7 0.0 copy-done.2
  105.7 0.0 copy-done.3
  105.7 0.0 copy-done.4
  105.8 0.0 copy-done.5
  105.8 6.9 %adamw.1 = (f32[192,512]{1,0:T(8,128)}, f32[192,512]{1,0:T(8,128)}, f32[192,512]{1,0:T(8,128)}, f32[64,512]{1,0:T(8,128)}, f32[64,512]{1,0:T(8,128)}, /*index=5*...) custom-call(f32[192,512]{1,0:T(8,128)S(1)} %get-tuple-element.69.ref, ...), custom_call_target="tpu_custom_call" | custom-call | tf_op jit(solution)/shard_map/adamw/pallas_call | solution.py:919
Async XLA Ops:
  0.7 105.0 %copy-start = (f32[4,512]{1,0:T(4,128)S(1)}, f32[4,512]{1,0:T(4,128)}, u32[]{:S(2)}) copy-start(f32[4,512]{1,0:T(4,128)} %refs_18_.1) | copy-start | bytes 24580
  0.7 105.0 %copy-start.1 = (f32[2,512]{1,0:T(2,128)S(1)}, f32[2,512]{1,0:T(2,128)}, u32[]{:S(2)}) copy-start(f32[2,512]{1,0:T(2,128)} %refs_15_.1) | copy-start | bytes 12292
  0.7 105.0 %copy-start.2 = (f32[4,512]{1,0:T(4,128)S(1)}, f32[4,512]{1,0:T(4,128)}, u32[]{:S(2)}) copy-start(f32[4,512]{1,0:T(4,128)} %refs_19_.1) | copy-start | bytes 24580
  0.7 105.0 %copy-start.3 = (f32[4,512]{1,0:T(4,128)S(1)}, f32[4,512]{1,0:T(4,128)}, u32[]{:S(2)}) copy-start(f32[4,512]{1,0:T(4,128)} %refs_20_.1) | copy-start | bytes 24580
  0.7 105.0 %copy-start.4 = (f32[2,512]{1,0:T(2,128)S(1)}, f32[2,512]{1,0:T(2,128)}, u32[]{:S(2)}) copy-start(f32[2,512]{1,0:T(2,128)} %refs_16_.1) | copy-start | bytes 12292
  0.7 105.0 %copy-start.5 = (f32[2,512]{1,0:T(2,128)S(1)}, f32[2,512]{1,0:T(2,128)}, u32[]{:S(2)}) copy-start(f32[2,512]{1,0:T(2,128)} %refs_17_.1) | copy-start | bytes 12292

commit v3 on v2

v3 whole, which is shorter than its diff:
```python
import jax
import jax.numpy as jnp
from jax import lax
from jax.experimental import pallas as pl
from jax.experimental.pallas import tpu as pltpu
from jax.sharding import PartitionSpec as P

F32 = jnp.float32
BF16 = jnp.bfloat16
STEP = 10
NORM_EPS = 1e-05
BETA_ONE = 0.9
BETA_TWO = 0.999
ADAM_EPS = 1e-08
DECAY = 0.01
RATES = (0.04, 0.1, 0.04, 0.02, 0.04, 0.4, 0.3)
D = 512
ROWS = 128
LEN = 1024
QB = 256
NN = ((1,), (0,))
NT = ((1,), (1,))
TN = ((0,), (0,))


def dot(a, b, dims=NN):
    return lax.dot_general(a, b, (dims, ((), ())), preferred_element_type=F32)


def aligned(value, by):
    return pl.multiple_of(value, by)


class Group:
    def __init__(self, links, total, receives=1, each=None):
        self.send_sem, self.total = links.semaphore(), total
        self.each = total if each is None else each
        self.recv_sems = [links.semaphore() for _ in range(receives)]
        links.groups.append(self)

    def send(self, src, dst, device, k=0):
        pltpu.make_async_remote_copy(
            src_ref=src,
            dst_ref=dst,
            send_sem=self.send_sem,
            recv_sem=self.recv_sems[k],
            device_id=device,
            device_id_type=pl.DeviceIdType.MESH,
        ).start()

    def wait(self, k=0):
        pltpu.make_async_copy(self.each, self.each, self.recv_sems[k]).wait()


class Links:
    def __init__(self, sems):
        self.sems, self.used, self.groups = sems, 0, []

    def semaphore(self):
        self.used += 1
        return self.sems.at[self.used - 1]

    def drain(self):
        for g in self.groups:
            pltpu.make_async_copy(g.total, g.total, g.send_sem).wait()


N_SEMS = 140
N_LOCAL = 19


SHAPES = ((192, D), (64, D), (D, 256), (256, D), (2 * D, D), (2, D), (4, D))


def adamw(weight, first, second, grad, rate):
    first = BETA_ONE * first + (1.0 - BETA_ONE) * grad
    second = BETA_TWO * second + (1.0 - BETA_TWO) * grad * grad
    first_hat = first * (1.0 / (1.0 - BETA_ONE**STEP))
    second_hat = second * (1.0 / (1.0 - BETA_TWO**STEP))
    weight = weight - rate * (first_hat / (jnp.sqrt(second_hat) + ADAM_EPS) + DECAY * weight)
    return (weight, first, second)


SCRATCH = {
    "x_ref": ((ROWS, D), BF16),
    "dy_ref": ((ROWS, D), BF16),
    "gains_ref": ((2, D), F32),
    "biases_ref": ((4, D), F32),
    "x_all": ((LEN, D), BF16),
    "h1_all": ((LEN, D), BF16),
    "w_all": ((1536, D), BF16),
    "out_all": ((D, D), BF16),
    "up_all": ((D, 1024), BF16),
    "down_all": ((1024, D), BF16),
    "gate_low": ((2, D, D), BF16),
    "proj_t": ((192, LEN), BF16),
    "k_nat": ((LEN, 64), BF16),
    "v_nat": ((LEN, 64), BF16),
    "s_buf": ((LEN, QB), F32),
    "p_buf": ((LEN, QB), BF16),
    "ds_buf": ((LEN, QB), BF16),
    "o_t": ((64, LEN), F32),
    "o_low": ((64, LEN), BF16),
    "lse": ((1, LEN), F32),
    "heads_t": ((D, 256), BF16),
    "g1_buf": ((ROWS, D), F32),
    "attn_buf": ((ROWS, D), F32),
    "x1_buf": ((ROWS, D), F32),
    "xhat_buf": ((ROWS, D), F32),
    "rstd_buf": ((ROWS, 128), F32),
    "h2_pair": ((256, D), BF16),
    "g2_buf": ((ROWS, D), F32),
    "act_buf": ((256, 1024), BF16),
    "dgelu_buf": ((256, 1024), F32),
    "ffn_own": ((ROWS, D), F32),
    "ffn_send": ((ROWS, D), BF16),
    "ffn_recv": ((ROWS, D), BF16),
    "dffn_pair": ((256, D), BF16),
    "dz2_full": ((ROWS, D), BF16),
    "dz1_full": ((ROWS, D), BF16),
    "dattn_full": ((ROWS, D), BF16),
    "dz2_half": ((256, 256), BF16),
    "dattn_half": ((256, 256), BF16),
    "dhid_buf": ((256, 1024), BF16),
    "dh2_own": ((ROWS, D), F32),
    "dh2_send": ((ROWS, D), BF16),
    "dh2_recv": ((ROWS, D), BF16),
    "dh2_gate": ((ROWS, D), F32),
    "back_send": ((8, 128, ROWS), BF16),
    "back_t": ((128, LEN), BF16),
    "vec": ((8, D), F32),
    "vec_s": ((8, D), F32),
    "vec_a": ((8, 8, D), F32),
    "vec_b": ((8, 8, D), F32),
    "dq_t": ((64, LEN), F32),
    "dk_t": ((64, LEN), F32),
    "dv_t": ((64, LEN), F32),
    "dproj_low": ((256, LEN), BF16),
    "dproj_all": ((1536, ROWS), BF16),
    "gq_low": ((256, D), BF16),
    "gq_sib": ((256, 256), BF16),
    "gq_send": ((8, 64, 128), BF16),
    "gq_recv": ((8, 64, 128), BF16),
    "gq_all": ((256, D), BF16),
    "g1t_all": ((D, D), BF16),
    "g1_nat": ((D, D), F32),
    "g2_low": ((D, 256), BF16),
    "gy_recv": ((4, 128, 256), BF16),
    "gy_sum": ((128, 256), BF16),
    "gz_recv": ((4, 32, 256), BF16),
    "gz_sum": ((32, 256), BF16),
    "gx_recv": ((4, 32, 256), BF16),
    "g2_all": ((D, D), BF16),
    "gout_low": ((D, 256), BF16),
    "gout_recv": ((2, 8, 64, 256), BF16),
    "gout_sum": ((64, 256), BF16),
    "gout_all": ((64, D), BF16),
    "gup_all": ((D, 256), BF16),
    "gdown_all": ((256, D), BF16),
    "ua_s1": ((64, 32, 128), BF16),
    "ua_r1": ((48, 32, 128), BF16),
    "ua_s2": ((16, 32, 128), BF16),
    "ua_r2": ((12, 32, 128), BF16),
    "ua_s3": ((4, 32, 128), BF16),
    "ua_r3": ((3, 32, 128), BF16),
    "ub_s1": ((64, 32, 128), BF16),
    "ub_r1": ((48, 32, 128), BF16),
    "ub_s2": ((16, 32, 128), BF16),
    "ub_r2": ((12, 32, 128), BF16),
    "ub_s3": ((4, 32, 128), BF16),
    "ub_r3": ((3, 32, 128), BF16),
    "da_s1": ((64, 16, 256), BF16),
    "da_r1": ((48, 16, 256), BF16),
    "da_s2": ((16, 16, 256), BF16),
    "da_r2": ((12, 16, 256), BF16),
    "da_s3": ((4, 16, 256), BF16),
    "da_r3": ((3, 16, 256), BF16),
    "db_s1": ((64, 16, 256), BF16),
    "db_r1": ((48, 16, 256), BF16),
    "db_s2": ((16, 16, 256), BF16),
    "db_r2": ((12, 16, 256), BF16),
    "db_s3": ((4, 16, 256), BF16),
    "db_r3": ((3, 16, 256), BF16),
}


def layer_kernel(*refs):
    x_hbm, dy_hbm, gains_hbm, biases_hbm = refs[0:4]
    states, (mixed_ref, ingrad_ref, vec_ref), kept = refs[4:19], refs[19:22], refs[22:37]
    sems, local_sems = refs[-2:]
    (
        x_ref,
        dy_ref,
        gains_ref,
        biases_ref,
        x_all,
        h1_all,
        w_all,
        out_all,
        up_all,
        down_all,
        gate_low,
        proj_t,
        k_nat,
        v_nat,
        s_buf,
        p_buf,
        ds_buf,
        o_t,
        o_low,
        lse,
        heads_t,
        g1_buf,
        attn_buf,
        x1_buf,
        xhat_buf,
        rstd_buf,
        h2_pair,
        g2_buf,
        act_buf,
        dgelu_buf,
        ffn_own,
        ffn_send,
        ffn_recv,
        dffn_pair,
        dz2_full,
        dz1_full,
        dattn_full,
        dz2_half,
        dattn_half,
        dhid_buf,
        dh2_own,
        dh2_send,
        dh2_recv,
        dh2_gate,
        back_send,
        back_t,
        vec,
        vec_s,
        vec_a,
        vec_b,
        dq_t,
        dk_t,
        dv_t,
        dproj_low,
        dproj_all,
        gq_low,
        gq_sib,
        gq_send,
        gq_recv,
        gq_all,
        g1t_all,
        g1_nat,
        g2_low,
        gy_recv,
        gy_sum,
        gz_recv,
        gz_sum,
        gx_recv,
        g2_all,
        gout_low,
        gout_recv,
        gout_sum,
        gout_all,
        gup_all,
        gdown_all,
        *part_refs,
    ) = refs[37:-2]
    pairs = [(x_hbm, x_ref)] + [(states[i], kept[i]) for i in (0, 3, 6, 9)]
    pairs += [(gains_hbm, gains_ref), (biases_hbm, biases_ref), (states[12], kept[12])]
    pairs += [(dy_hbm, dy_ref)]
    pairs += [(states[i], kept[i]) for i in range(15) if i % 3]
    loads = [
        pltpu.make_async_copy(src, dst, local_sems.at[i]) for i, (src, dst) in enumerate(pairs)
    ]
    for load in loads[0:9]:
        load.start()

    dp, head = lax.axis_index("dp"), lax.axis_index("head")
    x_hi, y, core = dp // 8, (dp // 2) % 4, dp % 2
    z, x_lo = head // 2, head % 2
    xx = x_hi * 2 + x_lo
    sub = x_hi * 4 + y
    links = Links(sems)

    def head_peer(o):
        return (head + o) % 8

    def in_head(o):
        return (dp, (head + o) % 8)

    def head_from(o):
        return (head + 8 - o) % 8

    def sub_peer(o):
        return (sub + o) % 8

    def in_sub(o):
        return (((sub + o) % 8) * 2 + core, head)

    def ring(axis, o):
        nx = (xx + o) % 4 if axis == "x" else xx
        ny = (y + o) % 4 if axis == "y" else y
        nz = (z + o) % 4 if axis == "z" else z
        return ((nx // 2) * 8 + ny * 2 + core, nz * 2 + nx % 2)

    sibling = (sub * 2 + (1 - core), head)

    barrier = pltpu.get_barrier_semaphore()
    greeted = [in_head(o) for o in range(1, 8)] + [in_sub(o) for o in range(1, 8)]
    greeted += [sibling, ((1 - x_hi) * 8 + y * 2 + core, z * 2 + 1 - x_lo)]
    for device in greeted:
        pl.semaphore_signal(
            barrier, inc=1, device_id=device, device_id_type=pl.DeviceIdType.MESH
        )

    own = pl.ds(aligned(head * ROWS, ROWS), ROWS)
    own_core = pl.ds(aligned(core * ROWS, ROWS), ROWS)
    sib_core = pl.ds(aligned((1 - core) * ROWS, ROWS), ROWS)
    half = pl.ds(aligned(core * 256, 256), 256)
    sib_half = pl.ds(aligned((1 - core) * 256, 256), 256)
    own_heads = pl.ds(aligned(head * 64, 64), 64)
    own_w = pl.ds(aligned(head * 192, 64), 192)
    sub_rows = pl.ds(aligned(sub * 128, 128), 128)

    for load in loads[0:5]:
        load.wait()
    x_all[own, :] = x_ref[...]
    w_all[own_w, :] = kept[0][...].astype(BF16)
    out_all[own_heads, :] = kept[3][...].astype(BF16)
    up_all[:, own] = kept[6][:, own_core].astype(BF16)
    down_all[own, :] = kept[9][own_core, :].astype(BF16)

    def rows_of(ref, first, unit):
        def at(s):
            parts = ((0, unit), (0, unit // 2), (unit // 2, unit // 2))
            return [ref.at[pl.ds(aligned(first(s) + a, unit // 2), n), :] for a, n in parts]

        return at

    def up_at(s):
        cols = pl.ds(aligned(s * 128, 128), 128)
        first = (y % 2) * 256
        parts = ((0, 256), (0, 128), (128, 128))
        return [up_all.at[pl.ds(aligned(first + a, 128), n), cols] for a, n in parts]

    class Spread:
        def __init__(self, at, three, four, seven=None, last=None):
            self.at, self.last, self.one = at, last, at(head)[0]
            self.ring_z = Group(links, three, 3, self.one)
            self.over_x = Group(links, four)
            self.over_last = None if last is None else Group(links, seven)

        def begin(self):
            for o in range(1, 4):
                self.ring_z.send(self.one, self.one, ring("z", o), o - 1)

        def forward(self, s):
            _, first, second = self.at(s)
            self.over_x.send(first, first, ring("x", 1))
            self.over_x.send(second, second, ring("x", 3))

        def pass_on(self):
            for o in range(1, 4):
                self.ring_z.wait(o - 1)
                s = ((z + 4 - o) % 4) * 2 + x_lo
                self.forward(s)
                if self.last is not None:
                    self.last(self.over_last, *self.at(s))

        def pass_last(self):
            self.over_x.wait()
            for o in range(4):
                self.last(self.over_last, *self.at(((z + o) % 4) * 2 + 1 - x_lo))

    def to_sibling(group, whole, first, second):
        group.send(whole, whole, sibling)

    def to_both_y(group, whole, first, second):
        group.send(first, first, ring("y", 1))
        group.send(second, second, ring("y", 3))

    spread_out = Spread(
        rows_of(out_all, lambda s: s * 64 + core * 32, 32),
        out_all.at[0:96, :],
        out_all.at[0:128, :],
        out_all.at[0:224, :],
        to_sibling,
    )
    spread_up = Spread(
        up_at,
        up_all.at[0:256, 0:384],
        up_all.at[0:256, 0:512],
        up_all.at[0:256, 0:896],
        to_both_y,
    )
    spread_down = Spread(
        rows_of(down_all, lambda s: s * 128 + (y % 2) * 64, 64),
        down_all.at[0:192, :],
        down_all.at[0:256, :],
        down_all.at[0:448, :],
        to_both_y,
    )
    spread_w = Spread(
        rows_of(w_all, lambda s: s * 192 + core * 96, 96),
        w_all.at[0:288, :],
        w_all.at[0:384, :],
        w_all.at[0:672, :],
        to_sibling,
    )
    x_group = Group(links, x_all.at[0 : 7 * ROWS, :], 7, x_ref)

    pl.semaphore_wait(barrier, len(greeted))
    beside = (dp, z * 2 + 1 - x_lo)
    for o in range(1, 4):
        x_group.send(x_ref, x_all.at[own, :], ring("z", o), o - 1)
    x_group.send(x_ref, x_all.at[own, :], beside, 3)
    spread_out.forward(head)
    spread_up.forward(head)
    spread_down.forward(head)
    for load in loads[9:19]:
        load.start()

    for load in loads[5:9]:
        load.wait()
    for i in range(2):
        gate_low[i] = kept[12][D * i : D * i + D, :].astype(BF16)
    gain_one, shift_one = gains_ref[0:1, :], biases_ref[0:1, :]
    gain_two, shift_two = gains_ref[1:2, :], biases_ref[1:2, :]

    def project(block):
        for s in range(4):
            rows = pl.ds(aligned(block * ROWS + 32 * s, 32), 32)
            v = x_all[rows, :].astype(F32)
            center = v - jnp.mean(v, axis=-1, keepdims=True)
            spread = jnp.mean(center * center, axis=-1, keepdims=True)
            h = center * lax.rsqrt(spread + NORM_EPS) * gain_one + shift_one
            h1_all[rows, :] = h.astype(BF16)
        rows = pl.ds(aligned(block * ROWS, ROWS), ROWS)
        pt = dot(w_all[own_w, :], h1_all[rows, :], NT)
        proj_t[0:64, rows] = (pt[0:64].astype(BF16).astype(F32) * 0.125).astype(BF16)
        proj_t[64:192, rows] = pt[64:192].astype(BF16)
        k_nat[rows, :] = pt[64:128].T.astype(BF16)
        v_nat[rows, :] = pt[128:192].T.astype(BF16)

    def from_z(o):
        return ((z + 4 - o) % 4) * 2

    project(head)
    x_group.wait(3)
    block = x_all.at[pl.ds(aligned((z * 2 + 1 - x_lo) * ROWS, ROWS), ROWS), :]
    x_group.send(block, block, ring("z", 1), 4)
    x_group.send(block, block, ring("z", 3), 5)
    spread_out.begin()
    spread_up.begin()
    spread_down.begin()
    project(z * 2 + 1 - x_lo)
    x_group.wait(0)
    project(from_z(1) + x_lo)
    x_group.wait(2)
    project(from_z(3) + x_lo)
    x_group.wait(1)
    block = x_all.at[pl.ds(aligned((from_z(2) + x_lo) * ROWS, ROWS), ROWS), :]
    x_group.send(block, block, beside, 6)
    project(from_z(2) + x_lo)
    spread_out.pass_on()
    x_group.wait(4)
    project(from_z(1) + 1 - x_lo)
    x_group.wait(5)
    project(from_z(3) + 1 - x_lo)
    x_group.wait(6)
    project(from_z(2) + 1 - x_lo)

    for j in range(LEN // QB):
        cols = slice(QB * j, QB * (j + 1))
        queries = proj_t[0:64, cols]
        ceiling = jnp.full((1, QB), -1e30, F32)
        tiles = QB * (j + 1) // ROWS
        for t in range(tiles):
            s = dot(k_nat[ROWS * t : ROWS * (t + 1), :], queries)
            if ROWS * t >= QB * j:
                keys_at = lax.broadcasted_iota(jnp.int32, (ROWS, QB), 0) + ROWS * t
                queries_at = lax.broadcasted_iota(jnp.int32, (ROWS, QB), 1) + QB * j
                s = jnp.where(keys_at <= queries_at, s, -1e30)
            s_buf[ROWS * t : ROWS * (t + 1), :] = s
            ceiling = jnp.maximum(ceiling, jnp.max(s, axis=0, keepdims=True))
        mass = jnp.zeros((1, QB), F32)
        for t in range(tiles):
            e = jnp.exp(s_buf[ROWS * t : ROWS * (t + 1), :] - ceiling)
            mass = mass + jnp.sum(e, axis=0, keepdims=True)
            p_buf[ROWS * t : ROWS * (t + 1), :] = e.astype(BF16)
        total = dot(proj_t[128:192, 0 : QB * (j + 1)], p_buf[0 : QB * (j + 1), :])
        total = total / mass
        o_t[:, cols] = total
        o_low[:, cols] = total.astype(BF16)
        lse[:, cols] = ceiling + jnp.log(mass)
    heads_group = Group(links, heads_t.at[0:448, 0:ROWS])
    for o in range(1, 8):
        block = o_low.at[:, pl.ds(aligned(head_peer(o) * ROWS, ROWS), ROWS)]
        heads_group.send(block, heads_t.at[own_heads, own_core], in_head(o))
    heads_t[own_heads, own_core] = o_low[:, own]

    g1_buf[...] = dot(h1_all[own, :], gate_low[0]) + biases_ref[2:3, :]
    spread_w.begin()
    spread_w.forward(head)
    spread_out.pass_last()
    spread_up.pass_on()
    spread_down.pass_on()
    spread_up.pass_last()
    heads_group.wait()
    headst_group = Group(links, heads_t.at[:, 0:ROWS])
    headst_group.send(heads_t.at[:, own_core], heads_t.at[:, own_core], sibling)
    spread_out.over_last.wait()
    attn_buf[...] = dot(heads_t[:, own_core], out_all[...], TN)
    for s in range(4):
        rows = slice(32 * s, 32 * s + 32)
        g1 = jax.nn.sigmoid(g1_buf[rows, :])
        g1_buf[rows, :] = g1
        x = x_ref[rows, :].astype(F32)
        x1 = g1 * attn_buf[rows, :] + (1.0 - g1) * x
        x1_buf[rows, :] = x1
        center = x1 - jnp.mean(x1, axis=-1, keepdims=True)
        spread = jnp.mean(center * center, axis=-1, keepdims=True)
        rstd = lax.rsqrt(spread + NORM_EPS)
        xhat = center * rstd
        xhat_buf[rows, :] = xhat
        rstd_buf[rows, :] = jnp.broadcast_to(rstd, (32, 128))
        h2 = xhat * gain_two + shift_two
        h2_pair[pl.ds(aligned(core * ROWS + 32 * s, 32), 32), :] = h2.astype(BF16)
    h2_group = Group(links, h2_pair.at[0:ROWS, :])
    h2_group.send(h2_pair.at[own_core, :], h2_pair.at[own_core, :], sibling)
    g2_buf[...] = dot(h2_pair[own_core, :], gate_low[1]) + biases_ref[3:4, :]
    spread_down.pass_last()
    spread_up.over_last.wait()
    h2_group.wait()
    for n in range(4):
        cols = slice(256 * n, 256 * n + 256)
        u = dot(h2_pair[...], up_all[:, cols])
        c0 = 0.7978845608028654
        inner = jnp.tanh(c0 * (u + 0.044715 * u * u * u))
        act_buf[:, cols] = (0.5 * u * (1.0 + inner)).astype(BF16)
        dgelu_buf[:, cols] = 0.5 * (1.0 + inner) + 0.5 * u * (1.0 - inner * inner) * c0 * (
            1.0 + 3.0 * 0.044715 * u * u
        )
    spread_down.over_last.wait()
    ffn_send[...] = dot(act_buf[sib_core, :], down_all[...]).astype(BF16)
    ffn_group = Group(links, ffn_recv)
    ffn_group.send(ffn_send, ffn_recv, sibling)
    spread_w.pass_on()
    ffn_own[...] = dot(act_buf[own_core, :], down_all[...])
    ffn_group.wait()
    bias_two = jnp.zeros((1, D), F32)
    for s in range(4):
        rows = slice(32 * s, 32 * s + 32)
        ffn = ffn_own[rows, :] + ffn_recv[rows, :].astype(F32)
        g2 = jax.nn.sigmoid(g2_buf[rows, :])
        g2_buf[rows, :] = g2
        x1 = x1_buf[rows, :]
        dy = dy_ref[rows, :].astype(F32)
        mixed_ref[rows, :] = g2 * ffn + (1.0 - g2) * x1
        dffn_pair[pl.ds(aligned(core * ROWS + 32 * s, 32), 32), :] = (g2 * dy).astype(BF16)
        dz = (dy * (ffn - x1) * g2 * (1.0 - g2)).astype(BF16)
        dz2_full[rows, :] = dz
        bias_two = bias_two + jnp.sum(dz.astype(F32), axis=0, keepdims=True)
    dffn_group = Group(links, dffn_pair.at[0:ROWS, :])
    dffn_group.send(dffn_pair.at[own_core, :], dffn_pair.at[own_core, :], sibling)
    dz2_group = Group(links, dz2_half.at[0:ROWS, :])
    dz2_group.send(dz2_full.at[:, sib_half], dz2_half.at[own_core, :], sibling)
    dz2_half[own_core, :] = dz2_full[:, half]
    dh2_gate[...] = dot(dz2_full[...], gate_low[1], NT)

    place = {"x": xx, "y": y, "z": z}

    class Staged:
        def __init__(self, axes, refs):
            self.axes, self.refs, self.step, self.group = axes, refs, 0, None

        def put(self, ch, value):
            a, b, c = (ch[axis] for axis in self.axes)
            self.refs[0][a * 16 + b * 4 + c] = value

        def send(self):
            axis, size = self.axes[self.step], (16, 4, 1)[self.step]
            src, got = self.refs[2 * self.step : 2 * self.step + 2]
            self.group = Group(links, got)
            for o in range(1, 4):
                t = (place[axis] + o) % 4
                block = got.at[pl.ds((o - 1) * size, size)]
                self.group.send(src.at[pl.ds(t * size, size)], block, ring(axis, o))

        def add(self, store=None):
            at, size = place[self.axes[self.step]], (16, 4, 1)[self.step]
            src, got = self.refs[2 * self.step : 2 * self.step + 2]
            self.group.wait()
            self.step += 1
            to = None if store else self.refs[2 * self.step]

            def one(i):
                total = src[at * size + i].astype(F32)
                for o in range(3):
                    total = total + got[o * size + i].astype(F32)
                return total.astype(BF16)

            if store:
                store(one(0))
                return

            def body(i, carry):
                to[i] = one(i)
                return carry

            lax.fori_loop(0, size, body, 0)

        def next(self):
            self.add()
            self.send()

    up_a, up_b, down_a, down_b = (
        Staged(axes, part_refs[6 * i : 6 * i + 6])
        for i, axes in enumerate(("yzx", "xyz", "yxz", "zxy"))
    )

    dz2_group.wait()
    g2_low[...] = dot(h2_pair[...], dz2_half[...], TN).astype(BF16)
    g2_group = Group(links, gy_recv.at[0:3])
    for o in range(1, 4):
        block = g2_low.at[pl.ds(aligned(((y + o) % 4) * 128, 128), 128), :]
        g2_group.send(block, gy_recv.at[y], ring("y", o))
    gy_recv[y] = g2_low[pl.ds(aligned(y * 128, 128), 128), :]

    dffn_group.wait()
    def chip_of(h, g):
        return {"x": (g // 4) * 2 + h % 2, "y": g % 4, "z": h // 2}

    for h in range(8):
        gd = dot(act_buf[:, 128 * h : 128 * h + 128], dffn_pair[...], TN).astype(BF16)
        for g in range(8):
            down_a.put(chip_of(h, g), gd[16 * g : 16 * g + 16, 0:256])
            down_b.put(chip_of(h, g), gd[16 * g : 16 * g + 16, 256:512])
    down_a.send()
    for n in range(4):
        cols = slice(256 * n, 256 * n + 256)
        da = dot(dffn_pair[...], down_all[cols, :], NT)
        dhid_buf[:, cols] = (da * dgelu_buf[:, cols]).astype(BF16)
    dh2_send[...] = dot(dhid_buf[sib_core, :], up_all[...], NT).astype(BF16)
    dh2_group = Group(links, dh2_recv)
    dh2_group.send(dh2_send, dh2_recv, sibling)
    for h in range(8):
        gu = dot(h2_pair[...], dhid_buf[:, 128 * h : 128 * h + 128], TN).astype(BF16)
        for g in range(8):
            up_a.put(chip_of(h, g), gu[64 * g : 64 * g + 32, :])
            up_b.put(chip_of(h, g), gu[64 * g + 32 : 64 * g + 64, :])
    up_a.send()
    dh2_own[...] = dot(dhid_buf[own_core, :], up_all[...], NT)
    dh2_group.wait()
    gain_sum = jnp.zeros((1, D), F32)
    shift_sum = jnp.zeros((1, D), F32)
    bias_one = jnp.zeros((1, D), F32)
    for s in range(4):
        rows = slice(32 * s, 32 * s + 32)
        dh2 = dh2_own[rows, :] + dh2_recv[rows, :].astype(F32) + dh2_gate[rows, :]
        xhat = xhat_buf[rows, :]
        gain_sum = gain_sum + jnp.sum(dh2 * xhat, axis=0, keepdims=True)
        shift_sum = shift_sum + jnp.sum(dh2, axis=0, keepdims=True)
        dxhat = dh2 * gain_two
        mean_a = jnp.mean(dxhat, axis=-1, keepdims=True)
        mean_b = jnp.mean(dxhat * xhat, axis=-1, keepdims=True)
        rstd = rstd_buf[rows, 0:1]
        dx1 = (1.0 - g2_buf[rows, :]) * dy_ref[rows, :].astype(F32) + rstd * (
            dxhat - mean_a - xhat * mean_b
        )
        g1 = g1_buf[rows, :]
        dattn_full[rows, :] = (g1 * dx1).astype(BF16)
        x = x_ref[rows, :].astype(F32)
        dz = (dx1 * (attn_buf[rows, :] - x) * g1 * (1.0 - g1)).astype(BF16)
        dz1_full[rows, :] = dz
        bias_one = bias_one + jnp.sum(dz.astype(F32), axis=0, keepdims=True)
        ingrad_ref[rows, :] = (1.0 - g1) * dx1
    vec[1:2, :] = gain_sum
    vec[3:4, :] = shift_sum
    vec[4:5, :] = bias_one
    vec[5:6, :] = bias_two
    vec[6:8, :] = jnp.zeros((2, D), F32)

    dheads = dot(out_all[...], dattn_full[...], NT).astype(BF16)
    dz1_t = dz1_full[...].astype(F32).T.astype(BF16)
    for h in range(8):
        back_send[h, 0:64, :] = dheads[64 * h : 64 * h + 64, :]
        back_send[h, 64:128, :] = dz1_t[64 * h : 64 * h + 64, :]
    back_group = Group(links, back_t.at[:, 0 : 7 * ROWS])
    for o in range(1, 8):
        back_group.send(back_send.at[head_peer(o)], back_t.at[:, own], in_head(o))
    back_t[:, own] = back_send[head]
    dattn_group = Group(links, dattn_half.at[0:ROWS, :])
    dattn_group.send(dattn_full.at[:, sib_half], dattn_half.at[own_core, :], sibling)
    dattn_half[own_core, :] = dattn_full[:, half]
    down_b.send()
    up_b.send()

    headst_group.wait()
    dattn_group.wait()
    gout_low[...] = dot(heads_t[...], dattn_half[...]).astype(BF16)

    def add_slots(ref, n=8):
        total = ref[0].astype(F32)
        for o in range(1, n):
            total = total + ref[o].astype(F32)
        return total

    g2_group.wait()
    gy_sum[...] = add_slots(gy_recv, 4).astype(BF16)
    g2_group = Group(links, gz_recv.at[0:3])
    for o in range(1, 4):
        block = gy_sum.at[pl.ds(aligned(((z + o) % 4) * 32, 32), 32), :]
        g2_group.send(block, gz_recv.at[z], ring("z", o))
    gz_recv[z] = gy_sum[pl.ds(aligned(z * 32, 32), 32), :]

    back_group.wait()
    dk_t[...] = jnp.zeros_like(dk_t)
    dv_t[...] = jnp.zeros_like(dv_t)
    for j in range(LEN // QB):
        cols = slice(QB * j, QB * (j + 1))
        upto = QB * (j + 1)
        queries = proj_t[0:64, cols]
        grads = back_t[0:64, cols]
        delta = jnp.sum(o_t[:, cols] * grads.astype(F32), axis=0, keepdims=True)
        row_lse = lse[:, cols]
        for t in range(upto // ROWS):
            keys = slice(ROWS * t, ROWS * (t + 1))
            p = jnp.exp(dot(k_nat[keys, :], queries) - row_lse)
            if ROWS * t >= QB * j:
                keys_at = lax.broadcasted_iota(jnp.int32, (ROWS, QB), 0) + ROWS * t
                queries_at = lax.broadcasted_iota(jnp.int32, (ROWS, QB), 1) + QB * j
                p = jnp.where(keys_at <= queries_at, p, 0.0)
            d = dot(v_nat[keys, :], grads)
            p_buf[keys, :] = p.astype(BF16)
            ds_buf[keys, :] = (p * (d - delta)).astype(BF16)
        dq_t[:, cols] = dot(proj_t[64:128, 0:upto], ds_buf[0:upto, :]) * 0.125
        dk_t[:, 0:upto] += dot(queries, ds_buf[0:upto, :], NT)
        dv_t[:, 0:upto] += dot(grads, p_buf[0:upto, :], NT)
    dproj_low[0:64, :] = dq_t[...].astype(BF16)
    dproj_low[64:128, :] = dk_t[...].astype(BF16)
    dproj_low[128:192, :] = dv_t[...].astype(BF16)
    dproj_low[192:256, :] = back_t[64:128, :]
    dproj_group = Group(links, dproj_all.at[0 : 7 * 192, :])
    for o in range(1, 8):
        block = dproj_low.at[0:192, pl.ds(aligned(head_peer(o) * ROWS, ROWS), ROWS)]
        dproj_group.send(block, dproj_all.at[own_w, :], in_head(o))
    dproj_all[own_w, :] = dproj_low[0:192, own]

    gq_low[...] = dot(dproj_low[...], h1_all[...]).astype(BF16)
    gq_pair = Group(links, gq_sib)
    gq_pair.send(gq_low.at[:, sib_half], gq_sib, sibling)

    gout_group = Group(links, gout_recv.at[0, 0:7])
    for o in range(1, 8):
        block = gout_low.at[pl.ds(aligned(head_peer(o) * 64, 64), 64), :]
        gout_group.send(block, gout_recv.at[0, head], in_head(o))
    gout_recv[0, head] = gout_low[own_heads, :]

    down_a.next()
    gq_pair.wait()
    total = gq_low[:, half].astype(F32) + gq_sib[...].astype(F32)
    for i in range(8):
        r, c = 64 * (i // 2), 128 * (i % 2)
        gq_send[i] = total[r : r + 64, c : c + 128].astype(BF16)
    gq_group = Group(links, gq_recv.at[0:7])
    for o in range(1, 8):
        gq_group.send(gq_send.at[sub_peer(o)], gq_recv.at[sub], in_sub(o))
    gq_recv[sub] = gq_send[sub]

    down_b.next()
    up_b.next()

    g2_group.wait()
    gz_sum[...] = add_slots(gz_recv, 4).astype(BF16)
    g2_group = Group(links, gx_recv.at[0:3])
    for o in range(1, 4):
        g2_group.send(gz_sum, gx_recv.at[xx], ring("x", o))
    gx_recv[xx] = gz_sum[...]
    spread_w.pass_last()
    up_a.next()


    gq_group.wait()
    gq_rows = pl.ds(aligned((sub // 2) * 64, 64), 64)
    gq_cols = pl.ds(aligned(core * 256 + (sub % 2) * 128, 128), 128)
    gq_all[gq_rows, gq_cols] = add_slots(gq_recv).astype(BF16)
    gq_group = Group(links, gq_recv.at[0:7])
    for o in range(1, 8):
        block = gq_all.at[gq_rows, gq_cols]
        gq_group.send(block, block, in_sub(o))

    g2_group.wait()
    g2_rows = pl.ds(aligned(y * 128 + z * 32, 32), 32)
    g2_all[g2_rows, half] = add_slots(gx_recv, 4).astype(BF16)
    g2_group = Group(links, gz_recv.at[0:3])
    for o in range(1, 4):
        block = g2_all.at[g2_rows, half]
        g2_group.send(block, block, ring("z", o))

    dproj_group.wait()
    spread_w.over_last.wait()
    dh2_own[...] = dot(dproj_all[...], w_all[...], TN) + dot(dz1_full[...], gate_low[0], NT)
    gain_sum = jnp.zeros((1, D), F32)
    shift_sum = jnp.zeros((1, D), F32)
    for s in range(4):
        rows = slice(32 * s, 32 * s + 32)
        v = x_ref[rows, :].astype(F32)
        center = v - jnp.mean(v, axis=-1, keepdims=True)
        spread = jnp.mean(center * center, axis=-1, keepdims=True)
        rstd = lax.rsqrt(spread + NORM_EPS)
        xhat = center * rstd
        dh = dh2_own[rows, :]
        gain_sum = gain_sum + jnp.sum(dh * xhat, axis=0, keepdims=True)
        shift_sum = shift_sum + jnp.sum(dh, axis=0, keepdims=True)
        dxhat = dh * gain_one
        mean_a = jnp.mean(dxhat, axis=-1, keepdims=True)
        mean_b = jnp.mean(dxhat * xhat, axis=-1, keepdims=True)
        ingrad_ref[rows, :] += rstd * (dxhat - mean_a - xhat * mean_b)
    vec[0:1, :] = gain_sum
    vec[2:3, :] = shift_sum
    vec_group = Group(links, vec_s)
    vec_group.send(vec, vec_s, sibling)

    def update(i, grad):
        rows, cols = SHAPES[i]
        step = 16 if cols == D else 32

        def strip(n, carry):
            at = pl.ds(aligned(n * step, step), step)
            refs = kept[3 * i : 3 * i + 3]
            new = adamw(*(r[at, :] for r in refs), grad[at, :].astype(F32), RATES[i])
            for r, value in zip(refs, new):
                r[at, :] = value
            return carry

        lax.fori_loop(0, rows // step, strip, 0)

    def update_gate(first, grad):
        def strip(n, carry):
            at = pl.ds(aligned(n * 16, 16), 16)
            into = pl.ds(aligned(first + n * 16, 16), 16)
            refs = kept[12:15]
            new = adamw(*(r[into, :] for r in refs), grad[at, :].astype(F32), RATES[4])
            for r, value in zip(refs, new):
                r[into, :] = value
            return carry

        lax.fori_loop(0, D // 16, strip, 0)

    for load in loads[9:19]:
        load.wait()

    down_a.next()
    down_b.next()
    up_b.next()
    gout_group.wait()
    gout_sum[...] = add_slots(gout_recv.at[0]).astype(BF16)
    gout_group = Group(links, gout_recv.at[1, 0:7])
    for o in range(1, 8):
        gout_group.send(gout_sum, gout_recv.at[1, sub], in_sub(o))
    gout_recv[1, sub] = gout_sum[...]

    vec_group.wait()
    vec_a[sub] = vec[...] + vec_s[...]
    vec_group = Group(links, vec_a.at[0:7])
    for o in range(1, 8):
        vec_group.send(vec_a.at[sub], vec_a.at[sub], in_sub(o))

    up_a.next()

    g2_group.wait()
    g2_group = Group(links, gy_recv.at[0:3])
    block = g2_all.at[pl.ds(aligned(y * 128, 128), 128), half]
    for o in range(1, 4):
        g2_group.send(block, block, ring("y", o))

    gq_group.wait()
    gq_pair = Group(links, gq_sib.at[0:192, :])
    gq_pair.send(gq_all.at[0:192, half], gq_all.at[0:192, half], sibling)
    g1_group = Group(links, g1t_all.at[0:448, 0:256])
    for o in range(1, 8):
        g1_group.send(gq_all.at[192:256, half], g1t_all.at[own_heads, half], in_head(o))
    g1t_all[own_heads, half] = gq_all[192:256, half]

    vec_group.wait()
    vec_b[head] = add_slots(vec_a)
    vec_group = Group(links, vec_b.at[0:7])
    for o in range(1, 8):
        vec_group.send(vec_b.at[head], vec_b.at[head], in_head(o))

    up_rows = pl.ds(aligned(sub * 64, 64), 64)
    down_rows = pl.ds(aligned(core * 128 + sub * 16, 16), 16)

    def to_down(cols):
        def store(value):
            gdown_all[down_rows, cols] = value

        return store

    def to_up(first):
        def store(value):
            gup_all[pl.ds(aligned(sub * 64 + first, 32), 32), own_core] = value

        return store

    down_a.add(to_down(slice(0, 256)))
    down_b.add(to_down(slice(256, 512)))
    down_group = Group(links, gdown_all.at[0:112, :])
    for o in range(1, 8):
        block = gdown_all.at[down_rows, :]
        down_group.send(block, block, in_sub(o))
    up_b.add(to_up(32))
    up_a.add(to_up(0))
    up_group = Group(links, gup_all.at[0:448, 0:128])
    for o in range(1, 8):
        block = gup_all.at[up_rows, own_core]
        up_group.send(block, block, in_sub(o))
    gout_group.wait()
    gout_all[:, half] = add_slots(gout_recv.at[1]).astype(BF16)
    gout_pair = Group(links, gout_sum)
    gout_pair.send(gout_all.at[:, half], gout_all.at[:, half], sibling)

    gq_pair.wait()
    update(0, gq_all)
    gout_pair.wait()
    update(1, gout_all)
    g2_group.wait()
    g2_pair = Group(links, g2_low)
    g2_pair.send(g2_all.at[:, half], g2_all.at[:, half], sibling)
    g1_group.wait()
    g1_pair = Group(links, g2_low)
    g1_pair.send(g1t_all.at[:, half], g1t_all.at[:, half], sibling)
    g2_pair.wait()
    update_gate(D, g2_all)
    down_group.wait()
    down_pair = Group(links, gdown_all.at[0:128, :])
    down_pair.send(gdown_all.at[own_core, :], gdown_all.at[own_core, :], sibling)
    up_group.wait()
    up_pair = Group(links, gup_all.at[:, 0:128])
    up_pair.send(gup_all.at[:, own_core], gup_all.at[:, own_core], sibling)
    g1_pair.wait()
    for n in range(4):
        at = slice(128 * n, 128 * n + 128)
        g1_nat[at, :] = g1t_all[:, at].astype(F32).T
    update_gate(0, g1_nat)
    down_pair.wait()
    update(3, gdown_all)
    up_pair.wait()
    update(2, gup_all)
    vec_group.wait()
    vec_ref[...] = add_slots(vec_b)
    links.drain()


VMEM = pl.BlockSpec(memory_space=pltpu.VMEM)
ANY = pl.BlockSpec(memory_space=pl.ANY)
HBM = pl.BlockSpec(memory_space=pltpu.HBM)


def run_layer(*args):
    in_vmem = [pltpu.VMEM(s, F32) for s in SHAPES[0:5] for _ in range(3)]
    shapes = [pltpu.VMEM(s, F32) for s in ((ROWS, D), (ROWS, D), (8, D))]
    return pl.pallas_call(
        layer_kernel,
        out_shape=shapes + in_vmem,
        in_specs=[HBM] * 19,
        out_specs=[VMEM] * 18,
        scratch_shapes=[pltpu.VMEM(s, t) for s, t in SCRATCH.values()]
        + [pltpu.SemaphoreType.DMA((N_SEMS,)), pltpu.SemaphoreType.DMA((N_LOCAL,))],
        compiler_params=pltpu.CompilerParams(
            collective_id=0, has_side_effects=True, vmem_limit_bytes=40 * 1024 * 1024
        ),
        name="layer",
    )(*args)


def finish_kernel(*refs):
    results, small, vec = refs[0:17], refs[17:23], refs[23]
    outs, new_small, sems = refs[24:41], refs[41:47], refs[47]
    copies = [
        pltpu.make_async_copy(a, b, sems.at[i]) for i, (a, b) in enumerate(zip(results, outs))
    ]
    for c in copies:
        c.start()
    for i, (lo, hi) in enumerate(((0, 2), (2, 6))):
        at = slice(3 * i, 3 * i + 3)
        for ref, value in zip(
            new_small[at], adamw(*(r[...] for r in small[at]), vec[lo:hi, :], RATES[5 + i])
        ):
            ref[...] = value
    for c in copies:
        c.wait()


def finish(results, small, vec):
    return pl.pallas_call(
        finish_kernel,
        out_shape=[jax.ShapeDtypeStruct(a.shape, F32) for a in (*results, *small)],
        in_specs=[VMEM] * 24,
        out_specs=[ANY] * 17 + [VMEM] * 6,
        scratch_shapes=[pltpu.SemaphoreType.DMA((17,))],
        compiler_params=pltpu.CompilerParams(vmem_limit_bytes=4 * 1024 * 1024),
        name="finish",
    )(*results, *small, vec)


def local(inputs, cotangent, *state):
    rows = inputs.shape[1]
    flat = list(state)
    for i in (0, 1, 2):
        flat[i] = jnp.transpose(flat[i], (0, 2, 1)).reshape(192, D)
    for i in (12, 13, 14):
        flat[i] = flat[i].reshape(2 * D, D)
    operands = (inputs.reshape(rows, D), cotangent.reshape(rows, D), flat[15], flat[18])
    operands += tuple(flat[0:15])
    mixed, ingrad, vec, *new = run_layer(
        *(pltpu.with_memory_space_constraint(a, pltpu.HBM) for a in operands)
    )
    mixed, ingrad, *new = finish((mixed, ingrad, *new), flat[15:21], vec)
    for i in (0, 1, 2):
        new[i] = jnp.transpose(new[i].reshape(3, 64, D), (0, 2, 1))
    for i in (12, 13, 14):
        new[i] = new[i].reshape(2, D, D)
    return (mixed.reshape(1, rows, D), ingrad.reshape(1, rows, D), *new)


def solution(mesh):
    batch = P("dp", "head", None)
    qkv = P(None, None, "head")
    first = P("head", None)
    second = P(None, "head")
    state = (qkv,) * 3 + (first,) * 3 + (second,) * 3 + (first,) * 3 + (P(),) * 9
    return jax.shard_map(
        local,
        mesh=mesh,
        in_specs=(batch, batch, *state),
        out_specs=(batch, batch, *state),
        check_vma=False,
    )
```

time: 113 us -> 91.8 us (0.81)
  Pallas kernels: 112 us -> 90.7 us
    pallas_call x2, Pallas kernels: 112 us -> 90.7 us  [the longest x1 85.6 us: run_layer(): pl.pallas_call(layer_kernel, out_shape=shapes + in_vmem, in_specs=[HBM] *...]
where the time goes in v3:
time: 91.8 us; the launch traced here: 91.7 us
  Pallas kernels  90.7 us (99%)
  between operations  0.93 us (1%)
    pallas_call x1, Pallas kernels, run_layer(): pl.pallas_call(layer_kernel, out_shape=shapes + in_vmem, in_specs=[HBM] *...  85.6 us
    pallas_call x1, Pallas kernels, finish(): pl.pallas_call(finish_kernel, out_shape=[jax.ShapeDtypeStruct(a.shape, F3...  5.11 us

profile of v3, /device:TPU:1, one launch (start us, length us, event | category | flops | bytes accessed | tf_op | source)
XLA Modules:
  0.0 91.7 jit_solution(2970942009034248475)
XLA Ops:
  0.7 0.0 copy-start
  0.7 0.0 copy-start.1
  0.7 0.0 copy-start.2
  0.7 0.0 copy-start.3
  0.7 0.0 copy-start.4
  0.7 0.0 copy-start.5
  0.7 85.6 %layer.1 = (f32[128,512]{1,0:T(8,128)S(1)}, f32[128,512]{1,0:T(8,128)S(1)}, f32[8,512]{1,0:T(8,128)S(1)}, f32[192,512]{1,0:T(8,128)S(1)}, f32[192,512]{1,0:T(8,1...) custom-call(bf16[128,512]{1,0:T(8,128)(2,1)} %bitcast.34, ...), custom_call_target="tpu_custom_call" | custom-call | tf_op jit(solution)/shard_map/layer/pallas_call | solution.py:965
  86.4 0.0 copy-done
  86.4 0.0 copy-done.1
  86.4 0.0 copy-done.2
  86.4 0.0 copy-done.3
  86.4 0.0 copy-done.4
  86.4 0.0 copy-done.5
  86.4 5.1 %finish.1 = (f32[128,512]{1,0:T(8,128)}, f32[128,512]{1,0:T(8,128)}, f32[192,512]{1,0:T(8,128)}, f32[192,512]{1,0:T(8,128)}, f32[192,512]{1,0:T(8,128)}, /*index...) custom-call(f32[128,512]{1,0:T(8,128)S(1)} %get-tuple-element.64.ref, ...), custom_call_target="tpu_custom_call" | custom-call | tf_op jit(solution)/shard_map/finish/pallas_call | solution.py:998
Async XLA Ops:
  0.7 85.7 %copy-start = (f32[4,512]{1,0:T(4,128)S(1)}, f32[4,512]{1,0:T(4,128)}, u32[]{:S(2)}) copy-start(f32[4,512]{1,0:T(4,128)} %refs_20_.1) | copy-start | bytes 24580
  0.7 85.7 %copy-start.1 = (f32[2,512]{1,0:T(2,128)S(1)}, f32[2,512]{1,0:T(2,128)}, u32[]{:S(2)}) copy-start(f32[2,512]{1,0:T(2,128)} %refs_17_.1) | copy-start | bytes 12292
  0.7 85.7 %copy-start.2 = (f32[4,512]{1,0:T(4,128)S(1)}, f32[4,512]{1,0:T(4,128)}, u32[]{:S(2)}) copy-start(f32[4,512]{1,0:T(4,128)} %refs_21_.1) | copy-start | bytes 24580
  0.7 85.7 %copy-start.3 = (f32[4,512]{1,0:T(4,128)S(1)}, f32[4,512]{1,0:T(4,128)}, u32[]{:S(2)}) copy-start(f32[4,512]{1,0:T(4,128)} %refs_22_.1) | copy-start | bytes 24580
  0.7 85.7 %copy-start.4 = (f32[2,512]{1,0:T(2,128)S(1)}, f32[2,512]{1,0:T(2,128)}, u32[]{:S(2)}) copy-start(f32[2,512]{1,0:T(2,128)} %refs_18_.1) | copy-start | bytes 12292
  0.7 85.7 %copy-start.5 = (f32[2,512]{1,0:T(2,128)S(1)}, f32[2,512]{1,0:T(2,128)}, u32[]{:S(2)}) copy-start(f32[2,512]{1,0:T(2,128)} %refs_19_.1) | copy-start | bytes 12292

commit v4 on v3

v4 whole, which is shorter than its diff:
```python
import jax
import jax.numpy as jnp
from jax import lax
from jax.experimental import pallas as pl
from jax.experimental.pallas import tpu as pltpu
from jax.sharding import PartitionSpec as P

F32 = jnp.float32
BF16 = jnp.bfloat16
STEP = 10
NORM_EPS = 1e-05
BETA_ONE = 0.9
BETA_TWO = 0.999
ADAM_EPS = 1e-08
DECAY = 0.01
RATES = (0.04, 0.1, 0.04, 0.02, 0.04, 0.4, 0.3)
D = 512
ROWS = 128
LEN = 1024
QB = 256
NN = ((1,), (0,))
NT = ((1,), (1,))
TN = ((0,), (0,))


def dot(a, b, dims=NN):
    return lax.dot_general(a, b, (dims, ((), ())), preferred_element_type=F32)


def aligned(value, by):
    return pl.multiple_of(value, by)


class Group:
    def __init__(self, links, total, receives=1, each=None):
        self.send_sem, self.total = links.semaphore(), total
        self.each = total if each is None else each
        self.recv_sems = [links.semaphore() for _ in range(receives)]
        links.groups.append(self)

    def send(self, src, dst, device, k=0):
        pltpu.make_async_remote_copy(
            src_ref=src,
            dst_ref=dst,
            send_sem=self.send_sem,
            recv_sem=self.recv_sems[k],
            device_id=device,
            device_id_type=pl.DeviceIdType.MESH,
        ).start()

    def wait(self, k=0):
        pltpu.make_async_copy(self.each, self.each, self.recv_sems[k]).wait()


class Links:
    def __init__(self, sems):
        self.sems, self.used, self.groups = sems, 0, []

    def semaphore(self):
        self.used += 1
        return self.sems.at[self.used - 1]

    def drain(self):
        for g in self.groups:
            pltpu.make_async_copy(g.total, g.total, g.send_sem).wait()


N_SEMS = 138
N_LOCAL = 23


SHAPES = ((192, D), (64, D), (D, 256), (256, D), (2 * D, D), (2, D), (4, D))


def adamw(weight, first, second, grad, rate):
    first = BETA_ONE * first + (1.0 - BETA_ONE) * grad
    second = BETA_TWO * second + (1.0 - BETA_TWO) * grad * grad
    root = (1.0 - BETA_TWO**STEP) ** 0.5
    step = (rate * root / (1.0 - BETA_ONE**STEP)) * first / (jnp.sqrt(second) + ADAM_EPS * root)
    return ((1.0 - rate * DECAY) * weight - step, first, second)


SCRATCH = [
    ((ROWS, D), BF16),
    ((ROWS, D), BF16),
    ((LEN, D), BF16),
    ((LEN, D), BF16),
    ((1536, D), BF16),
    ((D, D), BF16),
    ((D, 1024), BF16),
    ((1024, D), BF16),
    ((2, D, D), BF16),
    ((D, D), BF16),
    ((192, LEN), BF16),
    ((LEN, 64), BF16),
    ((LEN, 64), BF16),
    ((LEN, QB), F32),
    ((LEN, LEN), BF16),
    ((LEN, QB), BF16),
    ((64, LEN), F32),
    ((64, LEN), BF16),
    ((1, LEN), F32),
    ((D, 256), BF16),
    ((ROWS, D), F32),
    ((ROWS, D), F32),
    ((ROWS, D), F32),
    ((ROWS, D), F32),
    ((ROWS, 128), F32),
    ((256, D), BF16),
    ((ROWS, D), F32),
    ((256, 1024), BF16),
    ((256, 1024), F32),
    ((ROWS, D), F32),
    ((ROWS, D), BF16),
    ((ROWS, D), BF16),
    ((256, D), BF16),
    ((ROWS, D), BF16),
    ((ROWS, D), BF16),
    ((ROWS, D), BF16),
    ((256, 256), BF16),
    ((256, 256), BF16),
    ((256, 1024), BF16),
    ((ROWS, D), F32),
    ((ROWS, D), BF16),
    ((ROWS, D), BF16),
    ((ROWS, D), F32),
    ((8, 128, ROWS), BF16),
    ((128, LEN), BF16),
    ((8, D), F32),
    ((8, D), F32),
    ((8, 8, D), F32),
    ((8, 8, D), F32),
    ((64, LEN), F32),
    ((64, LEN), F32),
    ((64, LEN), F32),
    ((192, LEN), BF16),
    ((1536, ROWS), BF16),
    ((192, D), BF16),
    ((192, D), F32),
    ((64, D), F32),
    ((64, D), BF16),
    ((64, 256), BF16),
    ((8, 16, 128), BF16),
    ((8, 16, 128), BF16),
    ((192, 256), BF16),
    ((8, 48, 128), BF16),
    ((8, 48, 128), BF16),
    ((192, D), BF16),
    ((D, D), BF16),
    ((D, D), F32),
    ((D, 256), BF16),
    ((4, 128, 256), BF16),
    ((128, 256), BF16),
    ((4, 32, 256), BF16),
    ((32, 256), BF16),
    ((4, 32, 256), BF16),
    ((D, D), BF16),
    ((D, 256), BF16),
    ((4, 128, 256), BF16),
    ((128, 256), BF16),
    ((4, 32, 256), BF16),
    ((32, 256), BF16),
    ((4, 32, 256), BF16),
    ((64, D), BF16),
    ((D, 256), BF16),
    ((256, D), BF16),
]
for part in ((32, 128), (32, 128), (16, 256), (16, 256)):
    SCRATCH += [((count, *part), BF16) for count in (64, 48, 16, 12, 4, 3)]


def layer_kernel(*refs):
    x_hbm, dy_hbm, states = refs[0], refs[1], refs[2:23]
    mixed_ref, ingrad_ref, kept = refs[23], refs[24], refs[25:46]
    gains_ref, biases_ref = kept[15], kept[18]
    sems, local_sems = refs[-2:]
    (
        x_ref,
        dy_ref,
        x_all,
        h1_all,
        w_all,
        out_all,
        up_all,
        down_all,
        gate_low,
        gate_t,
        proj_t,
        k_nat,
        v_nat,
        s_buf,
        e_buf,
        ds_buf,
        o_t,
        o_low,
        inv_mass,
        heads_t,
        g1_buf,
        attn_buf,
        x1_buf,
        xhat_buf,
        rstd_buf,
        h2_pair,
        g2_buf,
        act_buf,
        dgelu_buf,
        ffn_own,
        ffn_send,
        ffn_recv,
        dffn_pair,
        dz2_full,
        dz1_full,
        dattn_full,
        dz2_half,
        dattn_half,
        dhid_buf,
        dh2_own,
        dh2_send,
        dh2_recv,
        dh2_gate,
        back_send,
        back_t,
        vec,
        vec_s,
        vec_a,
        vec_b,
        dq_t,
        dk_t,
        dv_t,
        dproj_low,
        dproj_all,
        gq_low,
        gq_f32,
        g1_f32,
        g1_low,
        g1_sib,
        g1_send,
        g1_recv,
        gq_sib,
        gq_send,
        gq_recv,
        gq_all,
        g1t_all,
        g1_nat,
        g2_low,
        gy_recv,
        gy_sum,
        gz_recv,
        gz_sum,
        gx_recv,
        g2_all,
        gout_low,
        go_z,
        go_zs,
        go_x,
        go_xs,
        go_y,
        gout_all,
        gup_all,
        gdown_all,
        *part_refs,
    ) = refs[46:-2]
    dp, head = lax.axis_index("dp"), lax.axis_index("head")
    x_hi, y, core = dp // 8, (dp // 2) % 4, dp % 2
    z, x_lo = head // 2, head % 2
    xx = x_hi * 2 + x_lo
    sub = x_hi * 4 + y
    links = Links(sems)

    def head_peer(o):
        return (head + o) % 8

    def in_head(o):
        return (dp, (head + o) % 8)

    def head_from(o):
        return (head + 8 - o) % 8

    def sub_peer(o):
        return (sub + o) % 8

    def in_sub(o):
        return (((sub + o) % 8) * 2 + core, head)

    def ring(axis, o):
        nx = (xx + o) % 4 if axis == "x" else xx
        ny = (y + o) % 4 if axis == "y" else y
        nz = (z + o) % 4 if axis == "z" else z
        return ((nx // 2) * 8 + ny * 2 + core, nz * 2 + nx % 2)

    sibling = (sub * 2 + (1 - core), head)

    barrier = pltpu.get_barrier_semaphore()
    greeted = [in_head(o) for o in range(1, 8)] + [in_sub(o) for o in range(1, 8)]
    greeted += [sibling, ((1 - x_hi) * 8 + y * 2 + core, z * 2 + 1 - x_lo)]
    for device in greeted:
        pl.semaphore_signal(
            barrier, inc=1, device_id=device, device_id_type=pl.DeviceIdType.MESH
        )

    pairs = [(x_hbm, x_ref)] + [(states[i], kept[i]) for i in (0, 3, 6, 9, 15, 18, 12)]
    pairs += [(dy_hbm, dy_ref)] + [(states[i], kept[i]) for i in range(21) if i % 3]
    loads = [
        pltpu.make_async_copy(src, dst, local_sems.at[i]) for i, (src, dst) in enumerate(pairs)
    ]
    for load in loads[0:9]:
        load.start()

    own = pl.ds(aligned(head * ROWS, ROWS), ROWS)
    own_core = pl.ds(aligned(core * ROWS, ROWS), ROWS)
    sib_core = pl.ds(aligned((1 - core) * ROWS, ROWS), ROWS)
    half = pl.ds(aligned(core * 256, 256), 256)
    sib_half = pl.ds(aligned((1 - core) * 256, 256), 256)
    own_heads = pl.ds(aligned(head * 64, 64), 64)
    own_w = pl.ds(aligned(head * 192, 64), 192)
    sub_rows = pl.ds(aligned(sub * 128, 128), 128)

    def rows_of(ref, first, unit):
        def at(s):
            parts = ((0, unit), (0, unit // 2), (unit // 2, unit // 2))
            return [ref.at[pl.ds(aligned(first(s) + a, unit // 2), n), :] for a, n in parts]

        return at

    def up_at(s):
        cols = pl.ds(aligned(s * 128, 128), 128)
        first = (y % 2) * 256
        parts = ((0, 256), (0, 128), (128, 128))
        return [up_all.at[pl.ds(aligned(first + a, 128), n), cols] for a, n in parts]

    class Spread:
        def __init__(self, at, three, four, seven=None, last=None):
            self.at, self.last, self.one = at, last, at(head)[0]
            self.ring_z = Group(links, three, 3, self.one)
            self.over_x = Group(links, four)
            self.over_last = None if last is None else Group(links, seven)

        def begin(self):
            for o in range(1, 4):
                self.ring_z.send(self.one, self.one, ring("z", o), o - 1)

        def begin_x(self):
            self.forward(head)

        def forward(self, s):
            _, first, second = self.at(s)
            self.over_x.send(first, first, ring("x", 1))
            self.over_x.send(second, second, ring("x", 3))

        def pass_on(self):
            for o in range(1, 4):
                self.ring_z.wait(o - 1)
                s = ((z + 4 - o) % 4) * 2 + x_lo
                self.forward(s)
                if self.last is not None:
                    self.last(self.over_last, *self.at(s))

        def pass_last(self):
            self.over_x.wait()
            for o in range(4):
                self.last(self.over_last, *self.at(((z + o) % 4) * 2 + 1 - x_lo))

    def to_sibling(group, whole, first, second):
        group.send(whole, whole, sibling)

    def to_both_y(group, whole, first, second):
        group.send(first, first, ring("y", 1))
        group.send(second, second, ring("y", 3))

    spread_out = Spread(
        rows_of(out_all, lambda s: s * 64 + core * 32, 32),
        out_all.at[0:96, :],
        out_all.at[0:128, :],
        out_all.at[0:224, :],
        to_sibling,
    )
    spread_up = Spread(
        up_at,
        up_all.at[0:256, 0:384],
        up_all.at[0:256, 0:512],
        up_all.at[0:256, 0:896],
        to_both_y,
    )
    spread_down = Spread(
        rows_of(down_all, lambda s: s * 128 + (y % 2) * 64, 64),
        down_all.at[0:192, :],
        down_all.at[0:256, :],
        down_all.at[0:448, :],
        to_both_y,
    )
    spread_w = Spread(
        rows_of(w_all, lambda s: s * 192 + core * 96, 96),
        w_all.at[0:288, :],
        w_all.at[0:384, :],
        w_all.at[0:672, :],
        to_sibling,
    )
    x_group = Group(links, x_all.at[0 : 7 * ROWS, :], 7, x_ref)

    class Groups:
        pass

    g = Groups()

    beside = (dp, z * 2 + 1 - x_lo)
    gain_one, shift_one = pl.ds(0, 1), pl.ds(0, 1)
    gain_two, shift_two = pl.ds(1, 1), pl.ds(1, 1)

    def project(block):
        for s in range(4):
            rows = pl.ds(aligned(block * ROWS + 32 * s, 32), 32)
            v = x_all[rows, :].astype(F32)
            center = v - jnp.mean(v, axis=-1, keepdims=True)
            spread = jnp.mean(center * center, axis=-1, keepdims=True)
            h = center * lax.rsqrt(spread + NORM_EPS) * gains_ref[gain_one, :] + biases_ref[shift_one, :]
            h1_all[rows, :] = h.astype(BF16)
        rows = pl.ds(aligned(block * ROWS, ROWS), ROWS)
        pt = dot(w_all[own_w, :], h1_all[rows, :], NT)
        proj_t[0:64, rows] = (pt[0:64].astype(BF16).astype(F32) * 0.125).astype(BF16)
        proj_t[64:192, rows] = pt[64:192].astype(BF16)
        k_nat[rows, :] = pt[64:128].T.astype(BF16)
        v_nat[rows, :] = pt[128:192].T.astype(BF16)

    def from_z(o):
        return ((z + 4 - o) % 4) * 2

    place = {"x": xx, "y": y, "z": z}

    class Staged:
        def __init__(self, axes, refs):
            self.axes, self.refs, self.step, self.group = axes, refs, 0, None

        def put(self, ch, value):
            a, b, c = (ch[axis] for axis in self.axes)
            self.refs[0][a * 16 + b * 4 + c] = value

        def send(self):
            axis, size = self.axes[self.step], (16, 4, 1)[self.step]
            src, got = self.refs[2 * self.step : 2 * self.step + 2]
            self.group = Group(links, got)
            for o in range(1, 4):
                t = (place[axis] + o) % 4
                block = got.at[pl.ds((o - 1) * size, size)]
                self.group.send(src.at[pl.ds(t * size, size)], block, ring(axis, o))

        def add(self, store=None):
            at, size = place[self.axes[self.step]], (16, 4, 1)[self.step]
            src, got = self.refs[2 * self.step : 2 * self.step + 2]
            self.group.wait()
            self.step += 1
            to = None if store else self.refs[2 * self.step]

            def some(i, n):
                total = src[pl.ds(at * size + i, n)].astype(F32)
                for o in range(3):
                    total = total + got[pl.ds(o * size + i, n)].astype(F32)
                return total.astype(BF16)

            if store:
                store(some(0, 1)[0])
                return

            def body(i, carry):
                to[pl.ds(i * 4, 4)] = some(i * 4, 4)
                return carry

            lax.fori_loop(0, size // 4, body, 0)

        def next(self):
            self.add()
            self.send()

    up_a, up_b, down_a, down_b = (
        Staged(axes, part_refs[6 * i : 6 * i + 6])
        for i, axes in enumerate(("yzx", "xyz", "yxz", "zxy"))
    )

    def chip_of(h, n):
        return {"x": (n // 4) * 2 + h % 2, "y": n % 4, "z": h // 2}

    def add_slots(ref, n=8):
        total = ref[0].astype(F32)
        for o in range(1, n):
            total = total + ref[o].astype(F32)
        return total

    def block_of(ref, at, rows, cols=slice(None)):
        return ref.at[pl.ds(aligned(at * rows, rows), rows), cols]

    def to_all(group, peers, ref):
        for o in range(1, 4 if peers not in (in_head, in_sub) else 8):
            group.send(ref, ref, peers(o))

    def in_ring(axis):
        return lambda o: ring(axis, o)

    def update(i, grad, first=0, rows=None):
        rows = SHAPES[i][0] if rows is None else rows
        step = 32 if SHAPES[i][1] == D else 64

        def strip(n, carry):
            at = pl.ds(aligned(n * step, step), step)
            into = pl.ds(aligned(first + n * step, step), step)
            refs = kept[3 * i : 3 * i + 3]
            values = adamw(*(r[into, :] for r in refs), grad[at, :].astype(F32), RATES[i])
            for r, value in zip(refs, values):
                r[into, :] = value
            return carry

        lax.fori_loop(0, rows // step, strip, 0, unroll=2)


    def x_out():
        for o in range(1, 4):
            x_group.send(x_ref, x_all.at[own, :], ring("z", o), o - 1)
        x_group.send(x_ref, x_all.at[own, :], beside, 3)

    def cast_weights():
        for load in loads[1:5]:
            load.wait()
        w_all[own_w, :] = kept[0][...].astype(BF16)
        out_all[own_heads, :] = kept[3][...].astype(BF16)
        up_all[:, own] = kept[6][:, own_core].astype(BF16)
        down_all[own, :] = kept[9][own_core, :].astype(BF16)

    def load_rest():
        for load in loads[9:]:
            load.start()
        for load in loads[5:9]:
            load.wait()
        for i in range(2):
            gate_low[i] = kept[12][D * i : D * i + D, :].astype(BF16)
        for n in range(4):
            cols = slice(128 * n, 128 * n + 128)
            gate_t[cols, :] = kept[12][0:D, cols].T.astype(BF16)

    def project_own():
        project(head)

    def x_pass_z():
        x_group.wait(3)
        block = block_of(x_all, z * 2 + 1 - x_lo, ROWS)
        x_group.send(block, block, ring("z", 1), 4)
        x_group.send(block, block, ring("z", 3), 5)

    def project_beside():
        project(z * 2 + 1 - x_lo)

    def from_z(o):
        return ((z + 4 - o) % 4) * 2

    def project_near():
        x_group.wait(0)
        project(from_z(1) + x_lo)
        x_group.wait(2)
        project(from_z(3) + x_lo)

    def x_pass_x():
        x_group.wait(1)
        block = block_of(x_all, from_z(2) + x_lo, ROWS)
        x_group.send(block, block, beside, 6)

    def project_far():
        project(from_z(2) + x_lo)

    def project_passed():
        x_group.wait(4)
        project(from_z(1) + 1 - x_lo)
        x_group.wait(5)
        project(from_z(3) + 1 - x_lo)

    def project_last():
        x_group.wait(6)
        project(from_z(2) + 1 - x_lo)


    def attention():
        for j in range(LEN // QB):
            cols = slice(QB * j, QB * (j + 1))
            queries = proj_t[0:64, cols]
            ceiling = jnp.full((1, QB), -1e30, F32)
            tiles = QB * (j + 1) // ROWS
            for t in range(tiles):
                s = dot(k_nat[ROWS * t : ROWS * (t + 1), :], queries)
                if ROWS * t >= QB * j:
                    keys_at = lax.broadcasted_iota(jnp.int32, (ROWS, QB), 0) + ROWS * t
                    queries_at = lax.broadcasted_iota(jnp.int32, (ROWS, QB), 1) + QB * j
                    s = jnp.where(keys_at <= queries_at, s, -1e30)
                s_buf[ROWS * t : ROWS * (t + 1), :] = s
                ceiling = jnp.maximum(ceiling, jnp.max(s, axis=0, keepdims=True))
            mass = jnp.zeros((1, QB), F32)
            for t in range(tiles):
                e = jnp.exp(s_buf[ROWS * t : ROWS * (t + 1), :] - ceiling)
                mass = mass + jnp.sum(e, axis=0, keepdims=True)
                e_buf[ROWS * t : ROWS * (t + 1), cols] = e.astype(BF16)
            total = dot(proj_t[128:192, 0 : QB * (j + 1)], e_buf[0 : QB * (j + 1), cols])
            total = total / mass
            o_t[:, cols] = total
            o_low[:, cols] = total.astype(BF16)
            inv_mass[:, cols] = 1.0 / mass
        group = g.heads = Group(links, heads_t.at[0:448, 0:ROWS])
        for o in range(1, 8):
            block = o_low.at[:, pl.ds(aligned(head_peer(o) * ROWS, ROWS), ROWS)]
            group.send(block, heads_t.at[own_heads, own_core], in_head(o))
        heads_t[own_heads, own_core] = o_low[:, own]


    def gate_one():
        g1_buf[...] = dot(h1_all[own, :], gate_low[0]) + biases_ref[2:3, :]

    def middle():
        g.heads.wait()
        group = g.heads_pair = Group(links, heads_t.at[:, 0:ROWS])
        group.send(heads_t.at[:, own_core], heads_t.at[:, own_core], sibling)
        spread_out.over_last.wait()
        attn_buf[...] = dot(heads_t[:, own_core], out_all[...], TN)
        for s in range(4):
            rows = slice(32 * s, 32 * s + 32)
            g1 = jax.nn.sigmoid(g1_buf[rows, :])
            g1_buf[rows, :] = g1
            x = x_ref[rows, :].astype(F32)
            x1 = g1 * attn_buf[rows, :] + (1.0 - g1) * x
            x1_buf[rows, :] = x1
            center = x1 - jnp.mean(x1, axis=-1, keepdims=True)
            spread = jnp.mean(center * center, axis=-1, keepdims=True)
            rstd = lax.rsqrt(spread + NORM_EPS)
            xhat = center * rstd
            xhat_buf[rows, :] = xhat
            rstd_buf[rows, :] = jnp.broadcast_to(rstd, (32, 128))
            h2 = xhat * gains_ref[gain_two, :] + biases_ref[shift_two, :]
            h2_pair[pl.ds(aligned(core * ROWS + 32 * s, 32), 32), :] = h2.astype(BF16)
        group = g.h2 = Group(links, h2_pair.at[0:ROWS, :])
        group.send(h2_pair.at[own_core, :], h2_pair.at[own_core, :], sibling)

    def gate_two():
        g2_buf[...] = dot(h2_pair[own_core, :], gate_low[1]) + biases_ref[3:4, :]

    def hidden():
        g.h2.wait()
        spread_up.over_last.wait()
        for n in range(4):
            cols = slice(256 * n, 256 * n + 256)
            u = dot(h2_pair[...], up_all[:, cols])
            c0 = 0.7978845608028654
            inner = jnp.tanh(c0 * (u + 0.044715 * u * u * u))
            act_buf[:, cols] = (0.5 * u * (1.0 + inner)).astype(BF16)
            dgelu_buf[:, cols] = 0.5 * (1.0 + inner) + 0.5 * u * (1.0 - inner * inner) * c0 * (
                1.0 + 3.0 * 0.044715 * u * u
            )

    def ffn():
        spread_down.over_last.wait()
        ffn_send[...] = dot(act_buf[sib_core, :], down_all[...]).astype(BF16)
        g.ffn = Group(links, ffn_recv)
        g.ffn.send(ffn_send, ffn_recv, sibling)
        ffn_own[...] = dot(act_buf[own_core, :], down_all[...])

    def mix():
        g.ffn.wait()
        bias_two = jnp.zeros((1, D), F32)
        for s in range(4):
            rows = slice(32 * s, 32 * s + 32)
            total = ffn_own[rows, :] + ffn_recv[rows, :].astype(F32)
            g2 = jax.nn.sigmoid(g2_buf[rows, :])
            g2_buf[rows, :] = g2
            x1 = x1_buf[rows, :]
            dy = dy_ref[rows, :].astype(F32)
            mixed_ref[rows, :] = g2 * total + (1.0 - g2) * x1
            dffn_pair[pl.ds(aligned(core * ROWS + 32 * s, 32), 32), :] = (g2 * dy).astype(BF16)
            dz = (dy * (total - x1) * g2 * (1.0 - g2)).astype(BF16)
            dz2_full[rows, :] = dz
            bias_two = bias_two + jnp.sum(dz.astype(F32), axis=0, keepdims=True)
        group = g.dffn = Group(links, dffn_pair.at[0:ROWS, :])
        group.send(dffn_pair.at[own_core, :], dffn_pair.at[own_core, :], sibling)
        group = g.dz2 = Group(links, dz2_half.at[0:ROWS, :])
        group.send(dz2_full.at[:, sib_half], dz2_half.at[own_core, :], sibling)
        dz2_half[own_core, :] = dz2_full[:, half]
        vec[5:6, :] = bias_two
        vec[6:8, :] = jnp.zeros((2, D), F32)


    def back_gate_two():
        dh2_gate[...] = dot(dz2_full[...], gate_low[1], NT)

    def back_hidden():
        g.dffn.wait()
        for n in range(4):
            cols = slice(256 * n, 256 * n + 256)
            da = dot(dffn_pair[...], down_all[cols, :], NT)
            dhid_buf[:, cols] = (da * dgelu_buf[:, cols]).astype(BF16)
        dh2_send[...] = dot(dhid_buf[sib_core, :], up_all[...], NT).astype(BF16)
        g.dh2 = Group(links, dh2_recv)
        g.dh2.send(dh2_send, dh2_recv, sibling)
        dh2_own[...] = dot(dhid_buf[own_core, :], up_all[...], NT)

    def back_middle():
        g.dh2.wait()
        gain_sum = jnp.zeros((1, D), F32)
        shift_sum = jnp.zeros((1, D), F32)
        bias_one = jnp.zeros((1, D), F32)
        for s in range(4):
            rows = slice(32 * s, 32 * s + 32)
            dh2 = dh2_own[rows, :] + dh2_recv[rows, :].astype(F32) + dh2_gate[rows, :]
            xhat = xhat_buf[rows, :]
            gain_sum = gain_sum + jnp.sum(dh2 * xhat, axis=0, keepdims=True)
            shift_sum = shift_sum + jnp.sum(dh2, axis=0, keepdims=True)
            dxhat = dh2 * gains_ref[gain_two, :]
            mean_a = jnp.mean(dxhat, axis=-1, keepdims=True)
            mean_b = jnp.mean(dxhat * xhat, axis=-1, keepdims=True)
            rstd = rstd_buf[rows, 0:1]
            dx1 = (1.0 - g2_buf[rows, :]) * dy_ref[rows, :].astype(F32) + rstd * (
                dxhat - mean_a - xhat * mean_b
            )
            g1 = g1_buf[rows, :]
            dattn_full[rows, :] = (g1 * dx1).astype(BF16)
            x = x_ref[rows, :].astype(F32)
            dz = (dx1 * (attn_buf[rows, :] - x) * g1 * (1.0 - g1)).astype(BF16)
            dz1_full[rows, :] = dz
            bias_one = bias_one + jnp.sum(dz.astype(F32), axis=0, keepdims=True)
            ingrad_ref[rows, :] = (1.0 - g1) * dx1
        dheads = dot(out_all[...], dattn_full[...], NT).astype(BF16)
        dz1_t = dz1_full[...].astype(F32).T.astype(BF16)
        for h in range(8):
            back_send[h, 0:64, :] = dheads[64 * h : 64 * h + 64, :]
            back_send[h, 64:128, :] = dz1_t[64 * h : 64 * h + 64, :]
        group = g.back = Group(links, back_t.at[:, 0 : 7 * ROWS])
        for o in range(1, 8):
            group.send(back_send.at[head_peer(o)], back_t.at[:, own], in_head(o))
        back_t[:, own] = back_send[head]
        group = g.dattn = Group(links, dattn_half.at[0:ROWS, :])
        group.send(dattn_full.at[:, sib_half], dattn_half.at[own_core, :], sibling)
        dattn_half[own_core, :] = dattn_full[:, half]
        vec[1:2, :] = gain_sum
        vec[3:4, :] = shift_sum
        vec[4:5, :] = bias_one

    def back_attention():
        dk_t[...] = jnp.zeros_like(dk_t)
        dv_t[...] = jnp.zeros_like(dv_t)
        for j in range(LEN // QB):
            cols = slice(QB * j, QB * (j + 1))
            upto = QB * (j + 1)
            queries = proj_t[0:64, cols]
            grads = back_t[0:64, cols]
            inverse = inv_mass[:, cols]
            delta = jnp.sum(o_t[:, cols] * grads.astype(F32), axis=0, keepdims=True)
            for t in range(upto // ROWS):
                keys = slice(ROWS * t, ROWS * (t + 1))
                p = e_buf[keys, cols].astype(F32) * inverse
                ds_buf[keys, :] = (p * (dot(v_nat[keys, :], grads) - delta)).astype(BF16)
            dq_t[:, cols] = dot(proj_t[64:128, 0:upto], ds_buf[0:upto, :]) * 0.125
            dk_t[:, 0:upto] += dot(queries, ds_buf[0:upto, :], NT)
            scaled = (grads.astype(F32) * inverse).astype(BF16)
            dv_t[:, 0:upto] += dot(scaled, e_buf[0:upto, cols], NT)
        dproj_low[0:64, :] = dq_t[...].astype(BF16)
        dproj_low[64:128, :] = dk_t[...].astype(BF16)
        dproj_low[128:192, :] = dv_t[...].astype(BF16)
        group = g.dproj = Group(links, dproj_all.at[0 : 7 * 192, :])
        for o in range(1, 8):
            block = dproj_low.at[:, pl.ds(aligned(head_peer(o) * ROWS, ROWS), ROWS)]
            group.send(block, dproj_all.at[own_w, :], in_head(o))
        dproj_all[own_w, :] = dproj_low[:, own]

    def input_grad():
        g.dproj.wait()
        spread_w.over_last.wait()
        dh2_own[...] = dot(dproj_all[...], w_all[...], TN) + dot(
            dz1_full[...], gate_low[0], NT
        )
        for s in range(4):
            rows = slice(32 * s, 32 * s + 32)
            v = x_ref[rows, :].astype(F32)
            center = v - jnp.mean(v, axis=-1, keepdims=True)
            spread = jnp.mean(center * center, axis=-1, keepdims=True)
            rstd = lax.rsqrt(spread + NORM_EPS)
            xhat = center * rstd
            dxhat = dh2_own[rows, :] * gains_ref[gain_one, :]
            mean_a = jnp.mean(dxhat, axis=-1, keepdims=True)
            mean_b = jnp.mean(dxhat * xhat, axis=-1, keepdims=True)
            ingrad_ref[rows, :] += rstd * (dxhat - mean_a - xhat * mean_b)

    def vec_pair():
        gain = jnp.zeros((1, D), F32)
        shift = jnp.zeros((1, D), F32)
        gate_rows = gate_t[own_heads, :]
        for n in range(4):
            rows = slice(64 * n, 64 * n + 64)
            grads = (dproj_low[rows, :] if n < 3 else back_t[64:128, :]).astype(F32)
            sums = jnp.sum(grads, axis=1, keepdims=True)
            weights = w_all[pl.ds(aligned(head * 192 + 64 * n, 64), 64), :] if n < 3 else gate_rows
            weights = weights.astype(F32)
            products = gq_f32[rows, :] if n < 3 else g1_f32[...]
            moved = products - biases_ref[shift_one, :] * sums
            gain = gain + jnp.sum(weights * moved, axis=0, keepdims=True)
            shift = shift + jnp.sum(weights * sums, axis=0, keepdims=True)
        vec[0:1, :] = gain / gains_ref[gain_one, :]
        vec[2:3, :] = shift
        g.vec_pair = Group(links, vec_s)
        g.vec_pair.send(vec, vec_s, sibling)

    def vec_sub():
        g.vec_pair.wait()
        vec_a[sub] = vec[...] + vec_s[...]
        g.vec_sub = Group(links, vec_a.at[0:7])
        to_all(g.vec_sub, in_sub, vec_a.at[sub])

    def vec_head():
        g.vec_sub.wait()
        vec_b[head] = add_slots(vec_a)
        g.vec_head = Group(links, vec_b.at[0:7])
        to_all(g.vec_head, in_head, vec_b.at[head])

    def vec_done():
        g.vec_head.wait()
        total = add_slots(vec_b)
        for i, grad in ((5, total[0:2]), (6, total[2:6])):
            refs = kept[3 * i : 3 * i + 3]
            for r, value in zip(refs, adamw(*(r[...] for r in refs), grad, RATES[i])):
                r[...] = value


    def grad_down():
        for h in range(8):
            gd = dot(act_buf[:, 128 * h : 128 * h + 128], dffn_pair[...], TN).astype(BF16)
            for n in range(8):
                down_a.put(chip_of(h, n), gd[16 * n : 16 * n + 16, 0:256])
                down_b.put(chip_of(h, n), gd[16 * n : 16 * n + 16, 256:512])

    def grad_up():
        for h in range(8):
            gu = dot(h2_pair[...], dhid_buf[:, 128 * h : 128 * h + 128], TN).astype(BF16)
            for n in range(8):
                up_a.put(chip_of(h, n), gu[64 * n : 64 * n + 32, :])
                up_b.put(chip_of(h, n), gu[64 * n + 32 : 64 * n + 64, :])

    def down_sub():
        rows = pl.ds(aligned(core * 128 + sub * 16, 16), 16)
        for part, cols in ((down_a, slice(0, 256)), (down_b, slice(256, 512))):

            def store(value, cols=cols):
                gdown_all[rows, cols] = value

            part.add(store)
        g.down_sub = Group(links, gdown_all.at[0:112, :])
        to_all(g.down_sub, in_sub, gdown_all.at[rows, :])

    def down_pair():
        g.down_sub.wait()
        group = g.down_pair = Group(links, gdown_all.at[0:128, :])
        group.send(gdown_all.at[own_core, :], gdown_all.at[own_core, :], sibling)

    def down_done():
        g.down_pair.wait()
        update(3, gdown_all)

    def up_sub():
        for part, first in ((up_a, 0), (up_b, 32)):

            def store(value, first=first):
                gup_all[pl.ds(aligned(sub * 64 + first, 32), 32), own_core] = value

            part.add(store)
        block = block_of(gup_all, sub, 64, own_core)
        g.up_sub = Group(links, gup_all.at[0:448, 0:128])
        to_all(g.up_sub, in_sub, block)

    def up_pair():
        g.up_sub.wait()
        group = g.up_pair = Group(links, gup_all.at[:, 0:128])
        group.send(gup_all.at[:, own_core], gup_all.at[:, own_core], sibling)

    def up_done():
        g.up_pair.wait()
        update(2, gup_all)


    def second_y():
        g.dz2.wait()
        g2_low[...] = dot(h2_pair[...], dz2_half[...], TN).astype(BF16)
        group = g.second_y = Group(links, gy_recv.at[0:3])
        for o in range(1, 4):
            group.send(block_of(g2_low, (y + o) % 4, 128), gy_recv.at[y], ring("y", o))
        gy_recv[y] = g2_low[pl.ds(aligned(y * 128, 128), 128), :]

    def second_z():
        g.second_y.wait()
        gy_sum[...] = add_slots(gy_recv, 4).astype(BF16)
        group = g.second_z = Group(links, gz_recv.at[0:3])
        for o in range(1, 4):
            group.send(block_of(gy_sum, (z + o) % 4, 32), gz_recv.at[z], ring("z", o))
        gz_recv[z] = gy_sum[pl.ds(aligned(z * 32, 32), 32), :]

    def second_x():
        g.second_z.wait()
        gz_sum[...] = add_slots(gz_recv, 4).astype(BF16)
        group = g.second_x = Group(links, gx_recv.at[0:3])
        for o in range(1, 4):
            group.send(gz_sum, gx_recv.at[xx], ring("x", o))
        gx_recv[xx] = gz_sum[...]

    def second_back_z():
        g.second_x.wait()
        rows = pl.ds(aligned(y * 128 + z * 32, 32), 32)
        g2_all[rows, half] = add_slots(gx_recv, 4).astype(BF16)
        g.second_back_z = Group(links, gz_recv.at[0:3])
        to_all(g.second_back_z, in_ring("z"), g2_all.at[rows, half])

    def second_back_y():
        g.second_back_z.wait()
        block = block_of(g2_all, y, 128, half)
        g.second_back_y = Group(links, gy_recv.at[0:3])
        to_all(g.second_back_y, in_ring("y"), block)

    def second_pair():
        g.second_back_y.wait()
        group = g.second_pair = Group(links, g2_low)
        group.send(g2_all.at[:, half], g2_all.at[:, half], sibling)

    def second_done():
        g.second_pair.wait()
        update(4, g2_all, D, D)


    def grad_out_z():
        g.heads_pair.wait()
        g.dattn.wait()
        gout_low[...] = dot(heads_t[...], dattn_half[...]).astype(BF16)
        group = g.grad_out_z = Group(links, go_z.at[0:3])
        for o in range(1, 4):
            group.send(block_of(gout_low, (z + o) % 4, 128), go_z.at[z], ring("z", o))
        go_z[z] = gout_low[pl.ds(aligned(z * 128, 128), 128), :]

    def grad_out_x():
        g.grad_out_z.wait()
        go_zs[...] = add_slots(go_z, 4).astype(BF16)
        group = g.grad_out_x = Group(links, go_x.at[0:3])
        for o in range(1, 4):
            to = (xx + o) % 4
            block = block_of(go_zs, (to % 2) * 2 + to // 2, 32)
            group.send(block, go_x.at[xx], ring("x", o))
        go_x[xx] = go_zs[pl.ds(aligned((x_lo * 2 + x_hi) * 32, 32), 32), :]

    def grad_out_y():
        g.grad_out_x.wait()
        go_xs[...] = add_slots(go_x, 4).astype(BF16)
        group = g.grad_out_y = Group(links, go_y.at[0:3])
        for o in range(1, 4):
            group.send(go_xs, go_y.at[y], ring("y", o))
        go_y[y] = go_xs[...]

    def grad_out_far():
        g.grad_out_y.wait()
        rows = pl.ds(aligned(x_hi * 32, 32), 32)
        gout_all[rows, half] = add_slots(go_y, 4).astype(BF16)
        group = g.grad_out_far = Group(links, go_xs)
        group.send(gout_all.at[rows, half], gout_all.at[rows, half], ring("x", 2))

    def grad_out_pair():
        g.grad_out_far.wait()
        group = g.grad_out_pair = Group(links, go_zs.at[0:64, :])
        group.send(gout_all.at[:, half], gout_all.at[:, half], sibling)

    def grad_out_done():
        g.grad_out_pair.wait()
        update(1, gout_all)


    def qkv_pair():
        gq_f32[...] = dot(dproj_low[...], h1_all[...])
        gq_low[...] = gq_f32[...].astype(BF16)
        g.qkv_pair = Group(links, gq_sib)
        g.qkv_pair.send(gq_low.at[:, sib_half], gq_sib, sibling)

    def qkv_sub():
        g.qkv_pair.wait()
        total = gq_low[:, half].astype(F32) + gq_sib[...].astype(F32)
        for i in range(8):
            r, c = 48 * (i // 2), 128 * (i % 2)
            gq_send[i] = total[r : r + 48, c : c + 128].astype(BF16)
        group = g.qkv_sub = Group(links, gq_recv.at[0:7])
        for o in range(1, 8):
            group.send(gq_send.at[sub_peer(o)], gq_recv.at[sub], in_sub(o))
        gq_recv[sub] = gq_send[sub]

    def qkv_back():
        g.qkv_sub.wait()
        rows = pl.ds(aligned((sub // 2) * 48, 48), 48)
        cols = pl.ds(aligned(core * 256 + (sub % 2) * 128, 128), 128)
        gq_all[rows, cols] = add_slots(gq_recv).astype(BF16)
        g.qkv_back = Group(links, gq_recv.at[0:7])
        to_all(g.qkv_back, in_sub, gq_all.at[rows, cols])


    def first_start():
        g.back.wait()
        g1_f32[...] = dot(back_t[64:128, :], h1_all[...])
        g1_low[...] = g1_f32[...].astype(BF16)
        g.first_start = Group(links, g1_sib)
        g.first_start.send(g1_low.at[:, sib_half], g1_sib, sibling)

    def first_sub():
        g.first_start.wait()
        total = g1_low[:, half].astype(F32) + g1_sib[...].astype(F32)
        for i in range(8):
            r, c = 16 * (i // 2), 128 * (i % 2)
            g1_send[i] = total[r : r + 16, c : c + 128].astype(BF16)
        group = g.first_sub = Group(links, g1_recv.at[0:7])
        for o in range(1, 8):
            group.send(g1_send.at[sub_peer(o)], g1_recv.at[sub], in_sub(o))
        g1_recv[sub] = g1_send[sub]

    def first_back():
        g.first_sub.wait()
        rows = pl.ds(aligned(head * 64 + (sub // 2) * 16, 16), 16)
        cols = pl.ds(aligned(core * 256 + (sub % 2) * 128, 128), 128)
        g1t_all[rows, cols] = add_slots(g1_recv).astype(BF16)
        g.first_back = Group(links, g1_recv.at[0:7])
        to_all(g.first_back, in_sub, g1t_all.at[rows, cols])

    def first_head():
        g.first_back.wait()
        g.first_head = Group(links, g1t_all.at[0:448, 0:256])
        to_all(g.first_head, in_head, g1t_all.at[own_heads, half])

    def qkv_back_pair():
        g.qkv_back.wait()
        g.qkv_back_pair = Group(links, gq_sib)
        g.qkv_back_pair.send(gq_all.at[:, half], gq_all.at[:, half], sibling)

    def qkv_done():
        g.qkv_back_pair.wait()
        update(0, gq_all)

    def first_pair():
        g.first_head.wait()
        group = g.first_pair = Group(links, g2_low)
        group.send(g1t_all.at[:, half], g1t_all.at[:, half], sibling)

    def first_done():
        g.first_pair.wait()
        for n in range(4):
            at = slice(128 * n, 128 * n + 128)
            g1_nat[at, :] = g1t_all[:, at].astype(F32).T
        update(4, g1_nat, 0, D)

    def moments():
        for load in loads[9:]:
            load.wait()

    loads[0].wait()
    x_all[own, :] = x_ref[...]
    pl.semaphore_wait(barrier, len(greeted))
    for run in (
        x_out,
        cast_weights,
        spread_up.begin_x,
        x_pass_z,
        spread_up.begin,
        load_rest,
        spread_down.begin,
        x_pass_x,
        project_beside,
        project_own,
        spread_out.begin_x,
        project_far,
        spread_out.begin,
        spread_down.begin_x,
        project_passed,
        project_near,
        project_last,
        spread_up.pass_on,
        attention,
        spread_down.pass_on,
        spread_out.pass_on,
        spread_up.pass_last,
        spread_w.begin,
        spread_down.pass_last,
        spread_w.begin_x,
        spread_out.pass_last,
        gate_one,
        middle,
        hidden,
        ffn,
        spread_w.pass_on,
        gate_two,
        mix,
        back_gate_two,
        back_hidden,
        second_y,
        back_middle,
        grad_down,
        down_a.send,
        grad_up,
        up_a.send,
        up_b.send,
        grad_out_z,
        second_z,
        first_start,
        down_b.send,
        down_a.next,
        first_sub,
        grad_out_x,
        second_x,
        back_attention,
        up_a.next,
        qkv_pair,
        first_back,
        grad_out_y,
        down_b.next,
        up_b.next,
        qkv_sub,
        vec_pair,
        spread_w.pass_last,
        second_back_z,
        grad_out_far,
        vec_sub,
        up_b.next,
        down_a.next,
        up_a.next,
        down_b.next,
        first_head,
        second_back_y,
        input_grad,
        qkv_back,
        up_sub,
        grad_out_pair,
        down_sub,
        moments,
        grad_out_done,
        second_pair,
        vec_head,
        first_pair,
        second_done,
        qkv_back_pair,
        first_done,
        up_pair,
        down_pair,
        qkv_done,
        vec_done,
        up_done,
        down_done,
    ):
        run()
    links.drain()


VMEM = pl.BlockSpec(memory_space=pltpu.VMEM)
ANY = pl.BlockSpec(memory_space=pl.ANY)
HBM = pl.BlockSpec(memory_space=pltpu.HBM)


def run_layer(*args):
    in_vmem = [pltpu.VMEM(s, F32) for s in SHAPES for _ in range(3)]
    shapes = [pltpu.VMEM((ROWS, D), F32)] * 2
    return pl.pallas_call(
        layer_kernel,
        out_shape=shapes + in_vmem,
        in_specs=[HBM] * 23,
        out_specs=[VMEM] * 23,
        scratch_shapes=[pltpu.VMEM(s, t) for s, t in SCRATCH]
        + [pltpu.SemaphoreType.DMA((N_SEMS,)), pltpu.SemaphoreType.DMA((N_LOCAL,))],
        compiler_params=pltpu.CompilerParams(
            collective_id=0, has_side_effects=True, vmem_limit_bytes=40 * 1024 * 1024
        ),
        name="layer",
    )(*args)


def finish_kernel(*refs):
    sems = refs[46]
    copies = [
        pltpu.make_async_copy(refs[i], refs[23 + i], sems.at[i]) for i in range(23)
    ]
    for c in copies:
        c.start()
    for c in copies:
        c.wait()


def finish(results):
    return pl.pallas_call(
        finish_kernel,
        out_shape=[jax.ShapeDtypeStruct(a.shape, F32) for a in results],
        in_specs=[ANY] * 23,
        out_specs=[ANY] * 23,
        scratch_shapes=[pltpu.SemaphoreType.DMA((23,))],
        compiler_params=pltpu.CompilerParams(vmem_limit_bytes=1024 * 1024),
        name="finish",
    )(*results)


def local(inputs, cotangent, *state):
    rows = inputs.shape[1]
    flat = list(state)
    for i in (0, 1, 2):
        flat[i] = jnp.transpose(flat[i], (0, 2, 1)).reshape(192, D)
    for i in (12, 13, 14):
        flat[i] = flat[i].reshape(2 * D, D)
    operands = (inputs.reshape(rows, D), cotangent.reshape(rows, D), *flat)
    results = run_layer(*(pltpu.with_memory_space_constraint(a, pltpu.HBM) for a in operands))
    mixed, ingrad, *new = finish(results)
    for i in (0, 1, 2):
        new[i] = jnp.transpose(new[i].reshape(3, 64, D), (0, 2, 1))
    for i in (12, 13, 14):
        new[i] = new[i].reshape(2, D, D)
    return (mixed.reshape(1, rows, D), ingrad.reshape(1, rows, D), *new)


def solution(mesh):
    batch = P("dp", "head", None)
    qkv = P(None, None, "head")
    first = P("head", None)
    second = P(None, "head")
    state = (qkv,) * 3 + (first,) * 3 + (second,) * 3 + (first,) * 3 + (P(),) * 9
    return jax.shard_map(
        local,
        mesh=mesh,
        in_specs=(batch, batch, *state),
        out_specs=(batch, batch, *state),
        check_vma=False,
    )
```

time: 91.8 us -> 81.5 us (0.89)
  Pallas kernels: 90.7 us -> 80.6 us
    pallas_call x1, Pallas kernels: 85.6 us -> 76 us  [run_layer(): pl.pallas_call(layer_kernel, out_shape=shapes + in_vmem, in_specs=[HBM] *...]
where the time goes in v4:
time: 81.5 us; the launch traced here: 81.4 us
  Pallas kernels  80.6 us (99%)
  between operations  0.84 us (1%)
    pallas_call x1, Pallas kernels, run_layer(): pl.pallas_call(layer_kernel, out_shape=shapes + in_vmem, in_specs=[HBM] *...  76 us
    pallas_call x1, Pallas kernels, finish(): pl.pallas_call(finish_kernel, out_shape=[jax.ShapeDtypeStruct(a.shape, F3...  4.52 us

profile of v4, /device:TPU:1, one launch (start us, length us, event | category | flops | bytes accessed | tf_op | source)
XLA Modules:
  0.0 81.4 jit_solution(11351353603635450374)
XLA Ops:
  0.7 76.0 %layer.1 = (f32[128,512]{1,0:T(8,128)S(1)}, f32[128,512]{1,0:T(8,128)S(1)}, f32[192,512]{1,0:T(8,128)S(1)}, f32[192,512]{1,0:T(8,128)S(1)}, f32[192,512]{1,0:T(8...) custom-call(bf16[128,512]{1,0:T(8,128)(2,1)} %bitcast.34, ...), custom_call_target="tpu_custom_call" | custom-call | tf_op jit(solution)/shard_map/layer/pallas_call | solution.py:1155
  76.7 4.5 %finish.1 = (f32[128,512]{1,0:T(8,128)}, f32[128,512]{1,0:T(8,128)}, f32[192,512]{1,0:T(8,128)}, f32[192,512]{1,0:T(8,128)}, f32[192,512]{1,0:T(8,128)}, /*index...) custom-call(f32[128,512]{1,0:T(8,128)S(1)} %get-tuple-element.69.ref, ...), custom_call_target="tpu_custom_call" | custom-call | tf_op jit(solution)/shard_map/finish/pallas_call | solution.py:1181

commit v5 on v4

--- a/solution.py
+++ b/solution.py
@@ -1,3 +1,5 @@
+import math
+
 import jax
 import jax.numpy as jnp
 from jax import lax
@@ -33,7 +35,7 @@
 
 class Group:
     def __init__(self, links, total, receives=1, each=None):
-        self.send_sem, self.total = links.semaphore(), total
+        self.send_sem, self.total = links.send_sem, total
         self.each = total if each is None else each
         self.recv_sems = [links.semaphore() for _ in range(receives)]
         links.groups.append(self)
@@ -54,18 +56,20 @@
 
 class Links:
     def __init__(self, sems):
-        self.sems, self.used, self.groups = sems, 0, []
+        self.sems, self.send_sem, self.used, self.groups = sems, sems.at[0], 1, []
 
     def semaphore(self):
         self.used += 1
         return self.sems.at[self.used - 1]
 
-    def drain(self):
-        for g in self.groups:
-            pltpu.make_async_copy(g.total, g.total, g.send_sem).wait()
-
-
-N_SEMS = 138
+    def drain(self, sent):
+        words = [t.dtype.itemsize * math.prod(t.shape) for t in (g.total for g in self.groups)]
+        if sum(words) != 2 * math.prod(sent.shape):
+            raise ValueError(sum(words))
+        pltpu.make_async_copy(sent, sent, self.send_sem).wait()
+
+
+N_SEMS = 78
 N_LOCAL = 23
 
 
@@ -76,10 +80,11 @@
     first = BETA_ONE * first + (1.0 - BETA_ONE) * grad
     second = BETA_TWO * second + (1.0 - BETA_TWO) * grad * grad
     root = (1.0 - BETA_TWO**STEP) ** 0.5
-    step = (rate * root / (1.0 - BETA_ONE**STEP)) * first / (jnp.sqrt(second) + ADAM_EPS * root)
+    step = (rate * root / (1.0 - BETA_ONE**STEP)) * first / (second * lax.rsqrt(second) + ADAM_EPS * root)
     return ((1.0 - rate * DECAY) * weight - step, first, second)
 
 
+SENT_ROWS = 42816
 SCRATCH = [
     ((ROWS, D), BF16),
     ((ROWS, D), BF16),
@@ -110,6 +115,7 @@
     ((ROWS, D), F32),
     ((256, 1024), BF16),
     ((256, 1024), F32),
+    ((256, 1024), F32),
     ((ROWS, D), F32),
     ((ROWS, D), BF16),
     ((ROWS, D), BF16),
@@ -124,8 +130,10 @@
     ((ROWS, D), BF16),
     ((ROWS, D), BF16),
     ((ROWS, D), F32),
-    ((8, 128, ROWS), BF16),
-    ((128, LEN), BF16),
+    ((D, ROWS), BF16),
+    ((D, ROWS), BF16),
+    ((64, LEN), BF16),
+    ((64, LEN), BF16),
     ((8, D), F32),
     ((8, D), F32),
     ((8, 8, D), F32),
@@ -164,6 +172,7 @@
     ((64, D), BF16),
     ((D, 256), BF16),
     ((256, D), BF16),
+    ((SENT_ROWS, 128), BF16),
 ]
 for part in ((32, 128), (32, 128), (16, 256), (16, 256)):
     SCRATCH += [((count, *part), BF16) for count in (64, 48, 16, 12, 4, 3)]
@@ -204,6 +213,7 @@
         g2_buf,
         act_buf,
         dgelu_buf,
+        tanh_buf,
         ffn_own,
         ffn_send,
         ffn_recv,
@@ -218,8 +228,10 @@
         dh2_send,
         dh2_recv,
         dh2_gate,
-        back_send,
-        back_t,
+        dheads_t,
+        dz1_t,
+        do_t,
+        dz_t,
         vec,
         vec_s,
         vec_a,
@@ -258,6 +270,7 @@
         gout_all,
         gup_all,
         gdown_all,
+        sent,
         *part_refs,
     ) = refs[46:-2]
     dp, head = lax.axis_index("dp"), lax.axis_index("head")
@@ -291,8 +304,8 @@
     sibling = (sub * 2 + (1 - core), head)
 
     barrier = pltpu.get_barrier_semaphore()
-    greeted = [in_head(o) for o in range(1, 8)] + [in_sub(o) for o in range(1, 8)]
-    greeted += [sibling, ((1 - x_hi) * 8 + y * 2 + core, z * 2 + 1 - x_lo)]
+    greeted = [in_sub(o) for o in range(7, 0, -1)] + [in_head(o) for o in range(7, 0, -1)]
+    greeted += [((1 - x_hi) * 8 + y * 2 + core, z * 2 + 1 - x_lo), sibling]
     for device in greeted:
         pl.semaphore_signal(
             barrier, inc=1, device_id=device, device_id_type=pl.DeviceIdType.MESH
@@ -644,9 +657,20 @@
             c0 = 0.7978845608028654
             inner = jnp.tanh(c0 * (u + 0.044715 * u * u * u))
             act_buf[:, cols] = (0.5 * u * (1.0 + inner)).astype(BF16)
-            dgelu_buf[:, cols] = 0.5 * (1.0 + inner) + 0.5 * u * (1.0 - inner * inner) * c0 * (
-                1.0 + 3.0 * 0.044715 * u * u
-            )
+            dgelu_buf[:, cols] = u
+            tanh_buf[:, cols] = inner
+
+    def gelu_slope():
+        c0 = 0.7978845608028654
+
+        def strip(n, carry):
+            rows = pl.ds(aligned(n * 16, 16), 16)
+            u, inner = dgelu_buf[rows, :], tanh_buf[rows, :]
+            slope = (1.0 - inner * inner) * (c0 + 3.0 * 0.044715 * c0 * u * u)
+            dgelu_buf[rows, :] = 0.5 * (1.0 + inner) + 0.5 * u * slope
+            return carry
+
+        lax.fori_loop(0, 16, strip, 0)
 
     def ffn():
         spread_down.over_last.wait()
@@ -718,15 +742,11 @@
             dz1_full[rows, :] = dz
             bias_one = bias_one + jnp.sum(dz.astype(F32), axis=0, keepdims=True)
             ingrad_ref[rows, :] = (1.0 - g1) * dx1
-        dheads = dot(out_all[...], dattn_full[...], NT).astype(BF16)
-        dz1_t = dz1_full[...].astype(F32).T.astype(BF16)
-        for h in range(8):
-            back_send[h, 0:64, :] = dheads[64 * h : 64 * h + 64, :]
-            back_send[h, 64:128, :] = dz1_t[64 * h : 64 * h + 64, :]
-        group = g.back = Group(links, back_t.at[:, 0 : 7 * ROWS])
+        dheads_t[...] = dot(out_all[...], dattn_full[...], NT).astype(BF16)
+        group = g.back = Group(links, do_t.at[:, 0 : 7 * ROWS])
         for o in range(1, 8):
-            group.send(back_send.at[head_peer(o)], back_t.at[:, own], in_head(o))
-        back_t[:, own] = back_send[head]
+            group.send(block_of(dheads_t, head_peer(o), 64), do_t.at[:, own], in_head(o))
+        do_t[:, own] = dheads_t[own_heads, :]
         group = g.dattn = Group(links, dattn_half.at[0:ROWS, :])
         group.send(dattn_full.at[:, sib_half], dattn_half.at[own_core, :], sibling)
         dattn_half[own_core, :] = dattn_full[:, half]
@@ -734,14 +754,22 @@
         vec[3:4, :] = shift_sum
         vec[4:5, :] = bias_one
 
+    def back_first():
+        dz1_t[...] = dz1_full[...].astype(F32).T.astype(BF16)
+        group = g.back_first = Group(links, dz_t.at[:, 0 : 7 * ROWS])
+        for o in range(1, 8):
+            group.send(block_of(dz1_t, head_peer(o), 64), dz_t.at[:, own], in_head(o))
+        dz_t[:, own] = dz1_t[own_heads, :]
+
     def back_attention():
+        g.back.wait()
         dk_t[...] = jnp.zeros_like(dk_t)
         dv_t[...] = jnp.zeros_like(dv_t)
         for j in range(LEN // QB):
             cols = slice(QB * j, QB * (j + 1))
             upto = QB * (j + 1)
             queries = proj_t[0:64, cols]
-            grads = back_t[0:64, cols]
+            grads = do_t[:, cols]
             inverse = inv_mass[:, cols]
             delta = jnp.sum(o_t[:, cols] * grads.astype(F32), axis=0, keepdims=True)
             for t in range(upto // ROWS):
@@ -785,7 +813,7 @@
         gate_rows = gate_t[own_heads, :]
         for n in range(4):
             rows = slice(64 * n, 64 * n + 64)
-            grads = (dproj_low[rows, :] if n < 3 else back_t[64:128, :]).astype(F32)
+            grads = (dproj_low[rows, :] if n < 3 else dz_t[...]).astype(F32)
             sums = jnp.sum(grads, axis=1, keepdims=True)
             weights = w_all[pl.ds(aligned(head * 192 + 64 * n, 64), 64), :] if n < 3 else gate_rows
             weights = weights.astype(F32)
@@ -992,8 +1020,8 @@
 
 
     def first_start():
-        g.back.wait()
-        g1_f32[...] = dot(back_t[64:128, :], h1_all[...])
+        g.back_first.wait()
+        g1_f32[...] = dot(dz_t[...], h1_all[...])
         g1_low[...] = g1_f32[...].astype(BF16)
         g.first_start = Group(links, g1_sib)
         g.first_start.send(g1_low.at[:, sib_half], g1_sib, sibling)
@@ -1081,6 +1109,7 @@
         middle,
         hidden,
         ffn,
+        gelu_slope,
         spread_w.pass_on,
         gate_two,
         mix,
@@ -1088,6 +1117,7 @@
         back_hidden,
         second_y,
         back_middle,
+        back_first,
         grad_down,
         down_a.send,
         grad_up,
@@ -1097,8 +1127,8 @@
         second_z,
         first_start,
         down_b.send,
+        first_sub,
         down_a.next,
-        first_sub,
         grad_out_x,
         second_x,
         back_attention,
@@ -1127,8 +1157,8 @@
         down_sub,
         moments,
         grad_out_done,
+        vec_head,
         second_pair,
-        vec_head,
         first_pair,
         second_done,
         qkv_back_pair,
@@ -1141,7 +1171,7 @@
         down_done,
     ):
         run()
-    links.drain()
+    links.drain(sent)
 
 
 VMEM = pl.BlockSpec(memory_space=pltpu.VMEM)
@@ -1160,7 +1190,7 @@
         scratch_shapes=[pltpu.VMEM(s, t) for s, t in SCRATCH]
         + [pltpu.SemaphoreType.DMA((N_SEMS,)), pltpu.SemaphoreType.DMA((N_LOCAL,))],
         compiler_params=pltpu.CompilerParams(
-            collective_id=0, has_side_effects=True, vmem_limit_bytes=40 * 1024 * 1024
+            collective_id=0, has_side_effects=True, vmem_limit_bytes=44 * 1024 * 1024
         ),
         name="layer",
     )(*args)

time: 81.5 us -> 81.3 us (level)
  no operation moved by 1% of the time
where the time goes in v5:
time: 81.3 us; the launch traced here: 81.2 us
  Pallas kernels  80.3 us (99%)
  between operations  0.84 us (1%)
    pallas_call x1, Pallas kernels, run_layer(): pl.pallas_call(layer_kernel, out_shape=shapes + in_vmem, in_specs=[HBM] *...  75.8 us
    pallas_call x1, Pallas kernels, finish(): pl.pallas_call(finish_kernel, out_shape=[jax.ShapeDtypeStruct(a.shape, F3...  4.52 us

profile of v5, /device:TPU:1, one launch (start us, length us, event | category | flops | bytes accessed | tf_op | source)
XLA Modules:
  0.0 81.2 jit_solution(12090087540931523715)
XLA Ops:
  0.7 75.8 %layer.1 = (f32[128,512]{1,0:T(8,128)S(1)}, f32[128,512]{1,0:T(8,128)S(1)}, f32[192,512]{1,0:T(8,128)S(1)}, f32[192,512]{1,0:T(8,128)S(1)}, f32[192,512]{1,0:T(8...) custom-call(bf16[128,512]{1,0:T(8,128)(2,1)} %bitcast.34, ...), custom_call_target="tpu_custom_call" | custom-call | tf_op jit(solution)/shard_map/layer/pallas_call | solution.py:1185
  76.5 4.5 %finish.1 = (f32[128,512]{1,0:T(8,128)}, f32[128,512]{1,0:T(8,128)}, f32[192,512]{1,0:T(8,128)}, f32[192,512]{1,0:T(8,128)}, f32[192,512]{1,0:T(8,128)}, /*index...) custom-call(f32[128,512]{1,0:T(8,128)S(1)} %get-tuple-element.69.ref, ...), custom_call_target="tpu_custom_call" | custom-call | tf_op jit(solution)/shard_map/finish/pallas_call | solution.py:1211

commit v6 on v5

--- a/solution.py
+++ b/solution.py
@@ -1063,13 +1063,13 @@
         g.first_head.wait()
         group = g.first_pair = Group(links, g2_low)
         group.send(g1t_all.at[:, half], g1t_all.at[:, half], sibling)
+        g1_nat[half, :] = g1t_all[:, half].astype(F32).T
+        update(4, g1_nat.at[half, :], core * 256, 256)
 
     def first_done():
         g.first_pair.wait()
-        for n in range(4):
-            at = slice(128 * n, 128 * n + 128)
-            g1_nat[at, :] = g1t_all[:, at].astype(F32).T
-        update(4, g1_nat, 0, D)
+        g1_nat[sib_half, :] = g1t_all[:, sib_half].astype(F32).T
+        update(4, g1_nat.at[sib_half, :], (1 - core) * 256, 256)
 
     def moments():
         for load in loads[9:]:

time: 81.3 us -> 81.3 us (level)
  no operation moved by 1% of the time
where the time goes in v6:
time: 81.3 us; the launch traced here: 81.2 us
  Pallas kernels  80.3 us (99%)
  between operations  0.84 us (1%)
    pallas_call x1, Pallas kernels, run_layer(): pl.pallas_call(layer_kernel, out_shape=shapes + in_vmem, in_specs=[HBM] *...  75.8 us
    pallas_call x1, Pallas kernels, finish(): pl.pallas_call(finish_kernel, out_shape=[jax.ShapeDtypeStruct(a.shape, F3...  4.52 us

profile of v6, /device:TPU:1, one launch (start us, length us, event | category | flops | bytes accessed | tf_op | source)
XLA Modules:
  0.0 81.2 jit_solution(15377923523413403887)
XLA Ops:
  0.7 75.8 %layer.1 = (f32[128,512]{1,0:T(8,128)S(1)}, f32[128,512]{1,0:T(8,128)S(1)}, f32[192,512]{1,0:T(8,128)S(1)}, f32[192,512]{1,0:T(8,128)S(1)}, f32[192,512]{1,0:T(8...) custom-call(bf16[128,512]{1,0:T(8,128)(2,1)} %bitcast.34, ...), custom_call_target="tpu_custom_call" | custom-call | tf_op jit(solution)/shard_map/layer/pallas_call | solution.py:1185
  76.5 4.5 %finish.1 = (f32[128,512]{1,0:T(8,128)}, f32[128,512]{1,0:T(8,128)}, f32[192,512]{1,0:T(8,128)}, f32[192,512]{1,0:T(8,128)}, f32[192,512]{1,0:T(8,128)}, /*index...) custom-call(f32[128,512]{1,0:T(8,128)S(1)} %get-tuple-element.69.ref, ...), custom_call_target="tpu_custom_call" | custom-call | tf_op jit(solution)/shard_map/finish/pallas_call | solution.py:1211
